TPU v7x, 128 devices: a whole 4x4x4 slice. The times are simulated.
128 devices in a mesh: dp: 16 (over z_lo, y, core), tensor: 8 (over z_hi, x).
Axes of the slice: x: 4, y: 4, z: 4 (z_hi: 2, z_lo: 2; z = z_hi * 2 + z_lo), core: 2. Of those that a mesh axis runs over, the one named last changes fastest.
Arguments:
- hidden_in: bfloat16 [16, 1024, 2048], P('dp', None, 'tensor'), may hold values from -6 to 6
- cotangent: bfloat16 [16, 1024, 2048], P('dp', None, 'tensor'), may hold values from -6 to 6
- sequence_order: int32 [16], replicated, may hold values from 0 to 15, each once
- seq_lengths: int32 [16], replicated, may hold values from 1 to 1024, 12288 in all
- expert_ids: int32 [16, 1024, 2], replicated, may hold values from 0 to 3, all different within a row
- gate_weights: float32 [16, 1024, 2], replicated, may hold values from 0.2 to 1
- w_query: bfloat16 [2048, 2048], P(None, 'tensor'), may hold values from -0.125 to 0.125
- w_key: bfloat16 [2048, 2048], P(None, 'tensor'), may hold values from -0.125 to 0.125
- w_value: bfloat16 [2048, 2048], P(None, 'tensor'), may hold values from -0.125 to 0.125
- w_output: bfloat16 [2048, 2048], P('tensor'), may hold values from -2 to 2
- gain_attn: float32 [2048], replicated, may hold values from 0.5 to 1.5
- gain_query: float32 [2048], P('tensor'), may hold values from 0.5 to 1.5
- gain_key: float32 [2048], P('tensor'), may hold values from 0.5 to 1.5
- gain_mlp: float32 [2048], replicated, may hold values from 0.5 to 1.5
- w_gate: bfloat16 [4, 2048, 1024], P(None, None, 'tensor'), may hold values from -0.125 to 0.125
- w_up: bfloat16 [4, 2048, 1024], P(None, None, 'tensor'), may hold values from -0.125 to 0.125
- w_down: bfloat16 [4, 1024, 2048], P(None, 'tensor'), may hold values from -0.1875 to 0.1875
Outputs:
- output: bfloat16 [16, 1024, 2048], P('dp', None, 'tensor')
- grad_input: bfloat16 [16, 1024, 2048], P('dp', None, 'tensor')
- grad_w_query: float32 [2048, 2048], P(None, 'tensor')
- grad_w_key: float32 [2048, 2048], P(None, 'tensor')
- grad_w_value: float32 [2048, 2048], P(None, 'tensor')
- grad_w_output: float32 [2048, 2048], P('tensor')
- grad_gain_attn: float32 [2048], replicated
- grad_gain_query: float32 [2048], P('tensor')
- grad_gain_key: float32 [2048], P('tensor')
- grad_gain_mlp: float32 [2048], replicated
- grad_w_gate: float32 [4, 2048, 1024], P(None, None, 'tensor')
- grad_w_up: float32 [4, 2048, 1024], P(None, None, 'tensor')
- grad_w_down: float32 [4, 1024, 2048], P(None, 'tensor')
Inputs may be any that keep to these rules, and one draw needn't show every extreme that they name: `sequence_order`: each sequence is named once. `seq_lengths`: some sequence has exactly 1024 tokens; the lengths sum to 12288. `expert_ids`: the 2 experts of a token differ.
All inputs are finite; a program needn't handle non-finite values.
Results may differ from a plain program's by a relative error of at most 0.03.
Values may be sent and summed in bfloat16 or wider, within the bound.
No kernel may reach another device: no remote copies, remote signals or barrier semaphores. Data moves between devices by JAX's collectives and lax.ppermute only.
A program may use at most 320 MiB of HBM per device.

v0:
```python
import math

import jax
import jax.numpy as jnp
import numpy as np
from jax import lax
from jax.experimental import pallas as pl
from jax.experimental.pallas import tpu as pltpu
from jax.sharding import Mesh
from jax.sharding import PartitionSpec as P

AXES = ("zl", "y", "c", "zh", "x")
SIZES = (2, 4, 2, 2, 4)
DP = ("zl", "y", "c")
TENSOR = ("zh", "x")
GROUPS = ("zl", "y", "zh")

HEAD_DIM = 128
EPS = 1e-06
BASE = 50000.0
BF = jnp.bfloat16
F32 = jnp.float32
SCALE = 1.0 / math.sqrt(HEAD_DIM)
VMEM = 32 * 1024 * 1024
BIG = 56 * 1024 * 1024


def rope_tables(length):
    half = HEAD_DIM // 2
    frequency = np.power(
        np.float32(BASE), np.float32(-2.0) * np.arange(half, dtype=np.float32) / HEAD_DIM
    ).astype(np.float32)
    angles = np.arange(length, dtype=np.float32)[:, None] * frequency[None, :]
    cosine = np.cos(angles.astype(np.float64)).astype(np.float32)
    sine = np.sin(angles.astype(np.float64)).astype(np.float32)
    return np.concatenate([cosine, cosine], 1), np.concatenate([-sine, sine], 1)


def along(value, axis, shift):
    size = SIZES[AXES.index(axis)]
    return lax.ppermute(value, axis, [(i, (i + shift) % size) for i in range(size)])


def other_core(value):
    return lax.ppermute(value, "c", [(0, 1), (1, 0)])


def other_half_chip(value):
    return lax.ppermute(value, ("zl", "zh"), [(i, 3 - i) for i in range(4)])


def sum_x(value):
    return value + along(value, "x", 1) + along(value, "x", 2) + along(value, "x", 3)


def gather_x(value, awaited=None):
    half = value.shape[0] // 2
    after, before = along(value, "x", -1), along(value, "x", 1)
    far = [after[:half], before[half:]]
    if awaited is not None:
        far = tie(far, awaited)
    return [value, after, along(far[0], "x", -1), along(far[1], "x", 1), before]


def tie_kernel(*refs):
    del refs


def tie(values, awaited):
    anywhere = pl.BlockSpec(memory_space=pl.ANY)
    count = len(values)
    return pl.pallas_call(
        tie_kernel,
        in_specs=[anywhere] * (count + 1),
        out_specs=[anywhere] * count,
        out_shape=[jax.ShapeDtypeStruct(v.shape, v.dtype) for v in values],
        input_output_aliases={i: i for i in range(count)},
    )(*values, awaited)


def later(start, awaited):
    ends = awaited[(0,) * awaited.ndim].astype(F32) + awaited[(-1,) * awaited.ndim].astype(F32)
    return start + (ends != ends).astype(jnp.int32)


def send_x(pieces):
    return [
        pieces[0],
        along(pieces[1], "x", 1),
        along(pieces[2], "x", 2),
        along(pieces[3], "x", -1),
    ]


def deal_in(value, zh, awaited=None):
    half = value.shape[0] // 2
    got = []
    for k in (0, 1):
        pairs = [(a * 2 + b, (b ^ k) * 2 + a) for a in range(2) for b in range(2)]
        start = (zh ^ k) * half
        if awaited is not None:
            start = later(start, awaited)
        part = lax.dynamic_slice_in_dim(value, start, half, 0)
        got.append(lax.ppermute(part, ("c", "zh"), pairs))
    return jnp.stack(got, 0)


def deal_line(parts):
    return lax.all_to_all(parts, ("c", "x"), 0, 0, tiled=True)


def deal_out(dealt, same):
    got = dealt.transpose(1, 0, 2, 3).reshape(2, 1024, 256)
    moved = lax.ppermute(got, ("c", "zh"), [(1, 2), (2, 1)])
    got = jnp.where(same, got, moved)
    return got[0], got[1]


def other_half(weights, c, awaited):
    half = weights[0].shape[0] // 2
    start = later(c * half, awaited)
    parts = [lax.dynamic_slice_in_dim(w, start, half, 0) for w in weights]
    return other_half_chip(jnp.concatenate(parts, parts[0].ndim - 1))


def send_y(pieces):
    return [pieces[0]] + [along(pieces[r], "y", r) for r in (1, 2, 3)]


def to_shard(value, zl, same):
    low, high = value[:256], value[256:]
    near = jnp.where(zl == 0, low, high)
    far = jnp.where(zl == 0, high, low)
    order = [(i, k, m) for i in range(2) for k in range(2) for m in range(2)]
    index = lambda i, k, m: (i * 2 + k) * 2 + m
    stay = [(index(i, k, m), index(i, m, k)) for i, k, m in order if k != m]
    flip = [(index(i, k, m), index(1 - i, m, k)) for i, k, m in order]
    axes = ("zl", "c", "zh")
    got = lax.ppermute(near, axes, stay)
    return jnp.where(same, near, got), lax.ppermute(far, axes, flip)


def from_groups(piece):
    pair = jnp.stack([piece, lax.ppermute(piece, "zl", [(0, 1), (1, 0)])], 0)
    return [pair] + [along(pair, "y", -r) for r in (1, 2, 3)]


def settle(value):
    return lax.ppermute(value, ("c", "zh"), [(0, 2), (3, 1)])


def dot(left, right, dims):
    return lax.dot_general(left, right, (dims, ((), ())), preferred_element_type=F32)


NT = ((1,), (1,))
NN = ((1,), (0,))
TN = ((0,), (0,))


def call(kernel, grid, in_specs, out_specs, out_shape, scratch=(), flops=1, vmem=VMEM):
    return pl.pallas_call(
        kernel,
        grid_spec=pltpu.PrefetchScalarGridSpec(
            num_scalar_prefetch=1,
            grid=grid,
            in_specs=in_specs,
            out_specs=out_specs,
            scratch_shapes=scratch,
        ),
        out_shape=out_shape,
        compiler_params=pltpu.CompilerParams(vmem_limit_bytes=vmem),
        cost_estimate=pl.CostEstimate(flops=flops, bytes_accessed=1, transcendentals=0),
    )


def shape(*dims, dtype=BF):
    return jax.ShapeDtypeStruct(dims, dtype)


def whole(*dims):
    return pl.BlockSpec(dims, lambda i, p: (0,) * len(dims))


ANYWHERE = pl.BlockSpec(memory_space=pl.ANY)


def line_rows(place, r, rows=128):
    return pl.ds(pl.multiple_of(lax.rem(place[0] + r, 4) * rows, rows), rows)


def pick(flag, yes, no):
    return jnp.where(flag == 1, yes, no)


def pair_of(i, p):
    return jnp.where(i == 0, p[1], jnp.where(i == 1, 1 - p[1], i - 2))


def send_pair(i, p):
    other = jnp.where(i == 0, p[1], 1 - p[1])
    return jnp.where(p[2] == 1, other, jnp.maximum(i - 2, 0))


def keep_pair(i, p):
    other = jnp.where(i == 0, p[1], 1 - p[1])
    return jnp.where(p[2] == 1, jnp.maximum(i - 2, 0), other)


def role(i, p, first):
    return jnp.where(i < first, 1 - p[2], p[2])


def column_blocks(place, pieces):
    own, after, far_low, far_high, before = pieces
    for r, (first, second) in enumerate(
        ((own, own), (after, after), (far_low, far_high), (before, before))
    ):
        for k, piece in enumerate((first, second)):
            index = lax.rem(place[1] + k, 2) * 4 + lax.rem(place[0] + r, 4)
            yield pl.multiple_of(index * 256, 256), piece[k if r != 2 else 0]


def norm_kernel(place, own, after, far_low, far_high, before, gain, low, normed, inv):
    squares = jnp.zeros((low.shape[0], 1), F32)
    for column, here in column_blocks(place, (own, after, far_low, far_high, before)):
        low[:, pl.ds(column, 256)] = here
        here = here.astype(F32)
        squares += jnp.sum(here * here, axis=1, keepdims=True)
    root = lax.rsqrt(squares / low.shape[1] + EPS)
    inv[...] = root
    normed[...] = (low[...].astype(F32) * root * gain[...]).astype(BF)


def piece_specs(step, rows_of):
    return [pl.BlockSpec((n, step, 256), rows_of) for n in (2, 2, 1, 1, 2)]


def norm_rows(pieces, place, gain):
    rows, step = pieces[0].shape[1], 128
    full = lambda: pl.BlockSpec((step, 2048), lambda i, p: (i, 0))
    return call(
        norm_kernel,
        (rows // step,),
        piece_specs(step, lambda i, p: (0, i, 0)) + [whole(1, 2048)],
        [full(), full(), pl.BlockSpec((step, 1), lambda i, p: (i, 0))],
        [shape(rows, 2048), shape(rows, 2048), shape(rows, 1, dtype=F32)],
    )(place, *pieces, gain)


def place_kernel(place, own, after, far_low, far_high, before, low):
    for column, here in column_blocks(place, (own, after, far_low, far_high, before)):
        low[:, pl.ds(column, 256)] = here


def place_rows(pieces, place):
    rows = pieces[0].shape[1]
    step = rows // 4
    return call(
        place_kernel,
        (4,),
        piece_specs(step, lambda i, p: (0, lax.rem(i + p[0], 4), 0)),
        pl.BlockSpec((step, 2048), lambda i, p: (i, 0)),
        shape(rows, 2048),
    )(place, *pieces)


def project_kernel(place, rows_in, *refs):
    *own, near, far, awaited, send, keep, squares, columns = refs
    i = pl.program_id(0)
    lane = lax.broadcasted_iota(jnp.int32, columns.shape, 1)

    @pl.when(i == 0)
    def _():
        columns[...] = jnp.zeros_like(columns)

    def finish(raw):
        kept = role(i, place, 3)

        @pl.when(kept == 1)
        def _():
            keep[...] = raw

        @pl.when(kept == 0)
        def _():
            send[...] = raw

        total = jnp.sum(raw * raw, axis=1, keepdims=True)
        columns[...] += jnp.where(lane == lax.rem(i, 3), total, 0.0)

    @pl.when(i < 3)
    def _():
        half = near.shape[0]
        here = pl.ds(pl.multiple_of(place[1] * half, half), half)
        there = pl.ds(pl.multiple_of((1 - place[1]) * half, half), half)
        finish(dot(rows_in[:, here], near[...], NN) + dot(rows_in[:, there], far[...], NN))

    for j, weight in enumerate(own):

        @pl.when(i == 3 + j)
        def _(weight=weight):
            finish(dot(rows_in[...], weight[...], NN))

    @pl.when(i == 5)
    def _():
        squares[...] = columns[...].T


def project(rows_in, own, near, far, awaited, place):
    rows, width = rows_in.shape
    other = lambda i: jnp.minimum(i, 2)
    mine = lambda i: jnp.maximum(i - 3, 0)
    return call(
        project_kernel,
        (6,),
        [
            whole(rows, width),
            whole(width, 256),
            whole(width, 256),
            whole(width, 256),
            pl.BlockSpec((width // 2, 256), lambda i, p: (0, other(i))),
            pl.BlockSpec((width // 2, 256), lambda i, p: (0, other(i))),
            ANYWHERE,
        ],
        [
            pl.BlockSpec((rows, 256), lambda i, p: (0, jnp.where(p[2] == 1, other(i), mine(i)))),
            pl.BlockSpec((rows, 256), lambda i, p: (0, jnp.where(p[2] == 1, mine(i), other(i)))),
            whole(8, rows),
        ],
        [shape(rows, 768, dtype=F32), shape(rows, 768, dtype=F32), shape(8, rows, dtype=F32)],
        scratch=[pltpu.VMEM((rows, 8), F32)],
    )(place, rows_in, *own, near, far, awaited)


def columns_of(rows_two):
    rest = jnp.zeros((6, rows_two.shape[1]), F32)
    return jnp.concatenate([rows_two, rest], 0).T


def prep_kernel(place, raw_send, raw_keep, inv_rows, gains, cosine, sine, first, second, out_send, out_keep):
    inv = columns_of(inv_rows[...])
    for part, (raw, out) in enumerate(((raw_keep, out_keep), (raw_send, out_send))):
        for i in range(2):
            for h in range(2):
                lo = i * 256 + h * 128
                normed = raw[:, lo : lo + 128] * inv[:, i : i + 1]
                out[:, 768 + lo : 896 + lo] = normed.astype(BF)
                normed = normed * gains[part * 2 + i : part * 2 + i + 1, h * 128 : h * 128 + 128]
                out[:, lo : lo + 128] = (
                    normed * cosine[...] + pltpu.roll(normed, 64, 1) * sine[...]
                ).astype(BF)
        out[:, 512:768] = raw[:, 512:768].astype(BF)


def prep(raw_send, raw_keep, inv_rows, gains, cosine, sine, awaited, place):
    rows, step = raw_send.shape[0], 128
    spec = lambda width: pl.BlockSpec((step, width), lambda i, p: (i, 0))
    return call(
        prep_kernel,
        (rows // step,),
        [
            spec(768),
            spec(768),
            pl.BlockSpec((2, step), lambda i, p: (0, i)),
            whole(4, 256),
            spec(128),
            spec(128),
            ANYWHERE,
            ANYWHERE,
        ],
        [spec(1280), spec(1280)],
        [shape(rows, 1280), shape(rows, 1280)],
    )(place, raw_send, raw_keep, inv_rows, gains, cosine, sine, *awaited)


def attend_kernel(place, mine, rest, bias, qkv, out_mine, out_rest, lse):
    rows = 256
    qkv[0:512, :] = mine[...]
    qkv[512:1024, :] = rest[...]
    for h in range(2):
        cols = slice(h * 128, h * 128 + 128)
        keys = qkv[:, 256 + h * 128 : 384 + h * 128]
        values = qkv[:, 512 + h * 128 : 640 + h * 128]
        for i in range(4):
            here = slice(i * rows, (i + 1) * rows)
            scores = dot(qkv[here, cols], keys, NT) * SCALE + bias[...]
            top = jnp.max(scores, axis=1, keepdims=True)
            weight = jnp.exp(scores - top)
            total = jnp.sum(weight, axis=1, keepdims=True)
            out = out_mine if i < 2 else out_rest
            out[i % 2 * rows : i % 2 * rows + rows, cols] = (
                dot(weight.astype(BF), values, NN) / total
            ).astype(BF)
            wide = jnp.broadcast_to(top + jnp.log(total), (rows, 8))
            lse[h : h + 1, here] = wide.T[0:1, :]


def attend(mine, rest, bias, place):
    return call(
        attend_kernel,
        (1,),
        [whole(512, 1280), whole(512, 1280), whole(1, 1024)],
        [whole(1024, 1280), whole(512, 256), whole(512, 256), whole(2, 1024)],
        [shape(1024, 1280), shape(512, 256), shape(512, 256), shape(2, 1024, dtype=F32)],
    )(place, mine, rest, bias)


def fill_other(place, near, far, other):
    half = near.shape[0]
    other[pl.ds(pl.multiple_of(place[1] * half, half), half), :] = near[...]
    other[pl.ds(pl.multiple_of((1 - place[1]) * half, half), half), :] = far[...]


def heads_to_rows_kernel(place, keep, send, own, near, far, first, second, a, b, c, d, other):
    fill_other(place, near, far, other)
    for r, out in enumerate((a, b, c, d)):
        here = line_rows(place, r)
        left, right = keep[here, :], send[here, :]
        part = dot(pick(place[2], left, right), own[...], NN)
        part += dot(pick(place[2], right, left), other[...], NN)
        out[...] = part.astype(BF)


def heads_to_rows(heads, rest, own, near, far, awaited, place):
    width = own.shape[1]
    step = width // 2
    tile = lambda n: pl.BlockSpec((n, step), lambda i, p: (0, i))
    return call(
        heads_to_rows_kernel,
        (2,),
        [whole(512, 256), whole(512, 256), tile(256), tile(128), tile(128), ANYWHERE, ANYWHERE],
        [tile(128)] * 4,
        [shape(128, width)] * 4,
        scratch=[pltpu.VMEM((256, step), BF)],
    )(place, heads, rest, own, near, far, *awaited)


def fill(rows, pieces):
    start = 0
    for piece in pieces:
        rows[start : start + piece.shape[0], :] = piece[...]
        start += piece.shape[0]


def rows_to_heads_kernel(
    place, own_rows, after, far_low, far_high, before, own, near, far,
    keep, send, rows, other,
):
    fill(rows, (own_rows, after, far_low, far_high, before))
    fill_other(place, near, far, other)
    mine = dot(rows[...], own[...], NT).astype(BF)
    rest = dot(rows[...], other[...], NT).astype(BF)
    for out, part in ((send, pick(place[2], rest, mine)), (keep, pick(place[2], mine, rest))):
        for r in range(4):
            out[line_rows(place, r), :] = part[r * 128 : r * 128 + 128]


def rows_to_heads(pieces, own, near, far, place):
    width = own.shape[1]
    return call(
        rows_to_heads_kernel,
        (1,),
        [whole(n, width) for n in (128, 128, 64, 64, 128, 256, 128, 128)],
        [whole(512, 256), whole(512, 256), whole(512, width)],
        [shape(512, 256), shape(512, 256), shape(512, width)],
        scratch=[pltpu.VMEM((256, width), BF)],
        vmem=BIG,
    )(place, *pieces, own, near, far)


def middle_kernel(place, a, b, c, d, low, gain, middle, normed, inv):
    total = sum((t[...].astype(F32) for t in (b, c, d)), a[...].astype(F32))
    total = low[...].astype(F32) + total
    middle[...] = total
    root = lax.rsqrt(jnp.mean(total * total, axis=1, keepdims=True) + EPS)
    inv[...] = root
    normed[...] = (total * root * gain[...]).astype(BF)


def middle_rows(terms, low, gain, place):
    width = low.shape[1]
    return call(
        middle_kernel,
        (1,),
        [whole(128, width)] * 4
        + [pl.BlockSpec((128, width), lambda i, p: (p[0], 0)), whole(1, width)],
        [whole(128, width), whole(128, width), whole(128, 1)],
        [shape(128, width, dtype=F32), shape(128, width), shape(128, 1, dtype=F32)],
    )(place, *terms, low, gain)


def middle_back_kernel(
    place, a, b, c, d, middle, inv, gain, cot, ready_a, ready_b, ready_c, d_middle, d_low, gain_part
):
    d_in = sum((t[...].astype(F32) for t in (b, c, d)), a[...].astype(F32))
    hat = middle[...] * inv[...]
    gain_part[...] = jnp.sum(d_in * hat, axis=0, keepdims=True)
    scaled = d_in * gain[...]
    mean = jnp.mean(scaled * hat, axis=1, keepdims=True)
    total = cot[...].astype(F32) + inv[...] * (scaled - hat * mean)
    d_middle[...] = total
    d_low[...] = total.astype(BF)


def middle_back(terms, middle, inv, gain, cot, ready, place):
    width = middle.shape[1]
    return call(
        middle_back_kernel,
        (1,),
        [whole(128, width)] * 5
        + [whole(128, 1), whole(1, width), whole(128, width)]
        + [ANYWHERE] * 3,
        [whole(128, width), whole(128, width), whole(1, width)],
        [shape(128, width, dtype=F32), shape(128, width), shape(1, width, dtype=F32)],
        vmem=BIG,
    )(place, *terms, middle, inv, gain, cot, *ready)


def cot_back_kernel(place, cot, own, near, far, out):
    def one(down):
        out[0] = dot(cot[...], down, NT)

    i = pl.program_id(0)
    pl.when(i == 0)(lambda: one(near[...].reshape(256, near.shape[2])))
    pl.when(i == 1)(lambda: one(far[...].reshape(256, far.shape[2])))
    pl.when(i >= 2)(lambda: one(own[...].reshape(256, own.shape[2])))


def own_pair(i, p):
    return (jnp.maximum(i - 2, 0), 0, 0)


def cot_back(cot, own, near, far, place):
    rows, width = cot.shape
    return call(
        cot_back_kernel,
        (4,),
        [
            whole(rows, width),
            pl.BlockSpec((2, 128, width), own_pair),
            whole(2, 128, width),
            whole(2, 128, width),
        ],
        pl.BlockSpec((1, rows, 256), lambda i, p: (i, 0, 0)),
        shape(4, rows, 256, dtype=F32),
        flops=5_000_000_000,
    )(place, cot, own, near, far)


def expert_kernel(
    place, own_rows, after, far_low, far_high, before, back, weights, own_gate, own_up, near, far,
    send, keep, rows, a, b, c, d, total, both_weights,
):
    i = pl.program_id(0)

    @pl.when(i == 0)
    def _():
        fill(rows, (own_rows, after, far_low, far_high, before))

    def two(gate, gate_start, up, up_start):
        for j in range(2):
            both_weights[:, j * 256 : j * 256 + 128] = gate[j, :, gate_start : gate_start + 128]
            both_weights[:, j * 256 + 128 : j * 256 + 256] = up[j, :, up_start : up_start + 128]
        lane = lax.broadcasted_iota(jnp.int32, weights.shape, 1)
        pre = dot(rows[...], both_weights[...], NN)
        grads, acts = [], []
        for j in range(2):
            named = lane == pair_of(i, place) * 2 + j
            weight = jnp.sum(jnp.where(named, weights[...], 0.0), axis=1, keepdims=True)
            gate = pre[:, j * 256 : j * 256 + 128]
            up = pre[:, j * 256 + 128 : j * 256 + 256]
            sig = 1.0 / (1.0 + jnp.exp(-gate))
            silu = gate * sig
            d_act = weight * back[0, :, j * 128 : j * 128 + 128]
            acts.append((weight * (silu * up)).astype(BF))
            grads.append((d_act * up * sig * (1.0 + gate * (1.0 - sig))).astype(BF))
            grads.append((d_act * silu).astype(BF))
        both = jnp.concatenate(grads, 1)
        hidden = jnp.concatenate([both] + acts, 1)
        kept = role(i, place, 2)

        @pl.when(kept == 1)
        def _():
            keep[0] = hidden

        @pl.when(kept == 0)
        def _():
            send[0] = hidden

        part = dot(both, both_weights[...], NT)

        @pl.when(i == 0)
        def _():
            total[...] = part

        @pl.when(i > 0)
        def _():
            total[...] += part

    pl.when(i == 0)(lambda: two(near, 0, near, 128))
    pl.when(i == 1)(lambda: two(far, 0, far, 128))
    pl.when(i >= 2)(lambda: two(own_gate, 0, own_up, 0))

    @pl.when(i == 3)
    def _():
        for r, out in enumerate((a, b, c, d)):
            out[...] = total[r * 128 : r * 128 + 128, :].astype(BF)


def expert_layer(pieces, back, weights, own_gate, own_up, near, far, place):
    rows, width = 512, pieces[0].shape[1]
    return call(
        expert_kernel,
        (4,),
        [whole(n, width) for n in (128, 128, 64, 64, 128)]
        + [
            pl.BlockSpec((1, rows, 256), lambda i, p: (i, 0, 0)),
            whole(rows, 4),
            pl.BlockSpec((2, width, 128), own_pair),
            pl.BlockSpec((2, width, 128), own_pair),
            whole(2, width, 256),
            whole(2, width, 256),
        ],
        [
            pl.BlockSpec((1, rows, 768), lambda i, p: (send_pair(i, p), 0, 0)),
            pl.BlockSpec((1, rows, 768), lambda i, p: (keep_pair(i, p), 0, 0)),
            whole(rows, width),
        ]
        + [whole(128, width)] * 4,
        [shape(2, rows, 768), shape(2, rows, 768), shape(rows, width)] + [shape(128, width)] * 4,
        scratch=[pltpu.VMEM((rows, width), F32), pltpu.VMEM((width, 512), BF)],
        vmem=44 * 1024 * 1024,
    )(place, *pieces, back, weights, own_gate, own_up, near, far)


def expert_out_kernel(place, send, keep, own, near, far, awaited, a, b, c, d, total):
    i = pl.program_id(0)

    def one(down):
        acts = pick(role(i, place, 2), keep[0], send[0])
        part = dot(acts, down, NN)

        @pl.when(i == 0)
        def _():
            total[...] = part

        @pl.when(i > 0)
        def _():
            total[...] += part

    pl.when(i == 0)(lambda: one(near[...].reshape(256, near.shape[2])))
    pl.when(i == 1)(lambda: one(far[...].reshape(256, far.shape[2])))
    pl.when(i >= 2)(lambda: one(own[...].reshape(256, own.shape[2])))

    @pl.when(i == 3)
    def _():
        for r, out in enumerate((a, b, c, d)):
            out[...] = total[r * 128 : r * 128 + 128, :].astype(BF)


def expert_out(send, keep, own, near, far, awaited, place):
    rows, width = 512, own.shape[2]
    return call(
        expert_out_kernel,
        (4,),
        [
            pl.BlockSpec((1, rows, 256), lambda i, p: (send_pair(i, p), 0, 2)),
            pl.BlockSpec((1, rows, 256), lambda i, p: (keep_pair(i, p), 0, 2)),
            pl.BlockSpec((2, 128, width), own_pair),
            whole(2, 128, width),
            whole(2, 128, width),
            ANYWHERE,
        ],
        [whole(128, width)] * 4,
        [shape(128, width)] * 4,
        scratch=[pltpu.VMEM((rows, width), F32)],
        flops=5_000_000_000,
    )(place, send, keep, own, near, far, awaited)


def attend_back_kernel(
    place, qkv, d_mine, d_rest, heads_mine, heads_rest, bias, lse, cosine, sine, d_query, d_key, d_value, sums, key_sum, value_sum
):
    rows = 256

    def unturn(grad, here):
        return grad * cosine[here, :] - pltpu.roll(grad, 64, 1) * sine[here, :]

    masked = jnp.broadcast_to(bias[...], (8, 1024)).T[:, 0:1]
    for h in range(2):
        cols = slice(h * 128, h * 128 + 128)
        keys = qkv[:, 256 + h * 128 : 384 + h * 128]
        keys_turned = keys.T
        values = qkv[:, 512 + h * 128 : 640 + h * 128]
        for i in range(4):
            here = slice(i * rows, (i + 1) * rows)
            query = qkv[here, cols]
            inside = slice(i % 2 * rows, i % 2 * rows + rows)
            d_here = (d_mine if i < 2 else d_rest)[inside, cols]
            heads = (heads_mine if i < 2 else heads_rest)[inside, cols]
            scores = dot(keys, query, NT) * SCALE + masked
            probs = jnp.exp(scores - lse[h : h + 1, here])
            mean = d_here.astype(F32) * heads.astype(F32)
            mean = jnp.sum(mean.T, axis=0, keepdims=True)
            d_scores = (probs * (dot(values, d_here, NT) - mean)).astype(BF)
            value_part = dot(probs.astype(BF), d_here, NN)
            key_part = dot(d_scores, query, NN)
            if i == 0:
                value_sum[...] = value_part
                key_sum[...] = key_part
            else:
                value_sum[...] += value_part
                key_sum[...] += key_part
            d_turned = dot(keys_turned, d_scores, NN) * SCALE
            inner = jnp.sum(d_turned * query.astype(F32).T, axis=0, keepdims=True)
            if h == 0:
                sums[0:1, here] = inner
            else:
                sums[0:1, here] += inner
            d_query[here, cols] = unturn(d_turned.T, here)
        d_value[:, cols] = value_sum[...].astype(BF)
        for i in range(4):
            here = slice(i * rows, (i + 1) * rows)
            d_rot = key_sum[here, :] * SCALE
            inner = d_rot * qkv[here, 256 + h * 128 : 384 + h * 128].astype(F32)
            inner = jnp.sum(inner.T, axis=0, keepdims=True)
            if h == 0:
                sums[1:2, here] = inner
            else:
                sums[1:2, here] += inner
            d_key[here, cols] = unturn(d_rot, here)


def attend_back(qkv, d_mine, d_rest, heads_mine, heads_rest, bias, lse, cosine, sine, place):
    return call(
        attend_back_kernel,
        (1,),
        [whole(1024, 1280)]
        + [whole(512, 256)] * 4
        + [whole(1, 1024), whole(2, 1024), whole(1024, 128), whole(1024, 128)],
        [whole(1024, 256), whole(1024, 256), whole(1024, 256), whole(2, 1024)],
        [
            shape(1024, 256, dtype=F32),
            shape(1024, 256, dtype=F32),
            shape(1024, 256),
            shape(2, 1024, dtype=F32),
        ],
        scratch=[pltpu.VMEM((1024, 128), F32), pltpu.VMEM((1024, 128), F32)],
        vmem=BIG,
    )(place, qkv, d_mine, d_rest, heads_mine, heads_rest, bias, lse, cosine, sine)


def raw_back_kernel(
    place, d_query, d_key, d_value, query_hat, key_hat, sums, inv_rows, gains, mine, rest, gain_parts
):
    step = pl.program_id(0)

    @pl.when(step == 0)
    def _():
        gain_parts[...] = jnp.zeros_like(gain_parts)

    mean, inv = columns_of(sums[...]), columns_of(inv_rows[...])
    parts = []
    for i, (grad, hat) in enumerate(((d_query, query_hat), (d_key, key_hat))):
        normed = hat[...].astype(F32)
        scaled = grad[...] * gains[i : i + 1, :]
        parts.append((inv[:, i : i + 1] * (scaled - normed * mean[:, i : i + 1])).astype(BF))
        gain_parts[i : i + 1, :] += jnp.sum(grad[...] * normed, axis=0, keepdims=True)
    total = jnp.concatenate(parts + [d_value[...]], 1)

    @pl.when(step < 2)
    def _():
        mine[...] = total

    @pl.when(step >= 2)
    def _():
        rest[...] = total


def raw_back(d_query, d_key, d_value, qkv, sums, inv_rows, gains, place):
    step = 256
    spec = lambda width, column=0: pl.BlockSpec((step, width), lambda i, p: (i, column))
    line = lambda: pl.BlockSpec((2, step), lambda i, p: (0, i))
    return call(
        raw_back_kernel,
        (4,),
        [
            spec(256),
            spec(256),
            spec(256),
            spec(256, 3),
            spec(256, 4),
            line(),
            line(),
            whole(2, 256),
        ],
        [
            pl.BlockSpec((step, 768), lambda i, p: (jnp.minimum(i, 1), 0)),
            pl.BlockSpec((step, 768), lambda i, p: (jnp.maximum(i - 2, 0), 0)),
            whole(2, 256),
        ],
        [shape(512, 768), shape(512, 768), shape(2, 256, dtype=F32)],
    )(place, d_query, d_key, d_value, qkv, qkv, sums, inv_rows, gains)


def back_kernel(place, *refs):
    rows_mine, rows_rest, d_mine, d_rest, raw_mine, raw_rest, raw_got = refs[:7]
    heads_mine, heads_rest, own_q, own_k, own_v, near, far, low, inv, gain_mlp, moe = refs[7:18]
    pieces, terms = refs[18:22], refs[22:26]
    mine, rest, total, d_own, d_other = refs[26:]
    i = pl.program_id(0)

    @pl.when(i == 0)
    def _():
        for r in range(4):
            mine[r * 128 : r * 128 + 128, :] = heads_mine[line_rows(place, r), :]
            rest[r * 128 : r * 128 + 128, :] = heads_rest[line_rows(place, r), :]
        d_own[...] = pick(place[2], raw_mine[...], raw_got[...])
        d_other[...] = pick(place[2], raw_got[...], raw_mine[...])

    qkv = dot(rows_mine[...], raw_mine[...], TN) + dot(rows_rest[...], raw_rest[...], TN)
    back = dot(d_mine[...], mine[...], TN) + dot(d_rest[...], rest[...], TN)
    grads = jnp.concatenate([qkv.astype(BF), back.astype(BF)], 1)
    for j, piece in enumerate(pieces):

        @pl.when(i // 2 == j)
        def _(piece=piece):
            piece[pl.ds(pl.multiple_of(lax.rem(i, 2) * 256, 256), 256), :] = grads

    other = jnp.where(i // 4 == place[1], near[...], far[...])
    own = jnp.concatenate([own_q[...], own_k[...], own_v[...]], 1)
    part = dot(d_own[...], own, NT) + dot(d_other[...], other, NT)
    total[...] = part
    gain = jnp.sum(part * (low[...].astype(F32) * inv[...]), axis=0, keepdims=True)
    zeros = jnp.zeros((14, gain.shape[1]), F32)
    gains = jnp.concatenate([gain, gain_mlp[...], zeros], 0).astype(BF)
    for r, out in enumerate(terms):
        out[0:128, :] = total[line_rows(place, r), :].astype(BF)
        out[128:144, :] = gains
    terms[2][144:272, :] = moe[...]


def back(
    rows_mine, rows_rest, d_mine, d_rest, raw_mine, raw_rest, raw_got, heads,
    own, near, far, low, inv, gain_mlp, moe, place,
):
    rows, width, step = 512, low.shape[1], 256
    block = lambda: pl.BlockSpec(
        (rows, step), lambda i, p: (0, lax.rem(p[3] + i // 2, 4) * 2 + lax.rem(i, 2))
    )
    half = lambda: pl.BlockSpec((step, 768), lambda i, p: (lax.rem(i, 4), 0))
    tile = lambda: pl.BlockSpec((step, 256), lambda i, p: (i, 0))
    column = lambda n: pl.BlockSpec((n, step), lambda i, p: (0, i))
    return call(
        back_kernel,
        (width // step,),
        [block(), block(), block(), block()]
        + [whole(rows, 768)] * 3
        + [whole(rows, 256)] * 2
        + [tile(), tile(), tile(), half(), half(), column(rows), whole(rows, 1), column(1), column(128)],
        [whole(512, 1024)] * 4 + [column(n) for n in (144, 144, 272, 144)],
        [shape(512, 1024)] * 4 + [shape(n, width) for n in (144, 144, 272, 144)],
        scratch=[
            pltpu.VMEM((rows, 256), BF),
            pltpu.VMEM((rows, 256), BF),
            pltpu.VMEM((rows, step), F32),
            pltpu.VMEM((rows, 768), BF),
            pltpu.VMEM((rows, 768), BF),
        ],
    )(
        place, rows_mine, rows_rest, d_mine, d_rest, raw_mine, raw_rest, raw_got, *heads,
        *own, near, far, low, inv, gain_mlp, moe,
    )


def last_rows_kernel(place, *refs):
    d_terms, moe_terms = refs[:4], refs[4:7]
    d_middle, middle, low, inv, gain = refs[7:12]
    parts, gains, rows = refs[-3:]
    total = sum((t[0:144].astype(F32) for t in d_terms[1:]), d_terms[0][...].astype(F32))
    gains[...] = total[128:130]
    d_in = total[:128]
    hat = low[...].astype(F32) * inv[...]
    scaled = d_in * gain[...]
    mean = jnp.mean(scaled * hat, axis=1, keepdims=True)
    rows[1] = (d_middle[...] + inv[...] * (scaled - hat * mean)).astype(BF)
    moe = sum((t[...].astype(F32) for t in moe_terms), d_terms[2][144:272].astype(F32))
    rows[0] = (middle[...] + moe).astype(BF)
    for i in range(8):
        parts[i] = rows[:, :, i * 256 : i * 256 + 256]


def last_rows(d_terms, moe_terms, d_middle, middle, low, inv, gain, awaited, place):
    width = low.shape[1]
    mine = lambda n: pl.BlockSpec((128, n), lambda i, p: (p[0], 0))
    return call(
        last_rows_kernel,
        (1,),
        [whole(n, width) for n in (144, 144, 272, 144)]
        + [whole(128, width)] * 5
        + [mine(width), mine(1), whole(1, width)]
        + [ANYWHERE] * len(awaited),
        [whole(8, 2, 128, 256), whole(2, width)],
        [shape(8, 2, 128, 256), shape(2, width, dtype=F32)],
        scratch=[pltpu.VMEM((2, 128, width), BF)],
        vmem=BIG,
    )(place, *d_terms, *moe_terms, d_middle, middle, low, inv, gain, *awaited)


def settle_attention_kernel(place, *refs):
    here, there = refs[:4], refs[4:8]
    query, key, value, back, small = refs[9:]
    i = pl.program_id(0)

    @pl.when(i == 0)
    def _():
        small[...] = jnp.zeros_like(small)

    def one(mine, rest):
        mine, rest = mine[0].astype(F32), rest[0].astype(F32)
        first = pick(place[1], rest[:128], mine[:128])
        second = pick(place[1], mine[:128], rest[:128])
        total = jnp.concatenate([first, second], 0)
        query[...] = total[:, :256]
        key[...] = total[:, 256:512]
        value[...] = total[:, 512:768]
        back[...] = total[:, 768:].T
        mine, rest = mine[128:], rest[128:]
        row = lax.broadcasted_iota(jnp.int32, mine.shape, 0)
        small[...] += jnp.where(row < 4, mine + rest, pick(place[2], mine, rest))

    for r in range(4):

        @pl.when(lax.rem(i // 2 + 4 - place[3], 4) == r)
        def _(r=r):
            one(here[r], there[r])


def settle_attention(here, there, awaited, place):
    piece = lambda: pl.BlockSpec((1, 144, 1024), lambda i, p: (lax.rem(i + p[4], 2), 0, 0))
    rows = lambda: pl.BlockSpec((256, 256), lambda i, p: (i, 0))
    return call(
        settle_attention_kernel,
        (8,),
        [piece() for _ in range(8)] + [ANYWHERE],
        [rows(), rows(), rows(), pl.BlockSpec((256, 256), lambda i, p: (0, i)), whole(16, 1024)],
        [shape(2048, 256, dtype=F32)] * 3
        + [shape(256, 2048, dtype=F32), shape(16, 1024, dtype=F32)],
    )(place, *here, *there, awaited)


def settle_experts_kernel(place, gu_mine, gu_got, down_mine, down_got, gate, up, down):
    total = pick(place[2], gu_mine[0], gu_got[0]).astype(F32)
    for j in range(2):
        gate[j] = total[:, j * 256 : j * 256 + 128]
        up[j] = total[:, j * 256 + 128 : j * 256 + 256]
    total = pick(place[2], down_mine[0], down_got[0]).astype(F32)
    down[...] = total.reshape(down.shape)


def settle_experts(gu_mine, gu_got, down_mine, down_got, place):
    def step(i, p, mine):
        return jnp.where(p[2] == mine, i, 0)

    def tall(mine):
        def index(i, p):
            j = step(i, p, mine)
            return (j // 4, lax.rem(j, 4), 0)

        return pl.BlockSpec((1, 512, 512), index)

    def flat(mine):
        def index(i, p):
            j = step(i, p, mine)
            return (j // 4, 0, lax.rem(j, 4))

        return pl.BlockSpec((1, 256, 512), index)

    thin = lambda: pl.BlockSpec((2, 512, 128), lambda i, p: (i // 4, lax.rem(i, 4), 0))
    return call(
        settle_experts_kernel,
        (8,),
        [tall(1), tall(0), flat(1), flat(0)],
        [thin(), thin(), pl.BlockSpec((2, 128, 512), lambda i, p: (i // 4, 0, lax.rem(i, 4)))],
        [shape(4, 2048, 128, dtype=F32)] * 2 + [shape(4, 128, 2048, dtype=F32)],
        flops=20_000_000_000,
    )(place, gu_mine, gu_got, down_mine, down_got)


def choice_weights(ids, gates, experts, capacity):
    named = ids[:, :, None] == jnp.arange(experts, dtype=jnp.int32)
    count = jnp.sum(named.astype(F32), axis=1)
    tokens = ids.shape[0]
    earlier = (
        jnp.arange(tokens, dtype=jnp.int32)[:, None] > jnp.arange(tokens, dtype=jnp.int32)[None, :]
    ).astype(BF)
    place = jnp.dot(earlier, count.astype(BF), preferred_element_type=F32)
    weight = jnp.sum(jnp.where(named, gates[:, :, None], 0.0), axis=1)
    return jnp.where(place < capacity, weight, 0.0)


def local(
    hidden_in,
    cotangent,
    sequence_order,
    seq_lengths,
    expert_ids,
    gate_weights,
    w_query,
    w_key,
    w_value,
    w_output,
    gain_attn,
    gain_query,
    gain_key,
    gain_mlp,
    w_gate,
    w_up,
    w_down,
):
    zl, y, c, zh, x = (lax.axis_index(a) for a in AXES)
    same = c == zh
    length = hidden_in.shape[1]
    half = length // 2
    experts = w_gate.shape[0]
    width = w_query.shape[0]
    place = jnp.stack([x, c, same.astype(jnp.int32), y, zl, zh]).astype(jnp.int32)
    sequence = (zl * SIZES[1] + y) * 2 + zh
    tokens_here = seq_lengths[sequence]
    ids_here = expert_ids[sequence]
    gates_here = gate_weights[sequence]

    x_dealt = deal_in(hidden_in[0], zh)
    qkv_own = [w_query, w_key, w_value]
    qkv_near = other_half(qkv_own, c, x_dealt)
    x_pieces = gather_x(x_dealt)
    cot_dealt = deal_in(cotangent[0], zh, x_pieces[1])
    gains_own = jnp.stack([gain_query, gain_key], 0)
    gains_other = other_half_chip(gains_own)

    cosine_np, sine_np = rope_tables(length)
    swap_halves = lambda t: lax.dynamic_slice_in_dim(
        jnp.concatenate([t, t], 0), c * half, length, 0
    )
    cosine_all, sine_all = swap_halves(jnp.asarray(cosine_np)), swap_halves(jnp.asarray(sine_np))
    positions = (jnp.arange(length, dtype=jnp.int32) + c * half) % length
    bias = jnp.where(positions < tokens_here, 0.0, -1e30).astype(F32)
    weight_all = choice_weights(ids_here, gates_here, experts, length * 2 // experts)
    weight_here = lax.dynamic_slice_in_dim(weight_all, c * half, half, 0)
    weight_here = lax.dynamic_slice_in_dim(
        jnp.concatenate([weight_here, weight_here], 0), x * (half // 4), half, 0
    )

    x_low, attn_in, inv_one = norm_rows(x_pieces, place, gain_attn[None, :])
    qkv_near, cot_first = tie([qkv_near, cot_dealt], attn_in)
    qkv_far = other_core(qkv_near)
    out_near = other_half([w_output], c, attn_in)
    raw_send, raw_keep, squares = project(attn_in, qkv_own, qkv_near, qkv_far, out_near, place)
    (gains_other,) = tie([gains_other], squares)
    gains_keep = jnp.where(same, gains_own, gains_other)
    gains_qk = jnp.concatenate([gains_keep, jnp.where(same, gains_other, gains_own)], 0)
    inv_qk = lax.rsqrt(sum_x(squares[:2]) / width + EPS)
    (out_near,) = tie([out_near], inv_qk)
    down_near = other_half([w_down], c, out_near)
    gu_near = other_half([w_gate, w_up], c, out_near)
    cot_pieces = gather_x(cot_first, inv_qk)
    ready_send, ready_keep = prep(
        raw_send,
        raw_keep,
        inv_qk,
        gains_qk,
        cosine_all[:half],
        sine_all[:half],
        (cot_pieces[1], cot_pieces[4]),
        place,
    )
    ready_rest = other_core(ready_send)
    qkv, heads_mine, heads_rest, lse = attend(ready_keep, ready_rest, bias[None, :], place)
    heads_got = other_core(heads_rest)
    out_near, inv_tied = tie([out_near, inv_qk], heads_got)
    out_far = other_core(out_near)
    inv_qk_rest = other_core(inv_tied)
    cot = place_rows(cot_pieces, place)
    attn_terms = send_x(
        heads_to_rows(heads_mine, heads_got, w_output, out_near, out_far, (cot, heads_got), place)
    )
    attn_in, cot = tie([attn_in, cot], heads_got)
    attn_in_rest = other_core(attn_in)
    cot_rest = other_core(cot)

    middle, moe_own, inv_two = middle_rows(attn_terms, x_low, gain_mlp[None, :], place)
    moe_pieces = gather_x(moe_own)
    gu_near, down_near = tie([gu_near, down_near], moe_pieces[1])
    gu_near, down_near = tie([gu_near, down_near], moe_pieces[4])
    down_far = other_core(down_near)
    cot_down = cot_back(cot, w_down, down_near, down_far, place)
    gu_far = other_core(gu_near)
    hidden_send, hidden_keep, moe_in, *d_moe_terms = expert_layer(
        moe_pieces, cot_down, weight_here, w_gate, w_up, gu_near, gu_far, place
    )
    d_moe_terms = send_x(d_moe_terms)
    moe_terms = expert_out(
        hidden_send, hidden_keep, w_down, down_near, down_far, hidden_keep, place
    )
    hidden_all = jnp.concatenate([hidden_keep, other_core(hidden_send)], 1)
    moe_all = jnp.concatenate([moe_in, other_core(moe_in)], 0)
    cot_all = jnp.concatenate([cot, cot_rest], 0)
    grad_gate_up = jnp.einsum(
        "td,etf->edf", moe_all, hidden_all[:, :, :512], preferred_element_type=F32
    ).astype(BF)
    grad_down = jnp.einsum(
        "etf,td->efd", hidden_all[:, :, 512:], cot_all, preferred_element_type=F32
    ).astype(BF)

    d_middle, d_own, gain_mlp_part = middle_back(
        d_moe_terms,
        middle,
        inv_two,
        gain_mlp[None, :],
        cot,
        (grad_gate_up, grad_down, moe_terms[0]),
        place,
    )
    grad_gate_up, grad_down = lax.psum((grad_gate_up, grad_down), GROUPS)
    d_pieces = gather_x(d_own)
    d_heads_keep, d_heads_send, d_attn = rows_to_heads(
        d_pieces, w_output, out_near, out_far, place
    )
    d_heads_rest = other_core(d_heads_send)
    *moe_terms, d_attn = tie(list(moe_terms) + [d_attn], d_heads_rest)
    moe_after, moe_before = along(moe_terms[1], "x", 1), along(moe_terms[3], "x", -1)
    d_attn_rest = other_core(d_attn)
    d_query, d_key, d_value, sums = attend_back(
        qkv,
        d_heads_keep,
        d_heads_rest,
        heads_mine,
        heads_rest,
        bias[None, :],
        lse,
        cosine_all,
        sine_all,
        place,
    )
    (sums,) = tie([sums], moe_after)
    (sums,) = tie([sums], moe_before)
    sums_rest = other_core(sums)
    sums = sums + jnp.concatenate([sums_rest[:, half:], sums_rest[:, :half]], 1)
    sums = sum_x(sums) / width
    raw_mine, raw_rest, gain_qk_parts = raw_back(
        d_query,
        d_key,
        d_value,
        qkv,
        sums,
        jnp.concatenate([inv_qk, inv_qk_rest], 1),
        gains_keep,
        place,
    )
    raw_got = other_core(raw_rest)
    pieces = back(
        attn_in,
        attn_in_rest,
        d_attn,
        d_attn_rest,
        raw_mine,
        raw_rest,
        raw_got,
        (heads_mine, heads_rest),
        qkv_own,
        qkv_near,
        qkv_far,
        x_low,
        inv_one,
        gain_mlp_part,
        moe_terms[2],
        place,
    )
    weight_terms = send_y(pieces[:4])
    d_in_terms = send_x(pieces[4:])
    moe_terms = [moe_terms[0], moe_after, moe_before]
    rows_dealt, gains = last_rows(
        d_in_terms,
        moe_terms,
        d_middle,
        middle,
        x_low,
        inv_one,
        gain_attn[None, :],
        weight_terms[1:],
        place,
    )
    dealt = deal_line(rows_dealt)
    grad_gate_up, grad_down = tie([grad_gate_up, grad_down], rows_dealt)
    total = sum((t.astype(F32) for t in weight_terms[1:]), weight_terms[0].astype(F32)).astype(BF)
    near, far = to_shard(total, zl, same)
    total = (near.astype(F32) + far.astype(F32)).astype(BF)
    first = c == 0
    got = other_core(jnp.where(first, total[128:], total[:128]))
    mine = jnp.where(first, total[:128], total[128:]).astype(F32) + got.astype(F32)
    small = jnp.concatenate([gains.reshape(-1), gain_qk_parts.reshape(-1)])
    small = (small + lax.ppermute(small, "zh", [(0, 1), (1, 0)])).reshape(9, 512)
    small = jnp.concatenate([small.reshape(-1), jnp.zeros((11776,), F32)]).reshape(16, 1024)
    (mine,) = tie([jnp.concatenate([mine, small], 0).astype(BF)], dealt)
    here = from_groups(mine)
    (dealt,) = tie([dealt], here[0])
    output, grad_input = deal_out(dealt, same)

    grad_gate, grad_up, grad_down = settle_experts(
        grad_gate_up, settle(grad_gate_up), grad_down, settle(grad_down), place
    )
    here = tie(list(here), grad_down)
    grad_query, grad_key, grad_value, grad_output, small = settle_attention(
        here, [other_core(t) for t in here], grad_down, place
    )
    small = small.reshape(-1)
    return (
        output[None],
        grad_input[None],
        grad_query,
        grad_key,
        grad_value,
        grad_output,
        small[:width],
        small[2 * width : 2 * width + 256],
        small[2 * width + 256 : 2 * width + 512],
        small[width : 2 * width],
        grad_gate,
        grad_up,
        grad_down,
    )


def solution(mesh):
    fine = Mesh(mesh.devices.reshape(SIZES), AXES)
    columns = P(None, TENSOR)
    placed = (
        P(DP, None, TENSOR),
        P(DP, None, TENSOR),
        P(),
        P(),
        P(),
        P(),
        columns,
        columns,
        columns,
        P(TENSOR, None),
        P(),
        P(TENSOR),
        P(TENSOR),
        P(),
        P(None, None, TENSOR),
        P(None, None, TENSOR),
        P(None, TENSOR, None),
    )
    return jax.shard_map(
        local,
        mesh=fine,
        in_specs=placed,
        out_specs=placed[:2]
        + (columns, columns, columns, P(TENSOR, None), P(), P(TENSOR), P(TENSOR), P())
        + placed[14:],
        check_vma=False,
    )
```

profile of v0, /device:TPU:1, one launch (start us, length us, event | category | flops | bytes accessed | tf_op | source)
XLA Modules:
  0.0 545.0 jit_solution(11430187137290747751)
XLA Ops:
  8.5 6.9 %collective-permute-start = (bf16[512,256]{1,0:T(8,128)(2,1)S(1)}, bf16[512,256]{1,0:T(8,128)(2,1)S(1)}, u32[]{:S(2)}, u32[]{:S(2)}) collective-permute-start(bf16[512,256]{1,0:T(8,128)(2,1)S(1)} %get-tuple-element.197), channel_id=1, source_target_pairs={{0,0},{4,8},{8,4},{12,12},{1,1},{5,9},{9,5},{13,13},{2,2},{6,10},{... | collective-permute-start | bytes 786440 | tf_op jit(solution)/shard_map/ppermute | solution.py:104
  15.5 3.9 collective-permute-done
  26.1 3.6 collective-permute-start.6
  32.2 10.9 %collective-permute-done.2.after = bf16[2,512,256]{2,1,0:T(8,128)(2,1)S(1)} collective-permute-done((bf16[2,512,256]{2,1,0:T(8,128)(2,1)S(1)}, bf16[2,512,256]{2,1,0:T(8,128)(2,1)S(1)}, u32[]{:S(2)}, u32[]{:S(2)}) %collective-permute-start.2) | collective-permute-done | bytes 524320 | tf_op jit(solution)/shard_map/ppermute | solution.py:41
  45.7 3.4 collective-permute-start.3
  51.8 4.9 collective-permute-start.7
  60.4 3.6 shard_map.273
  82.6 6.7 %collective-permute-done.12.refs_5_.refs_0_ = bf16[128,2048]{1,0:T(8,128)(2,1)S(1)} collective-permute-done((bf16[128,2048]{1,0:T(8,128)(2,1)}, bf16[128,2048]{1,0:T(8,128)(2,1)S(1)}, u32[]{:S(2)}, u32[]{:S(2)}) %collective-permute-start.12) | collective-permute-done | bytes 524320 | tf_op jit(solution)/shard_map/ppermute | solution.py:49
  94.6 7.7 %shard_map.275 = (f32[512,768]{1,0:T(8,128)S(1)}, f32[512,768]{1,0:T(8,128)S(1)}, f32[8,512]{1,0:T(8,128)S(1)}) custom-call(s32[6]{0:T(128)S(1)} %stack.67.place, bf16[512,2048]{1,0:T(8,128)(2,1)S(1)} %copy-done.3, bf16[2048,256]{1,0:T(8,128)(2,1)S(1)} %copy-done.28, bf16[2048,256]{1,0:T(8,128)(2,1)S(1)} %copy-done.21, bf16[2048,256]{1,0:T(8,128)(2,1)S(1)} %copy-done.24, ...), custom_call_target="tpu_custom_call" | custom-call | flops 1 | bytes 1 | tf_op jit(solution)/shard_map/pallas_call | solution.py:313
  117.3 3.1 shard_map.279
  120.4 3.2 collective-permute-start.19
  133.4 6.3 %shard_map.280 = (bf16[1024,1280]{1,0:T(8,128)(2,1)S(1)}, bf16[512,256]{1,0:T(8,128)(2,1)S(1)}, bf16[512,256]{1,0:T(8,128)(2,1)S(1)}, f32[2,1024]{1,0:T(2,128)S(1)}) custom-call(s32[6]{0:T(128)S(1)} %stack.67.place, bf16[512,1280]{1,0:T(8,128)(2,1)S(1)} %get-tuple-element.105.mine, bf16[512,1280]{1,0:T(8,128)(2,1)} %collective-permute-done.19.rest, ...), custom_call_target="tpu_custom_call" | custom-call | flops 1 | bytes 1 | tf_op jit(solution)/shard_map/pallas_call | solution.py:399
  147.5 6.5 %collective-permute-done.16.far_low = bf16[1,512,256]{2,1,0:T(8,128)(2,1)S(1)} collective-permute-done((bf16[1,512,256]{2,1,0:T(8,128)(2,1)}, bf16[1,512,256]{2,1,0:T(8,128)(2,1)S(1)}, u32[]{:S(2)}, u32[]{:S(2)}) %collective-permute-start.16) | collective-permute-done | bytes 262176 | tf_op jit(solution)/shard_map/ppermute | solution.py:41
  155.1 2.8 shard_map.277.refs_1_.first
  164.6 11.3 %collective-permute-done.23.b = bf16[128,2048]{1,0:T(8,128)(2,1)S(1)} collective-permute-done((bf16[128,2048]{1,0:T(8,128)(2,1)S(1)}, bf16[128,2048]{1,0:T(8,128)(2,1)S(1)}, u32[]{:S(2)}, u32[]{:S(2)}) %collective-permute-start.23) | collective-permute-done | bytes 524320 | tf_op jit(solution)/shard_map/ppermute | solution.py:41
  176.0 8.6 %collective-permute-done.24.c = bf16[128,2048]{1,0:T(8,128)(2,1)S(1)} collective-permute-done((bf16[128,2048]{1,0:T(8,128)(2,1)S(1)}, bf16[128,2048]{1,0:T(8,128)(2,1)S(1)}, u32[]{:S(2)}, u32[]{:S(2)}) %collective-permute-start.24) | collective-permute-done | bytes 524320 | tf_op jit(solution)/shard_map/ppermute | solution.py:41
  189.4 3.4 collective-permute-start.26
  192.8 8.8 %collective-permute-done.31.refs_1_ = bf16[2,128,2048]{2,1,0:T(8,128)(2,1)S(1)} collective-permute-done((bf16[2,128,2048]{2,1,0:T(8,128)(2,1)S(1)}, bf16[2,128,2048]{2,1,0:T(8,128)(2,1)S(1)}, u32[]{:S(2)}, u32[]{:S(2)}) %collective-permute-start.31) | collective-permute-done | bytes 1048608 | tf_op jit(solution)/shard_map/ppermute | solution.py:49
  219.4 4.8 shard_map.288.back
  225.6 18.0 %shard_map.289 = (bf16[2,512,768]{2,1,0:T(8,128)(2,1)S(1)}, bf16[2,512,768]{2,1,0:T(8,128)(2,1)S(1)}, bf16[512,2048]{1,0:T(8,128)(2,1)S(1)}, bf16[128,2048]{1,0:...) custom-call(s32[6]{0:T(128)S(1)} %stack.67.place, ...), custom_call_target="tpu_custom_call" | custom-call | flops 1 | bytes 1 | tf_op jit(solution)/shard_map/pallas_call | solution.py:612
  246.4 6.3 %shard_map.290 = (bf16[128,2048]{1,0:T(8,128)(2,1)S(1)}, bf16[128,2048]{1,0:T(8,128)(2,1)S(1)}, bf16[128,2048]{1,0:T(8,128)(2,1)S(1)}, bf16[128,2048]{1,0:T(8,128)(2,1)S(1)}) custom-call(s32[6]{0:T(128)S(1)} %stack.67.place, bf16[2,512,768]{2,1,0:T(8,128)(2,1)S(1)} %get-tuple-element.122.send, bf16[2,512,768]{2,1,0:T(8,128)(2,1)S(1)} %get-tuple-element.123.keep.awaited, ...), custom_call_target="tpu_custom_call" | custom-call | flops 5000000000 | bytes 1 | tf_op jit(solution)/shard_map/pallas_call | solution.py:663
  255.6 3.7 fusion.7.ready_b
  259.4 6.1 %convert_bitcast_fusion.ready_a = bf16[2,2048,512]{2,1,0:T(8,128)(2,1)} fusion(bf16[512,2048]{1,0:T(8,128)(2,1)S(1)} %collective-permute-done.38, bf16[512,2048]{1,0:T(8,128)(2,1)S(1)} %get-tuple-element.134, bf16[2,1024,768]{2,1,0:T(8,128)(2,1)S(1)} %constant_dynamic-update-slice_fusion), kind=kOutput, calls=%fused_computation.8 | convolution fusion | flops 4305453056 | bytes 10485760 | tf_op jit(solution)/shard_map/td,etf->edf/dot_general | solution.py:1108
  265.5 3.8 collective-permute-done.35.c
  271.3 4.6 shard_map.291
  276.9 3.3 collective-permute-start.40
  280.2 10.8 %collective-permute-done.40.after = bf16[128,2048]{1,0:T(8,128)(2,1)S(1)} collective-permute-done((bf16[128,2048]{1,0:T(8,128)(2,1)S(1)}, bf16[128,2048]{1,0:T(8,128)(2,1)S(1)}, u32[]{:S(2)}, u32[]{:S(2)}) %collective-permute-start.40) | collective-permute-done | bytes 524320 | tf_op jit(solution)/shard_map/ppermute | solution.py:41
  291.1 3.5 collective-permute-start.41
  294.9 3.9 collective-permute-done.41.far_low
  298.8 3.5 collective-permute-done.43.far_high
  303.1 5.8 %shard_map.292 = (bf16[512,256]{1,0:T(8,128)(2,1)}, bf16[512,256]{1,0:T(8,128)(2,1)}, bf16[512,2048]{1,0:T(8,128)(2,1)}) custom-call(s32[6]{0:T(128)} %copy-done.78, bf16[128,2048]{1,0:T(8,128)(2,1)} %get-tuple-element.135.own_rows, bf16[128,2048]{1,0:T(8,128)(2,1)} %copy-done.99, bf16[64,2048]{1,0:T(8,128)(2,1)} %copy-done.109, ...), custom_call_target="tpu_custom_call" | custom-call | flops 1 | bytes 1 | tf_op jit(solution)/shard_map/pallas_call | solution.py:460
  313.4 2.7 collective-permute-start.47
  319.3 10.4 %shard_map.294 = (f32[1024,256]{1,0:T(8,128)}, f32[1024,256]{1,0:T(8,128)}, bf16[1024,256]{1,0:T(8,128)(2,1)}, f32[2,1024]{1,0:T(2,128)}) custom-call(s32[6]{0:T(128)} %copy-done.78, bf16[1024,1280]{1,0:T(8,128)(2,1)} %copy-done.8, bf16[512,256]{1,0:T(8,128)(2,1)} %get-tuple-element.140.d_mine, bf16[512,256]{1,0:T(8,128)(2,1)} %copy-done.102, ...), custom_call_target="tpu_custom_call" | custom-call | flops 1 | bytes 1 | tf_op jit(solution)/shard_map/pallas_call | solution.py:735
  350.2 15.6 %shard_map.298 = (bf16[512,1024]{1,0:T(8,128)(2,1)S(1)}, bf16[512,1024]{1,0:T(8,128)(2,1)S(1)}, bf16[512,1024]{1,0:T(8,128)(2,1)S(1)}, bf16[512,1024]{1,0:T(8,12...) custom-call(s32[6]{0:T(128)S(1)} %copy-done.79, ...), custom_call_target="tpu_custom_call" | custom-call | flops 1 | bytes 1 | tf_op jit(solution)/shard_map/pallas_call | solution.py:854
  370.8 2.7 collective-permute-start.58
  374.5 8.0 %collective-permute-done.54.refs_1_ = bf16[144,2048]{1,0:T(8,128)(2,1)S(1)} collective-permute-done((bf16[144,2048]{1,0:T(8,128)(2,1)S(1)}, bf16[144,2048]{1,0:T(8,128)(2,1)S(1)}, u32[]{:S(2)}, u32[]{:S(2)}) %collective-permute-start.54) | collective-permute-done | bytes 589856 | tf_op jit(solution)/shard_map/ppermute | solution.py:41
  382.9 23.7 %collective-permute-done.56.refs_3_ = bf16[144,2048]{1,0:T(8,128)(2,1)S(1)} collective-permute-done((bf16[144,2048]{1,0:T(8,128)(2,1)S(1)}, bf16[144,2048]{1,0:T(8,128)(2,1)S(1)}, u32[]{:S(2)}, u32[]{:S(2)}) %collective-permute-start.56) | collective-permute-done | bytes 589856 | tf_op jit(solution)/shard_map/ppermute | solution.py:41
  406.7 5.0 collective-permute-done.57.refs_12_
  411.7 32.0 %collective-permute-done.58.refs_13_ = bf16[512,1024]{1,0:T(8,128)(2,1)S(1)} collective-permute-done((bf16[512,1024]{1,0:T(8,128)(2,1)S(1)}, bf16[512,1024]{1,0:T(8,128)(2,1)S(1)}, u32[]{:S(2)}, u32[]{:S(2)}) %collective-permute-start.58) | collective-permute-done | bytes 1048608 | tf_op jit(solution)/shard_map/ppermute | solution.py:41
  445.3 6.1 %shard_map.299 = (bf16[8,2,128,256]{3,2,1,0:T(8,128)(2,1)}, f32[2,2048]{1,0:T(2,128)}) custom-call(s32[6]{0:T(128)} %copy-done.78, bf16[144,2048]{1,0:T(8,128)(2,1)} %copy-done.65, bf16[144,2048]{1,0:T(8,128)(2,1)} %copy-done.103, bf16[272,2048]{1,0:T(8,128)(2,1)} %copy-done.101, bf16[144,2048]{1,0:T(8,128)(2,1)} %copy-done.104, ...), custom_call_target="tpu_custom_call" | custom-call | flops 1 | bytes 1 | tf_op jit(solution)/shard_map/pallas_call | solution.py:896
  460.7 5.9 %all-to-all-start = ((bf16[8,2,128,256]{3,2,1,0:T(8,128)(2,1)}), bf16[8,2,128,256]{3,2,1,0:T(8,128)(2,1)S(1)}, u32[]{:S(2)}, u32[]{:S(2)}) async-start(bf16[8,2,128,256]{3,2,1,0:T(8,128)(2,1)} %get-tuple-element.163.refs_2_), calls=%async_computation | async-start | bytes 2097152 | tf_op jit(solution)/shard_map/all_to_all | solution.py:109
  466.6 7.2 %collective-permute-done.60 = bf16[256,1024]{1,0:T(8,128)(2,1)S(1)} collective-permute-done((bf16[256,1024]{1,0:T(8,128)(2,1)S(1)}, bf16[256,1024]{1,0:T(8,128)(2,1)S(1)}, u32[]{:S(2)}, u32[]{:S(2)}) %collective-permute-start.60) | collective-permute-done | bytes 524320 | tf_op jit(solution)/shard_map/ppermute | solution.py:139
  475.6 2.8 collective-permute-done.63
  483.9 7.1 %collective-permute-done.64 = bf16[144,1024]{1,0:T(8,128)(2,1)S(1)} collective-permute-done((bf16[144,1024]{1,0:T(8,128)(2,1)}, bf16[144,1024]{1,0:T(8,128)(2,1)S(1)}, u32[]{:S(2)}, u32[]{:S(2)}) %collective-permute-start.64) | collective-permute-done | bytes 294944 | tf_op jit(solution)/shard_map/ppermute | solution.py:144
  496.1 5.6 %collective-permute-start.65 = (bf16[2,1024,256]{2,1,0:T(8,128)(2,1)S(1)}, bf16[2,1024,256]{2,1,0:T(8,128)(2,1)}, u32[]{:S(2)}, u32[]{:S(2)}) collective-permute-start(bf16[2,1024,256]{2,1,0:T(8,128)(2,1)S(1)} %bitcast.72), channel_id=1, source_target_pairs={{4,8},{8,4},{5,9},{9,5},{6,10},{10,6},{7,11},{11,7},{20,24},{24,20... | collective-permute-start | bytes 3145736 | tf_op jit(solution)/shard_map/ppermute | solution.py:114
  504.0 9.6 %shard_map.303 = (f32[4,2048,128]{2,1,0:T(8,128)}, f32[4,2048,128]{2,1,0:T(8,128)}, f32[4,128,2048]{2,1,0:T(8,128)}) custom-call(s32[6]{0:T(128)S(1)} %copy-done.80, bf16[2,2048,512]{2,1,0:T(8,128)(2,1)S(1)} %copy-done.36, bf16[2,2048,512]{2,1,0:T(8,128)(2,1)} %collective-permute-done.69.gu_got, bf16[2,256,2048]{2,1,0:T(8,128)(2,1)} %get-tuple-element.168.down_mine, ...), custom_call_target="tpu_custom_call" | custom-call | flops 20000000000 | bytes 1 | tf_op jit(solution)/shard_map/pallas_call | solution.py:980
  513.6 8.0 %collective-permute-done.68.refs_3_ = bf16[2,144,1024]{2,1,0:T(8,128)(2,1)S(1)} collective-permute-done((bf16[2,144,1024]{2,1,0:T(8,128)(2,1)S(1)}, bf16[2,144,1024]{2,1,0:T(8,128)(2,1)S(1)}, u32[]{:S(2)}, u32[]{:S(2)}) %collective-permute-start.68) | collective-permute-done | bytes 589856 | tf_op jit(solution)/shard_map/ppermute | solution.py:41
  530.5 5.4 shard_map.305
  (447 shorter events, 182.5 us)
Async XLA Ops:
  26.1 43.3 %collective-permute-start.6 = (bf16[1024,768]{1,0:T(8,128)(2,1)}, bf16[1024,768]{1,0:T(8,128)(2,1)S(1)}, u32[]{:S(2)}, u32[]{:S(2)}) collective-permute-start(bf16[1024,768]{1,0:T(8,128)(2,1)} %pad_maximum_fusion.1), channel_id=1, source_target_pairs={{0,68},{4,64},{64,4},{68,0},{1,69},{5,65},{65,5},{69,1},{2,70},{6,... | collective-permute-start | bytes 4718600 | tf_op jit(solution)/shard_map/ppermute | solution.py:49
  29.7 13.4 %collective-permute-start.2 = (bf16[2,512,256]{2,1,0:T(8,128)(2,1)S(1)}, bf16[2,512,256]{2,1,0:T(8,128)(2,1)S(1)}, u32[]{:S(2)}, u32[]{:S(2)}) collective-permute-start(bf16[2,512,256]{2,1,0:T(8,128)(2,1)S(1)} %pad_maximum_fusion.3.own), channel_id=1, source_target_pairs={{0,3},{1,0},{2,1},{3,2},{4,7},{5,4},{6,5},{7,6},{8,11},{9,8},{10,9... | collective-permute-start | bytes 1572872 | tf_op jit(solution)/shard_map/ppermute | solution.py:41
  32.2 16.9 %collective-permute-start.4 = (bf16[2,512,256]{2,1,0:T(8,128)(2,1)S(1)}, bf16[2,512,256]{2,1,0:T(8,128)(2,1)S(1)}, u32[]{:S(2)}, u32[]{:S(2)}) collective-permute-start(bf16[2,512,256]{2,1,0:T(8,128)(2,1)S(1)} %pad_maximum_fusion.3.own), channel_id=1, source_target_pairs={{0,1},{1,2},{2,3},{3,0},{4,5},{5,6},{6,7},{7,4},{8,9},{9,10},{10,1... | collective-permute-start | bytes 1572872 | tf_op jit(solution)/shard_map/ppermute | solution.py:41
  51.8 14.8 %collective-permute-start.8 = (bf16[512,256]{1,0:T(8,128)(2,1)}, bf16[512,256]{1,0:T(8,128)(2,1)}, u32[]{:S(2)}, u32[]{:S(2)}) collective-permute-start(bf16[512,256]{1,0:T(8,128)(2,1)} %get-tuple-element.194), channel_id=1, source_target_pairs={{0,8},{4,0},{8,12},{12,4},{1,9},{5,1},{9,13},{13,5},{2,10},{6,2},{... | collective-permute-start | bytes 786440 | tf_op jit(solution)/shard_map/ppermute | solution.py:104
  51.8 14.8 %collective-permute-start.7 = (bf16[512,256]{1,0:T(8,128)(2,1)}, bf16[512,256]{1,0:T(8,128)(2,1)}, u32[]{:S(2)}, u32[]{:S(2)}) collective-permute-start(bf16[512,256]{1,0:T(8,128)(2,1)} %get-tuple-element.193), channel_id=1, source_target_pairs={{0,0},{4,8},{8,4},{12,12},{1,1},{5,9},{9,5},{13,13},{2,2},{6,10},{... | collective-permute-start | bytes 786440 | tf_op jit(solution)/shard_map/ppermute | solution.py:104
  70.6 18.7 %collective-permute-start.11 = (bf16[1024,768]{1,0:T(8,128)(2,1)}, bf16[1024,768]{1,0:T(8,128)(2,1)}, u32[]{:S(2)}, u32[]{:S(2)}) collective-permute-start(bf16[1024,768]{1,0:T(8,128)(2,1)} %get-tuple-element.99.refs_3_.refs_12_), channel_id=1, source_target_pairs={{0,8},{8,0},{1,9},{9,1},{2,10},{10,2},{3,11},{11,3},{4,12},{12,4},... | collective-permute-start | bytes 4718600 | tf_op jit(solution)/shard_map/ppermute | solution.py:45
  75.0 14.3 %collective-permute-start.12 = (bf16[128,2048]{1,0:T(8,128)(2,1)}, bf16[128,2048]{1,0:T(8,128)(2,1)S(1)}, u32[]{:S(2)}, u32[]{:S(2)}) collective-permute-start(bf16[128,2048]{1,0:T(8,128)(2,1)} %constant_dynamic-slice_fusion.7), channel_id=1, source_target_pairs={{0,68},{4,64},{64,4},{68,0},{1,69},{5,65},{65,5},{69,1},{2,70},{6,... | collective-permute-start | bytes 1572872 | tf_op jit(solution)/shard_map/ppermute | solution.py:49
  77.8 30.3 %collective-permute-start.18 = (f32[2,256]{1,0:T(2,128)}, f32[2,256]{1,0:T(2,128)S(1)}, u32[]{:S(2)}, u32[]{:S(2)}) collective-permute-start(f32[2,256]{1,0:T(2,128)} %pad_maximum_fusion.8), channel_id=1, source_target_pairs={{0,68},{4,64},{64,4},{68,0},{1,69},{5,65},{65,5},{69,1},{2,70},{6,... | collective-permute-start | bytes 6152 | tf_op jit(solution)/shard_map/ppermute | solution.py:49
  80.1 32.4 %collective-permute-start.9 = (bf16[2,512,256]{2,1,0:T(8,128)(2,1)}, bf16[2,512,256]{2,1,0:T(8,128)(2,1)S(1)}, u32[]{:S(2)}, u32[]{:S(2)}) collective-permute-start(bf16[2,512,256]{2,1,0:T(8,128)(2,1)} %get-tuple-element.98.own), channel_id=1, source_target_pairs={{0,3},{1,0},{2,1},{3,2},{4,7},{5,4},{6,5},{7,6},{8,11},{9,8},{10,9... | collective-permute-start | bytes 1572872 | tf_op jit(solution)/shard_map/ppermute | solution.py:41
  82.6 30.0 %collective-permute-start.10 = (bf16[2,512,256]{2,1,0:T(8,128)(2,1)}, bf16[2,512,256]{2,1,0:T(8,128)(2,1)}, u32[]{:S(2)}, u32[]{:S(2)}) collective-permute-start(bf16[2,512,256]{2,1,0:T(8,128)(2,1)} %get-tuple-element.98.own), channel_id=1, source_target_pairs={{0,1},{1,2},{2,3},{3,0},{4,5},{5,6},{6,7},{7,4},{8,9},{9,10},{10,1... | collective-permute-start | bytes 1572872 | tf_op jit(solution)/shard_map/ppermute | solution.py:41
  120.4 13.0 %collective-permute-start.19 = (bf16[512,1280]{1,0:T(8,128)(2,1)}, bf16[512,1280]{1,0:T(8,128)(2,1)}, u32[]{:S(2)}, u32[]{:S(2)}) collective-permute-start(bf16[512,1280]{1,0:T(8,128)(2,1)} %get-tuple-element.106), channel_id=1, source_target_pairs={{0,8},{8,0},{1,9},{9,1},{2,10},{10,2},{3,11},{11,3},{4,12},{12,4},... | collective-permute-start | bytes 3932168 | tf_op jit(solution)/shard_map/ppermute | solution.py:45
  130.3 71.3 %collective-permute-start.30 = (bf16[2,2048,256]{2,1,0:T(8,128)(2,1)}, bf16[2,2048,256]{2,1,0:T(8,128)(2,1)}, u32[]{:S(2)}, u32[]{:S(2)}) collective-permute-start(bf16[2,2048,256]{2,1,0:T(8,128)(2,1)} %pad_maximum_fusion), channel_id=1, source_target_pairs={{0,68},{4,64},{64,4},{68,0},{1,69},{5,65},{65,5},{69,1},{2,70},{6,... | collective-permute-start | bytes 6291464 | tf_op jit(solution)/shard_map/ppermute | solution.py:49
  143.4 14.6 %collective-permute-start.22 = (bf16[128,2048]{1,0:T(8,128)(2,1)}, bf16[128,2048]{1,0:T(8,128)(2,1)S(1)}, u32[]{:S(2)}, u32[]{:S(2)}) collective-permute-start(bf16[128,2048]{1,0:T(8,128)(2,1)} %get-tuple-element.110.near), channel_id=1, source_target_pairs={{0,8},{8,0},{1,9},{9,1},{2,10},{10,2},{3,11},{11,3},{4,12},{12,4},... | collective-permute-start | bytes 1572872 | tf_op jit(solution)/shard_map/ppermute | solution.py:45
  161.1 14.8 %collective-permute-start.23 = (bf16[128,2048]{1,0:T(8,128)(2,1)S(1)}, bf16[128,2048]{1,0:T(8,128)(2,1)S(1)}, u32[]{:S(2)}, u32[]{:S(2)}) collective-permute-start(bf16[128,2048]{1,0:T(8,128)(2,1)S(1)} %get-tuple-element.112), channel_id=1, source_target_pairs={{0,1},{1,2},{2,3},{3,0},{4,5},{5,6},{6,7},{7,4},{8,9},{9,10},{10,1... | collective-permute-start | bytes 1572872 | tf_op jit(solution)/shard_map/ppermute | solution.py:41
  161.2 23.3 %collective-permute-start.24 = (bf16[128,2048]{1,0:T(8,128)(2,1)S(1)}, bf16[128,2048]{1,0:T(8,128)(2,1)S(1)}, u32[]{:S(2)}, u32[]{:S(2)}) collective-permute-start(bf16[128,2048]{1,0:T(8,128)(2,1)S(1)} %get-tuple-element.113), channel_id=1, source_target_pairs={{0,2},{1,3},{2,0},{3,1},{4,6},{5,7},{6,4},{7,5},{8,10},{9,11},{10,... | collective-permute-start | bytes 1572872 | tf_op jit(solution)/shard_map/ppermute | solution.py:41
  162.5 24.1 %collective-permute-start.25 = (bf16[128,2048]{1,0:T(8,128)(2,1)S(1)}, bf16[128,2048]{1,0:T(8,128)(2,1)S(1)}, u32[]{:S(2)}, u32[]{:S(2)}) collective-permute-start(bf16[128,2048]{1,0:T(8,128)(2,1)S(1)} %get-tuple-element.114), channel_id=1, source_target_pairs={{0,3},{1,0},{2,1},{3,2},{4,7},{5,4},{6,5},{7,6},{8,11},{9,8},{10,9... | collective-permute-start | bytes 1572872 | tf_op jit(solution)/shard_map/ppermute | solution.py:41
  164.1 37.5 %collective-permute-start.31 = (bf16[2,128,2048]{2,1,0:T(8,128)(2,1)S(1)}, bf16[2,128,2048]{2,1,0:T(8,128)(2,1)S(1)}, u32[]{:S(2)}, u32[]{:S(2)}) collective-permute-start(bf16[2,128,2048]{2,1,0:T(8,128)(2,1)S(1)} %constant_dynamic-slice_fusion.2), channel_id=1, source_target_pairs={{0,68},{4,64},{64,4},{68,0},{1,69},{5,65},{65,5},{69,1},{2,70},{6,... | collective-permute-start | bytes 3145736 | tf_op jit(solution)/shard_map/ppermute | solution.py:49
  189.4 14.0 %collective-permute-start.26 = (bf16[128,2048]{1,0:T(8,128)(2,1)S(1)}, bf16[128,2048]{1,0:T(8,128)(2,1)S(1)}, u32[]{:S(2)}, u32[]{:S(2)}) collective-permute-start(bf16[128,2048]{1,0:T(8,128)(2,1)S(1)} %get-tuple-element.116.own_rows), channel_id=1, source_target_pairs={{0,3},{1,0},{2,1},{3,2},{4,7},{5,4},{6,5},{7,6},{8,11},{9,8},{10,9... | collective-permute-start | bytes 1572872 | tf_op jit(solution)/shard_map/ppermute | solution.py:41
  192.8 13.7 %collective-permute-start.28 = (bf16[128,2048]{1,0:T(8,128)(2,1)S(1)}, bf16[128,2048]{1,0:T(8,128)(2,1)S(1)}, u32[]{:S(2)}, u32[]{:S(2)}) collective-permute-start(bf16[128,2048]{1,0:T(8,128)(2,1)S(1)} %get-tuple-element.116.own_rows), channel_id=1, source_target_pairs={{0,1},{1,2},{2,3},{3,0},{4,5},{5,6},{6,7},{7,4},{8,9},{9,10},{10,1... | collective-permute-start | bytes 1572872 | tf_op jit(solution)/shard_map/ppermute | solution.py:41
  207.3 18.3 %collective-permute-start.33 = (bf16[2,2048,256]{2,1,0:T(8,128)(2,1)}, bf16[2,2048,256]{2,1,0:T(8,128)(2,1)}, u32[]{:S(2)}, u32[]{:S(2)}) collective-permute-start(bf16[2,2048,256]{2,1,0:T(8,128)(2,1)} %get-tuple-element.121.near), channel_id=1, source_target_pairs={{0,8},{8,0},{1,9},{9,1},{2,10},{10,2},{3,11},{11,3},{4,12},{12,4},... | collective-permute-start | bytes 6291464 | tf_op jit(solution)/shard_map/ppermute | solution.py:45
  210.6 43.7 %collective-permute-start.39 = (bf16[512,2048]{1,0:T(8,128)(2,1)}, bf16[512,2048]{1,0:T(8,128)(2,1)S(1)}, u32[]{:S(2)}, u32[]{:S(2)}) collective-permute-start(bf16[512,2048]{1,0:T(8,128)(2,1)} %get-tuple-element.117.cot), channel_id=1, source_target_pairs={{0,8},{8,0},{1,9},{9,1},{2,10},{10,2},{3,11},{11,3},{4,12},{12,4},... | collective-permute-start | bytes 6291464 | tf_op jit(solution)/shard_map/ppermute | solution.py:45
  211.6 14.0 %collective-permute-start.27 = (bf16[64,2048]{1,0:T(8,128)(2,1)S(1)}, bf16[64,2048]{1,0:T(8,128)(2,1)S(1)}, u32[]{:S(2)}, u32[]{:S(2)}) collective-permute-start(bf16[64,2048]{1,0:T(8,128)(2,1)S(1)} %slice.154), channel_id=1, source_target_pairs={{0,3},{1,0},{2,1},{3,2},{4,7},{5,4},{6,5},{7,6},{8,11},{9,8},{10,9... | collective-permute-start | bytes 786440 | tf_op jit(solution)/shard_map/ppermute | solution.py:41
  212.5 13.1 %collective-permute-start.29 = (bf16[64,2048]{1,0:T(8,128)(2,1)S(1)}, bf16[64,2048]{1,0:T(8,128)(2,1)S(1)}, u32[]{:S(2)}, u32[]{:S(2)}) collective-permute-start(bf16[64,2048]{1,0:T(8,128)(2,1)S(1)} %slice.155), channel_id=1, source_target_pairs={{0,1},{1,2},{2,3},{3,0},{4,5},{5,6},{6,7},{7,4},{8,9},{9,10},{10,1... | collective-permute-start | bytes 786440 | tf_op jit(solution)/shard_map/ppermute | solution.py:41
  244.1 15.3 %collective-permute-start.38 = (bf16[512,2048]{1,0:T(8,128)(2,1)S(1)}, bf16[512,2048]{1,0:T(8,128)(2,1)S(1)}, u32[]{:S(2)}, u32[]{:S(2)}) collective-permute-start(bf16[512,2048]{1,0:T(8,128)(2,1)S(1)} %get-tuple-element.134), channel_id=1, source_target_pairs={{0,8},{8,0},{1,9},{9,1},{2,10},{10,2},{3,11},{11,3},{4,12},{12,4},... | collective-permute-start | bytes 6291464 | tf_op jit(solution)/shard_map/ppermute | solution.py:45
  244.2 21.3 %collective-permute-start.34 = (bf16[128,2048]{1,0:T(8,128)(2,1)}, bf16[128,2048]{1,0:T(8,128)(2,1)S(1)}, u32[]{:S(2)}, u32[]{:S(2)}) collective-permute-start(bf16[128,2048]{1,0:T(8,128)(2,1)} %get-tuple-element.129), channel_id=1, source_target_pairs={{0,1},{1,2},{2,3},{3,0},{4,5},{5,6},{6,7},{7,4},{8,9},{9,10},{10,1... | collective-permute-start | bytes 1572872 | tf_op jit(solution)/shard_map/ppermute | solution.py:41
  244.2 25.1 %collective-permute-start.35 = (bf16[128,2048]{1,0:T(8,128)(2,1)}, bf16[128,2048]{1,0:T(8,128)(2,1)S(1)}, u32[]{:S(2)}, u32[]{:S(2)}) collective-permute-start(bf16[128,2048]{1,0:T(8,128)(2,1)} %get-tuple-element.130), channel_id=1, source_target_pairs={{0,2},{1,3},{2,0},{3,1},{4,6},{5,7},{6,4},{7,5},{8,10},{9,11},{10,... | collective-permute-start | bytes 1572872 | tf_op jit(solution)/shard_map/ppermute | solution.py:41
  253.3 17.2 %collective-permute-start.36 = (bf16[128,2048]{1,0:T(8,128)(2,1)}, bf16[128,2048]{1,0:T(8,128)(2,1)S(1)}, u32[]{:S(2)}, u32[]{:S(2)}) collective-permute-start(bf16[128,2048]{1,0:T(8,128)(2,1)} %get-tuple-element.131), channel_id=1, source_target_pairs={{0,3},{1,0},{2,1},{3,2},{4,7},{5,4},{6,5},{7,6},{8,11},{9,8},{10,9... | collective-permute-start | bytes 1572872 | tf_op jit(solution)/shard_map/ppermute | solution.py:41
  275.9 175.5 %all-reduce.4.cloned.1.call-start = ((), (), s32[]{:S(2)}) async-start(), calls=%async_computation.1 | async-start | bytes 12582912 | tf_op jit(solution)/shard_map/psum | solution.py:1124
  276.9 14.1 %collective-permute-start.40 = (bf16[128,2048]{1,0:T(8,128)(2,1)S(1)}, bf16[128,2048]{1,0:T(8,128)(2,1)S(1)}, u32[]{:S(2)}, u32[]{:S(2)}) collective-permute-start(bf16[128,2048]{1,0:T(8,128)(2,1)S(1)} %copy-done.105), channel_id=1, source_target_pairs={{0,3},{1,0},{2,1},{3,2},{4,7},{5,4},{6,5},{7,6},{8,11},{9,8},{10,9... | collective-permute-start | bytes 1572872 | tf_op jit(solution)/shard_map/ppermute | solution.py:41
  280.2 14.3 %collective-permute-start.42 = (bf16[128,2048]{1,0:T(8,128)(2,1)S(1)}, bf16[128,2048]{1,0:T(8,128)(2,1)S(1)}, u32[]{:S(2)}, u32[]{:S(2)}) collective-permute-start(bf16[128,2048]{1,0:T(8,128)(2,1)S(1)} %copy-done.105), channel_id=1, source_target_pairs={{0,1},{1,2},{2,3},{3,0},{4,5},{5,6},{6,7},{7,4},{8,9},{9,10},{10,1... | collective-permute-start | bytes 1572872 | tf_op jit(solution)/shard_map/ppermute | solution.py:41
  313.4 16.3 %collective-permute-start.46 = (bf16[128,2048]{1,0:T(8,128)(2,1)}, bf16[128,2048]{1,0:T(8,128)(2,1)S(1)}, u32[]{:S(2)}, u32[]{:S(2)}) collective-permute-start(bf16[128,2048]{1,0:T(8,128)(2,1)} %get-tuple-element.146), channel_id=1, source_target_pairs={{0,1},{1,2},{2,3},{3,0},{4,5},{5,6},{6,7},{7,4},{8,9},{9,10},{10,1... | collective-permute-start | bytes 1572872 | tf_op jit(solution)/shard_map/ppermute | solution.py:41
  313.4 17.1 %collective-permute-start.47 = (bf16[128,2048]{1,0:T(8,128)(2,1)}, bf16[128,2048]{1,0:T(8,128)(2,1)S(1)}, u32[]{:S(2)}, u32[]{:S(2)}) collective-permute-start(bf16[128,2048]{1,0:T(8,128)(2,1)} %get-tuple-element.147), channel_id=1, source_target_pairs={{0,3},{1,0},{2,1},{3,2},{4,7},{5,4},{6,5},{7,6},{8,11},{9,8},{10,9... | collective-permute-start | bytes 1572872 | tf_op jit(solution)/shard_map/ppermute | solution.py:41
  316.1 32.2 %collective-permute-start.21 = (bf16[512,2048]{1,0:T(8,128)(2,1)S(1)}, bf16[512,2048]{1,0:T(8,128)(2,1)}, u32[]{:S(2)}, u32[]{:S(2)}) collective-permute-start(bf16[512,2048]{1,0:T(8,128)(2,1)S(1)} %copy-done.4), channel_id=1, source_target_pairs={{0,8},{8,0},{1,9},{9,1},{2,10},{10,2},{3,11},{11,3},{4,12},{12,4},... | collective-permute-start | bytes 6291464 | tf_op jit(solution)/shard_map/ppermute | solution.py:45
  317.0 33.1 %collective-permute-start.45 = (bf16[512,2048]{1,0:T(8,128)(2,1)}, bf16[512,2048]{1,0:T(8,128)(2,1)}, u32[]{:S(2)}, u32[]{:S(2)}) collective-permute-start(bf16[512,2048]{1,0:T(8,128)(2,1)} %get-tuple-element.138.refs_2_), channel_id=1, source_target_pairs={{0,8},{8,0},{1,9},{9,1},{2,10},{10,2},{3,11},{11,3},{4,12},{12,4},... | collective-permute-start | bytes 6291464 | tf_op jit(solution)/shard_map/ppermute | solution.py:45
  366.6 15.9 %collective-permute-start.54 = (bf16[144,2048]{1,0:T(8,128)(2,1)S(1)}, bf16[144,2048]{1,0:T(8,128)(2,1)S(1)}, u32[]{:S(2)}, u32[]{:S(2)}) collective-permute-start(bf16[144,2048]{1,0:T(8,128)(2,1)S(1)} %get-tuple-element.155), channel_id=1, source_target_pairs={{0,1},{1,2},{2,3},{3,0},{4,5},{5,6},{6,7},{7,4},{8,9},{9,10},{10,1... | collective-permute-start | bytes 1769480 | tf_op jit(solution)/shard_map/ppermute | solution.py:41
  367.2 76.5 %collective-permute-start.55 = (bf16[272,2048]{1,0:T(8,128)(2,1)S(1)}, bf16[272,2048]{1,0:T(8,128)(2,1)S(1)}, u32[]{:S(2)}, u32[]{:S(2)}) collective-permute-start(bf16[272,2048]{1,0:T(8,128)(2,1)S(1)} %get-tuple-element.156), channel_id=1, source_target_pairs={{0,2},{1,3},{2,0},{3,1},{4,6},{5,7},{6,4},{7,5},{8,10},{9,11},{10,... | collective-permute-start | bytes 3342344 | tf_op jit(solution)/shard_map/ppermute | solution.py:41
  369.5 42.2 %collective-permute-start.57 = (bf16[512,1024]{1,0:T(8,128)(2,1)S(1)}, bf16[512,1024]{1,0:T(8,128)(2,1)S(1)}, u32[]{:S(2)}, u32[]{:S(2)}) collective-permute-start(bf16[512,1024]{1,0:T(8,128)(2,1)S(1)} %get-tuple-element.160), channel_id=1, source_target_pairs={{0,16},{16,32},{32,48},{48,0},{1,17},{17,33},{33,49},{49,1},{2,18}... | collective-permute-start | bytes 3145736 | tf_op jit(solution)/shard_map/ppermute | solution.py:41
  370.8 72.8 %collective-permute-start.58 = (bf16[512,1024]{1,0:T(8,128)(2,1)S(1)}, bf16[512,1024]{1,0:T(8,128)(2,1)S(1)}, u32[]{:S(2)}, u32[]{:S(2)}) collective-permute-start(bf16[512,1024]{1,0:T(8,128)(2,1)S(1)} %get-tuple-element.161), channel_id=1, source_target_pairs={{0,32},{16,48},{32,0},{48,16},{1,33},{17,49},{33,1},{49,17},{2,34}... | collective-permute-start | bytes 3145736 | tf_op jit(solution)/shard_map/ppermute | solution.py:41
  373.5 70.1 %collective-permute-start.59 = (bf16[512,1024]{1,0:T(8,128)(2,1)S(1)}, bf16[512,1024]{1,0:T(8,128)(2,1)S(1)}, u32[]{:S(2)}, u32[]{:S(2)}) collective-permute-start(bf16[512,1024]{1,0:T(8,128)(2,1)S(1)} %get-tuple-element.162), channel_id=1, source_target_pairs={{0,48},{16,0},{32,16},{48,32},{1,49},{17,1},{33,17},{49,33},{2,50}... | collective-permute-start | bytes 3145736 | tf_op jit(solution)/shard_map/ppermute | solution.py:41
  382.5 24.2 %collective-permute-start.56 = (bf16[144,2048]{1,0:T(8,128)(2,1)S(1)}, bf16[144,2048]{1,0:T(8,128)(2,1)S(1)}, u32[]{:S(2)}, u32[]{:S(2)}) collective-permute-start(bf16[144,2048]{1,0:T(8,128)(2,1)S(1)} %get-tuple-element.157), channel_id=1, source_target_pairs={{0,3},{1,0},{2,1},{3,2},{4,7},{5,4},{6,5},{7,6},{8,11},{9,8},{10,9... | collective-permute-start | bytes 1769480 | tf_op jit(solution)/shard_map/ppermute | solution.py:41
  451.5 50.3 %collective-permute-start.69 = (bf16[2,2048,512]{2,1,0:T(8,128)(2,1)}, bf16[2,2048,512]{2,1,0:T(8,128)(2,1)}, u32[]{:S(2)}, u32[]{:S(2)}) collective-permute-start(bf16[2,2048,512]{2,1,0:T(8,128)(2,1)} %get-tuple-element.167.gu_mine), channel_id=1, source_target_pairs={{0,8},{12,4},{1,9},{13,5},{2,10},{14,6},{3,11},{15,7},{16,24},{28,... | collective-permute-start | bytes 12582920 | tf_op jit(solution)/shard_map/ppermute | solution.py:149
  457.5 16.3 %collective-permute-start.60 = (bf16[256,1024]{1,0:T(8,128)(2,1)S(1)}, bf16[256,1024]{1,0:T(8,128)(2,1)S(1)}, u32[]{:S(2)}, u32[]{:S(2)}) collective-permute-start(bf16[256,1024]{1,0:T(8,128)(2,1)S(1)} %get-tuple-element.189), channel_id=1, source_target_pairs={{4,8},{8,4},{68,72},{72,68},{5,9},{9,5},{69,73},{73,69},{6,10},{10... | collective-permute-start | bytes 1572872 | tf_op jit(solution)/shard_map/ppermute | solution.py:139
  459.4 36.7 %collective-permute-start.70 = (bf16[2,256,2048]{2,1,0:T(8,128)(2,1)}, bf16[2,256,2048]{2,1,0:T(8,128)(2,1)}, u32[]{:S(2)}, u32[]{:S(2)}) collective-permute-start(bf16[2,256,2048]{2,1,0:T(8,128)(2,1)} %get-tuple-element.168.down_mine), channel_id=1, source_target_pairs={{0,8},{12,4},{1,9},{13,5},{2,10},{14,6},{3,11},{15,7},{16,24},{28,... | collective-permute-start | bytes 6291464 | tf_op jit(solution)/shard_map/ppermute | solution.py:149
  460.7 20.9 %all-to-all-start = ((bf16[8,2,128,256]{3,2,1,0:T(8,128)(2,1)}), bf16[8,2,128,256]{3,2,1,0:T(8,128)(2,1)S(1)}, u32[]{:S(2)}, u32[]{:S(2)}) async-start(bf16[8,2,128,256]{3,2,1,0:T(8,128)(2,1)} %get-tuple-element.163.refs_2_), calls=%async_computation | async-start | bytes 2097152 | tf_op jit(solution)/shard_map/all_to_all | solution.py:109
  492.0 21.5 %collective-permute-start.66 = (bf16[2,144,1024]{2,1,0:T(8,128)(2,1)S(1)}, bf16[2,144,1024]{2,1,0:T(8,128)(2,1)S(1)}, u32[]{:S(2)}, u32[]{:S(2)}) collective-permute-start(bf16[2,144,1024]{2,1,0:T(8,128)(2,1)S(1)} %pad_maximum_fusion.2.refs_1_.refs_0_), channel_id=1, source_target_pairs={{0,48},{16,0},{32,16},{48,32},{1,49},{17,1},{33,17},{49,33},{2,50}... | collective-permute-start | bytes 1769480 | tf_op jit(solution)/shard_map/ppermute | solution.py:41
  492.1 21.5 %collective-permute-start.67 = (bf16[2,144,1024]{2,1,0:T(8,128)(2,1)S(1)}, bf16[2,144,1024]{2,1,0:T(8,128)(2,1)S(1)}, u32[]{:S(2)}, u32[]{:S(2)}) collective-permute-start(bf16[2,144,1024]{2,1,0:T(8,128)(2,1)S(1)} %pad_maximum_fusion.2.refs_1_.refs_0_), channel_id=1, source_target_pairs={{0,32},{16,48},{32,0},{48,16},{1,33},{17,49},{33,1},{49,17},{2,34}... | collective-permute-start | bytes 1769480 | tf_op jit(solution)/shard_map/ppermute | solution.py:41
  494.0 27.5 %collective-permute-start.68 = (bf16[2,144,1024]{2,1,0:T(8,128)(2,1)S(1)}, bf16[2,144,1024]{2,1,0:T(8,128)(2,1)S(1)}, u32[]{:S(2)}, u32[]{:S(2)}) collective-permute-start(bf16[2,144,1024]{2,1,0:T(8,128)(2,1)S(1)} %pad_maximum_fusion.2.refs_1_.refs_0_), channel_id=1, source_target_pairs={{0,16},{16,32},{32,48},{48,0},{1,17},{17,33},{33,49},{49,1},{2,18}... | collective-permute-start | bytes 1769480 | tf_op jit(solution)/shard_map/ppermute | solution.py:41
  496.1 27.3 %collective-permute-start.65 = (bf16[2,1024,256]{2,1,0:T(8,128)(2,1)S(1)}, bf16[2,1024,256]{2,1,0:T(8,128)(2,1)}, u32[]{:S(2)}, u32[]{:S(2)}) collective-permute-start(bf16[2,1024,256]{2,1,0:T(8,128)(2,1)S(1)} %bitcast.72), channel_id=1, source_target_pairs={{4,8},{8,4},{5,9},{9,5},{6,10},{10,6},{7,11},{11,7},{20,24},{24,20... | collective-permute-start | bytes 3145736 | tf_op jit(solution)/shard_map/ppermute | solution.py:114
  (146 other events, 1390.6 us)
Sparse Core Ops, SparseCore 0:
  281.4 166.8 all-reduce.3
where the time goes:
time: 556 us; the launch traced here: 545 us
  waiting for transfers between devices  203 us (37%)
  Pallas kernels  116 us (21%)
  starting transfers between devices  105 us (19%)
  local copies, waits for them, and re-layouts  76.2 us (14%)
  between operations  20.9 us (4%)
  other arithmetic  14.2 us (3%)
  matrix products  10.3 us (2%)
    ppermute x39, waiting for transfers between devices, along(): lax.ppermute(value, axis, [(i, (i + shift) % size) for i in range(size)])  152 us
    unnamed x244, local copies, waits for them, and re-layouts  53.1 us
    ppermute x39, starting transfers between devices, along(): lax.ppermute(value, axis, [(i, (i + shift) % size) for i in range(size)])  47 us
    pallas_call x1, Pallas kernels, expert_layer(): call(expert_kernel, (4,), [whole(n, width) for n in (128, 128, 64, 64, 12...  18 us
    ppermute x5, waiting for transfers between devices, other_half_chip(): return lax.ppermute(value, ('zl', 'zh'), [(i, 3 - i) for i in range(4)])  16.4 us
    pallas_call x1, Pallas kernels, back(): call(back_kernel, (width // step,), [block(), block(), block(), block()]...  15.6 us
    ppermute x20, starting transfers between devices, other_core(): return lax.ppermute(value, 'c', [(0, 1), (1, 0)])  15.4 us
    ppermute x4, starting transfers between devices, deal_in(): got.append(lax.ppermute(part, ('c', 'zh'), pairs))  11.8 us
  transfers between devices with their start and end apart: 77, of which 40 were waited for; matrix products, arithmetic and copies ran while one was open for 8% of the time, Pallas kernels for 19%

commit v1 on v0

--- a/solution.py
+++ b/solution.py
@@ -33,7 +33,7 @@
     angles = np.arange(length, dtype=np.float32)[:, None] * frequency[None, :]
     cosine = np.cos(angles.astype(np.float64)).astype(np.float32)
     sine = np.sin(angles.astype(np.float64)).astype(np.float32)
-    return np.concatenate([cosine, cosine], 1), np.concatenate([-sine, sine], 1)
+    return np.concatenate([cosine, cosine, -sine, sine], 1)
 
 
 def along(value, axis, shift):
@@ -124,7 +124,13 @@
 
 
 def send_y(pieces):
-    return [pieces[0]] + [along(pieces[r], "y", r) for r in (1, 2, 3)]
+    own, after, far, before = pieces
+    half = far.shape[0] // 2
+    up, down = along(far[:half], "y", 1), along(far[half:], "y", -1)
+    add = lambda a, b: (a.astype(F32) + b.astype(F32)).astype(a.dtype)
+    after = jnp.concatenate([add(after[:half], up), after[half:]], 0)
+    before = jnp.concatenate([before[:half], add(before[half:], down)], 0)
+    return [own, along(after, "y", 1), along(before, "y", -1)]
 
 
 def to_shard(value, zl, same):
@@ -337,7 +343,8 @@
     return jnp.concatenate([rows_two, rest], 0).T
 
 
-def prep_kernel(place, raw_send, raw_keep, inv_rows, gains, cosine, sine, first, second, out_send, out_keep):
+def prep_kernel(place, raw_send, raw_keep, inv_rows, gains, table, first, second, out_send, out_keep):
+    cosine, sine = table[:, :128], table[:, 128:]
     inv = columns_of(inv_rows[...])
     for part, (raw, out) in enumerate(((raw_keep, out_keep), (raw_send, out_send))):
         for i in range(2):
@@ -347,12 +354,12 @@
                 out[:, 768 + lo : 896 + lo] = normed.astype(BF)
                 normed = normed * gains[part * 2 + i : part * 2 + i + 1, h * 128 : h * 128 + 128]
                 out[:, lo : lo + 128] = (
-                    normed * cosine[...] + pltpu.roll(normed, 64, 1) * sine[...]
+                    normed * cosine + pltpu.roll(normed, 64, 1) * sine
                 ).astype(BF)
         out[:, 512:768] = raw[:, 512:768].astype(BF)
 
 
-def prep(raw_send, raw_keep, inv_rows, gains, cosine, sine, awaited, place):
+def prep(raw_send, raw_keep, inv_rows, gains, table, awaited, place):
     rows, step = raw_send.shape[0], 128
     spec = lambda width: pl.BlockSpec((step, width), lambda i, p: (i, 0))
     return call(
@@ -363,14 +370,13 @@
             spec(768),
             pl.BlockSpec((2, step), lambda i, p: (0, i)),
             whole(4, 256),
-            spec(128),
-            spec(128),
+            pl.BlockSpec((step, 256), lambda i, p: (p[1] * 4 + i, 0)),
             ANYWHERE,
             ANYWHERE,
         ],
         [spec(1280), spec(1280)],
         [shape(rows, 1280), shape(rows, 1280)],
-    )(place, raw_send, raw_keep, inv_rows, gains, cosine, sine, *awaited)
+    )(place, raw_send, raw_keep, inv_rows, gains, table, *awaited)
 
 
 def attend_kernel(place, mine, rest, bias, qkv, out_mine, out_rest, lse):
@@ -679,12 +685,14 @@
 
 
 def attend_back_kernel(
-    place, qkv, d_mine, d_rest, heads_mine, heads_rest, bias, lse, cosine, sine, d_query, d_key, d_value, sums, key_sum, value_sum
+    place, qkv, d_mine, d_rest, heads_mine, heads_rest, bias, lse, table_mine, table_rest,
+    d_query, d_key, d_value, sums, key_sum, value_sum,
 ):
     rows = 256
 
-    def unturn(grad, here):
-        return grad * cosine[here, :] - pltpu.roll(grad, 64, 1) * sine[here, :]
+    def unturn(grad, i):
+        table = (table_mine if i < 2 else table_rest)[i % 2 * rows : i % 2 * rows + rows, :]
+        return grad * table[:, :128] - pltpu.roll(grad, 64, 1) * table[:, 128:]
 
     masked = jnp.broadcast_to(bias[...], (8, 1024)).T[:, 0:1]
     for h in range(2):
@@ -717,7 +725,7 @@
                 sums[0:1, here] = inner
             else:
                 sums[0:1, here] += inner
-            d_query[here, cols] = unturn(d_turned.T, here)
+            d_query[here, cols] = unturn(d_turned.T, i)
         d_value[:, cols] = value_sum[...].astype(BF)
         for i in range(4):
             here = slice(i * rows, (i + 1) * rows)
@@ -728,16 +736,20 @@
                 sums[1:2, here] = inner
             else:
                 sums[1:2, here] += inner
-            d_key[here, cols] = unturn(d_rot, here)
-
-
-def attend_back(qkv, d_mine, d_rest, heads_mine, heads_rest, bias, lse, cosine, sine, place):
+            d_key[here, cols] = unturn(d_rot, i)
+
+
+def attend_back(qkv, d_mine, d_rest, heads_mine, heads_rest, bias, lse, table, place):
     return call(
         attend_back_kernel,
         (1,),
         [whole(1024, 1280)]
         + [whole(512, 256)] * 4
-        + [whole(1, 1024), whole(2, 1024), whole(1024, 128), whole(1024, 128)],
+        + [whole(1, 1024), whole(2, 1024)]
+        + [
+            pl.BlockSpec((512, 256), lambda i, p: (p[1], 0)),
+            pl.BlockSpec((512, 256), lambda i, p: (1 - p[1], 0)),
+        ],
         [whole(1024, 256), whole(1024, 256), whole(1024, 256), whole(2, 1024)],
         [
             shape(1024, 256, dtype=F32),
@@ -747,7 +759,7 @@
         ],
         scratch=[pltpu.VMEM((1024, 128), F32), pltpu.VMEM((1024, 128), F32)],
         vmem=BIG,
-    )(place, qkv, d_mine, d_rest, heads_mine, heads_rest, bias, lse, cosine, sine)
+    )(place, qkv, d_mine, d_rest, heads_mine, heads_rest, bias, lse, table, table)
 
 
 def raw_back_kernel(
@@ -1038,11 +1050,7 @@
     gains_own = jnp.stack([gain_query, gain_key], 0)
     gains_other = other_half_chip(gains_own)
 
-    cosine_np, sine_np = rope_tables(length)
-    swap_halves = lambda t: lax.dynamic_slice_in_dim(
-        jnp.concatenate([t, t], 0), c * half, length, 0
-    )
-    cosine_all, sine_all = swap_halves(jnp.asarray(cosine_np)), swap_halves(jnp.asarray(sine_np))
+    table = jnp.asarray(rope_tables(length))
     positions = (jnp.arange(length, dtype=jnp.int32) + c * half) % length
     bias = jnp.where(positions < tokens_here, 0.0, -1e30).astype(F32)
     weight_all = choice_weights(ids_here, gates_here, experts, length * 2 // experts)
@@ -1069,8 +1077,7 @@
         raw_keep,
         inv_qk,
         gains_qk,
-        cosine_all[:half],
-        sine_all[:half],
+        table,
         (cot_pieces[1], cot_pieces[4]),
         place,
     )
@@ -1138,8 +1145,7 @@
         heads_rest,
         bias[None, :],
         lse,
-        cosine_all,
-        sine_all,
+        table,
         place,
     )
     (sums,) = tie([sums], moe_after)

time: 556 us -> 535 us (0.962)
  waiting for transfers between devices: 203 us -> 189 us
  local copies, waits for them, and re-layouts: 76.2 us -> 66.9 us
  starting transfers between devices: 105 us -> 111 us
    ppermute x39 -> x40, waiting for transfers between devices: 152 us -> 132 us  [along(): lax.ppermute(value, axis, [(i, (i + shift) % size) for i in range(size)])]
    ppermute x5, waiting for transfers between devices: 16.4 us -> 21.9 us  [other_half_chip(): return lax.ppermute(value, ('zl', 'zh'), [(i, 3 - i) for i in range(4)])]
    ppermute x39 -> x40, starting transfers between devices: 47 us -> 52 us  [along(): lax.ppermute(value, axis, [(i, (i + shift) % size) for i in range(size)])]
    unnamed x244 -> x234, local copies, waits for them, and re-layouts: 53.1 us -> 49.6 us
  transfers between devices with their start and end apart: 77 -> 78, of which waited for: 40 -> 40; matrix products, arithmetic and copies ran while one was open for 8% -> 7% of each run, Pallas kernels for 19% -> 19%
where the time goes in v1:
time: 535 us; the launch traced here: 525 us
  waiting for transfers between devices  189 us (35%)
  Pallas kernels  114 us (21%)
  starting transfers between devices  111 us (21%)
  local copies, waits for them, and re-layouts  66.9 us (13%)
  between operations  21 us (4%)
  other arithmetic  12.6 us (2%)
  matrix products  10.3 us (2%)
    ppermute x40, waiting for transfers between devices, along(): lax.ppermute(value, axis, [(i, (i + shift) % size) for i in range(size)])  132 us
    ppermute x40, starting transfers between devices, along(): lax.ppermute(value, axis, [(i, (i + shift) % size) for i in range(size)])  52 us
    unnamed x234, local copies, waits for them, and re-layouts  49.6 us
    ppermute x5, waiting for transfers between devices, other_half_chip(): return lax.ppermute(value, ('zl', 'zh'), [(i, 3 - i) for i in range(4)])  21.9 us
    pallas_call x1, Pallas kernels, expert_layer(): call(expert_kernel, (4,), [whole(n, width) for n in (128, 128, 64, 64, 12...  17.8 us
    ppermute x20, starting transfers between devices, other_core(): return lax.ppermute(value, 'c', [(0, 1), (1, 0)])  16.2 us
    pallas_call x1, Pallas kernels, back(): call(back_kernel, (width // step,), [block(), block(), block(), block()]...  15.6 us
    ppermute x4, starting transfers between devices, deal_in(): got.append(lax.ppermute(part, ('c', 'zh'), pairs))  11.8 us
  transfers between devices with their start and end apart: 78, of which 40 were waited for; matrix products, arithmetic and copies ran while one was open for 7% of the time, Pallas kernels for 19%

profile of v1, /device:TPU:1, one launch (start us, length us, event | category | flops | bytes accessed | tf_op | source)
XLA Modules:
  0.0 524.6 jit_solution(17348787097467819342)
XLA Ops:
  8.5 6.9 %collective-permute-start = (bf16[512,256]{1,0:T(8,128)(2,1)S(1)}, bf16[512,256]{1,0:T(8,128)(2,1)S(1)}, u32[]{:S(2)}, u32[]{:S(2)}) collective-permute-start(bf16[512,256]{1,0:T(8,128)(2,1)S(1)} %get-tuple-element.199), channel_id=1, source_target_pairs={{0,0},{4,8},{8,4},{12,12},{1,1},{5,9},{9,5},{13,13},{2,2},{6,10},{... | collective-permute-start | bytes 786440 | tf_op jit(solution)/shard_map/ppermute | solution.py:104
  15.5 3.9 collective-permute-done
  26.1 3.6 collective-permute-start.6
  32.2 10.9 %collective-permute-done.2.after = bf16[2,512,256]{2,1,0:T(8,128)(2,1)S(1)} collective-permute-done((bf16[2,512,256]{2,1,0:T(8,128)(2,1)S(1)}, bf16[2,512,256]{2,1,0:T(8,128)(2,1)S(1)}, u32[]{:S(2)}, u32[]{:S(2)}) %collective-permute-start.2) | collective-permute-done | bytes 524320 | tf_op jit(solution)/shard_map/ppermute | solution.py:41
  45.7 3.4 collective-permute-start.3
  51.8 4.9 collective-permute-start.7
  59.4 3.6 shard_map.264
  79.5 8.7 %collective-permute-done.12.refs_5_.refs_0_ = bf16[128,2048]{1,0:T(8,128)(2,1)S(1)} collective-permute-done((bf16[128,2048]{1,0:T(8,128)(2,1)S(1)}, bf16[128,2048]{1,0:T(8,128)(2,1)S(1)}, u32[]{:S(2)}, u32[]{:S(2)}) %collective-permute-start.12) | collective-permute-done | bytes 524320 | tf_op jit(solution)/shard_map/ppermute | solution.py:49
  93.5 7.7 %shard_map.266 = (f32[512,768]{1,0:T(8,128)S(1)}, f32[512,768]{1,0:T(8,128)S(1)}, f32[8,512]{1,0:T(8,128)S(1)}) custom-call(s32[6]{0:T(128)S(1)} %stack.67.place, bf16[512,2048]{1,0:T(8,128)(2,1)S(1)} %copy-done.3, bf16[2048,256]{1,0:T(8,128)(2,1)S(1)} %copy-done.29, bf16[2048,256]{1,0:T(8,128)(2,1)S(1)} %copy-done.22, bf16[2048,256]{1,0:T(8,128)(2,1)S(1)} %copy-done.25, ...), custom_call_target="tpu_custom_call" | custom-call | flops 1 | bytes 1 | tf_op jit(solution)/shard_map/pallas_call | solution.py:319
  115.0 3.1 shard_map.270
  118.1 3.3 collective-permute-start.19
  131.2 6.3 %shard_map.271 = (bf16[1024,1280]{1,0:T(8,128)(2,1)S(1)}, bf16[512,256]{1,0:T(8,128)(2,1)S(1)}, bf16[512,256]{1,0:T(8,128)(2,1)S(1)}, f32[2,1024]{1,0:T(2,128)S(1)}) custom-call(s32[6]{0:T(128)S(1)} %stack.67.place, bf16[512,1280]{1,0:T(8,128)(2,1)S(1)} %get-tuple-element.105.mine, bf16[512,1280]{1,0:T(8,128)(2,1)} %collective-permute-done.19.rest, ...), custom_call_target="tpu_custom_call" | custom-call | flops 1 | bytes 1 | tf_op jit(solution)/shard_map/pallas_call | solution.py:405
  144.4 6.5 %collective-permute-done.16.far_low = bf16[1,512,256]{2,1,0:T(8,128)(2,1)S(1)} collective-permute-done((bf16[1,512,256]{2,1,0:T(8,128)(2,1)}, bf16[1,512,256]{2,1,0:T(8,128)(2,1)S(1)}, u32[]{:S(2)}, u32[]{:S(2)}) %collective-permute-start.16) | collective-permute-done | bytes 262176 | tf_op jit(solution)/shard_map/ppermute | solution.py:41
  159.8 11.4 %collective-permute-done.23.b = bf16[128,2048]{1,0:T(8,128)(2,1)S(1)} collective-permute-done((bf16[128,2048]{1,0:T(8,128)(2,1)S(1)}, bf16[128,2048]{1,0:T(8,128)(2,1)S(1)}, u32[]{:S(2)}, u32[]{:S(2)}) %collective-permute-start.23) | collective-permute-done | bytes 524320 | tf_op jit(solution)/shard_map/ppermute | solution.py:41
  171.2 8.6 %collective-permute-done.24.c = bf16[128,2048]{1,0:T(8,128)(2,1)S(1)} collective-permute-done((bf16[128,2048]{1,0:T(8,128)(2,1)S(1)}, bf16[128,2048]{1,0:T(8,128)(2,1)S(1)}, u32[]{:S(2)}, u32[]{:S(2)}) %collective-permute-start.24) | collective-permute-done | bytes 524320 | tf_op jit(solution)/shard_map/ppermute | solution.py:41
  184.6 3.4 collective-permute-start.26
  188.0 11.4 %collective-permute-done.31.refs_1_ = bf16[2,128,2048]{2,1,0:T(8,128)(2,1)S(1)} collective-permute-done((bf16[2,128,2048]{2,1,0:T(8,128)(2,1)S(1)}, bf16[2,128,2048]{2,1,0:T(8,128)(2,1)S(1)}, u32[]{:S(2)}, u32[]{:S(2)}) %collective-permute-start.31) | collective-permute-done | bytes 1048608 | tf_op jit(solution)/shard_map/ppermute | solution.py:49
  214.7 4.8 shard_map.279.back
  220.8 17.8 %shard_map.280 = (bf16[2,512,768]{2,1,0:T(8,128)(2,1)S(1)}, bf16[2,512,768]{2,1,0:T(8,128)(2,1)S(1)}, bf16[512,2048]{1,0:T(8,128)(2,1)S(1)}, bf16[128,2048]{1,0:...) custom-call(s32[6]{0:T(128)S(1)} %stack.67.place, ...), custom_call_target="tpu_custom_call" | custom-call | flops 1 | bytes 1 | tf_op jit(solution)/shard_map/pallas_call | solution.py:618
  241.5 6.3 %shard_map.281 = (bf16[128,2048]{1,0:T(8,128)(2,1)S(1)}, bf16[128,2048]{1,0:T(8,128)(2,1)S(1)}, bf16[128,2048]{1,0:T(8,128)(2,1)S(1)}, bf16[128,2048]{1,0:T(8,128)(2,1)S(1)}) custom-call(s32[6]{0:T(128)S(1)} %stack.67.place, bf16[2,512,768]{2,1,0:T(8,128)(2,1)S(1)} %get-tuple-element.122.send, bf16[2,512,768]{2,1,0:T(8,128)(2,1)S(1)} %get-tuple-element.123.keep.awaited, ...), custom_call_target="tpu_custom_call" | custom-call | flops 5000000000 | bytes 1 | tf_op jit(solution)/shard_map/pallas_call | solution.py:669
  250.2 3.7 fusion.7.ready_b
  253.9 6.1 %convert_bitcast_fusion.ready_a = bf16[2,2048,512]{2,1,0:T(8,128)(2,1)} fusion(bf16[512,2048]{1,0:T(8,128)(2,1)S(1)} %collective-permute-done.38, bf16[512,2048]{1,0:T(8,128)(2,1)S(1)} %get-tuple-element.134, bf16[2,1024,768]{2,1,0:T(8,128)(2,1)S(1)} %constant_dynamic-update-slice_fusion), kind=kOutput, calls=%fused_computation.8 | convolution fusion | flops 4305453056 | bytes 10485760 | tf_op jit(solution)/shard_map/td,etf->edf/dot_general | solution.py:1115
  260.1 4.3 collective-permute-done.35.c
  266.3 4.5 shard_map.282
  271.9 3.4 collective-permute-start.40
  275.3 10.8 %collective-permute-done.40.after = bf16[128,2048]{1,0:T(8,128)(2,1)S(1)} collective-permute-done((bf16[128,2048]{1,0:T(8,128)(2,1)S(1)}, bf16[128,2048]{1,0:T(8,128)(2,1)S(1)}, u32[]{:S(2)}, u32[]{:S(2)}) %collective-permute-start.40) | collective-permute-done | bytes 524320 | tf_op jit(solution)/shard_map/ppermute | solution.py:41
  286.1 3.5 collective-permute-start.41
  289.9 3.9 collective-permute-done.41.far_low
  293.8 3.5 collective-permute-done.43.far_high
  298.1 5.8 %shard_map.283 = (bf16[512,256]{1,0:T(8,128)(2,1)}, bf16[512,256]{1,0:T(8,128)(2,1)}, bf16[512,2048]{1,0:T(8,128)(2,1)}) custom-call(s32[6]{0:T(128)} %copy-done.76, bf16[128,2048]{1,0:T(8,128)(2,1)} %get-tuple-element.135.own_rows, bf16[128,2048]{1,0:T(8,128)(2,1)} %copy-done.94, bf16[64,2048]{1,0:T(8,128)(2,1)} %copy-done.104, ...), custom_call_target="tpu_custom_call" | custom-call | flops 1 | bytes 1 | tf_op jit(solution)/shard_map/pallas_call | solution.py:466
  308.4 2.7 collective-permute-start.47
  312.0 10.5 %shard_map.285 = (f32[1024,256]{1,0:T(8,128)}, f32[1024,256]{1,0:T(8,128)}, bf16[1024,256]{1,0:T(8,128)(2,1)}, f32[2,1024]{1,0:T(2,128)}) custom-call(s32[6]{0:T(128)} %copy-done.76, bf16[1024,1280]{1,0:T(8,128)(2,1)} %copy-done.8, bf16[512,256]{1,0:T(8,128)(2,1)} %get-tuple-element.140.d_mine, bf16[512,256]{1,0:T(8,128)(2,1)} %copy-done.97, ...), custom_call_target="tpu_custom_call" | custom-call | flops 1 | bytes 1 | tf_op jit(solution)/shard_map/pallas_call | solution.py:743
  330.4 3.0 collective-permute-done.50
  345.2 15.6 %shard_map.289 = (bf16[512,1024]{1,0:T(8,128)(2,1)S(1)}, bf16[512,1024]{1,0:T(8,128)(2,1)S(1)}, bf16[512,1024]{1,0:T(8,128)(2,1)S(1)}, bf16[512,1024]{1,0:T(8,12...) custom-call(s32[6]{0:T(128)S(1)} %copy-done.77, ...), custom_call_target="tpu_custom_call" | custom-call | flops 1 | bytes 1 | tf_op jit(solution)/shard_map/pallas_call | solution.py:866
  365.7 12.8 %collective-permute-done.57 = bf16[256,1024]{1,0:T(8,128)(2,1)S(1)} collective-permute-done((bf16[256,1024]{1,0:T(8,128)(2,1)S(1)}, bf16[256,1024]{1,0:T(8,128)(2,1)S(1)}, u32[]{:S(2)}, u32[]{:S(2)}) %collective-permute-start.57) | collective-permute-done | bytes 524320 | tf_op jit(solution)/shard_map/ppermute | solution.py:41
  380.2 3.6 collective-permute-start.60
  383.8 2.7 collective-permute-start.56
  386.4 17.8 %collective-permute-done.54.refs_1_ = bf16[144,2048]{1,0:T(8,128)(2,1)S(1)} collective-permute-done((bf16[144,2048]{1,0:T(8,128)(2,1)S(1)}, bf16[144,2048]{1,0:T(8,128)(2,1)S(1)}, u32[]{:S(2)}, u32[]{:S(2)}) %collective-permute-start.54) | collective-permute-done | bytes 589856 | tf_op jit(solution)/shard_map/ppermute | solution.py:41
  404.2 19.0 %collective-permute-done.58.refs_12_ = bf16[512,1024]{1,0:T(8,128)(2,1)S(1)} collective-permute-done((bf16[512,1024]{1,0:T(8,128)(2,1)S(1)}, bf16[512,1024]{1,0:T(8,128)(2,1)S(1)}, u32[]{:S(2)}, u32[]{:S(2)}) %collective-permute-start.58) | collective-permute-done | bytes 1048608 | tf_op jit(solution)/shard_map/ppermute | solution.py:41
  424.5 6.1 %shard_map.290 = (bf16[8,2,128,256]{3,2,1,0:T(8,128)(2,1)}, f32[2,2048]{1,0:T(2,128)}) custom-call(s32[6]{0:T(128)} %copy-done.76, bf16[144,2048]{1,0:T(8,128)(2,1)} %copy-done.65, bf16[144,2048]{1,0:T(8,128)(2,1)} %copy-done.98, bf16[272,2048]{1,0:T(8,128)(2,1)} %copy-done.96, bf16[144,2048]{1,0:T(8,128)(2,1)} %copy-done.99, ...), custom_call_target="tpu_custom_call" | custom-call | flops 1 | bytes 1 | tf_op jit(solution)/shard_map/pallas_call | solution.py:908
  437.9 5.9 %all-to-all-start = ((bf16[8,2,128,256]{3,2,1,0:T(8,128)(2,1)}), bf16[8,2,128,256]{3,2,1,0:T(8,128)(2,1)S(1)}, u32[]{:S(2)}, u32[]{:S(2)}) async-start(bf16[8,2,128,256]{3,2,1,0:T(8,128)(2,1)} %get-tuple-element.163.refs_2_), calls=%async_computation | async-start | bytes 2097152 | tf_op jit(solution)/shard_map/all_to_all | solution.py:109
  444.4 6.6 %collective-permute-done.61 = bf16[256,1024]{1,0:T(8,128)(2,1)S(1)} collective-permute-done((bf16[256,1024]{1,0:T(8,128)(2,1)S(1)}, bf16[256,1024]{1,0:T(8,128)(2,1)S(1)}, u32[]{:S(2)}, u32[]{:S(2)}) %collective-permute-start.61) | collective-permute-done | bytes 524320 | tf_op jit(solution)/shard_map/ppermute | solution.py:145
  452.6 3.0 collective-permute-done.64
  461.5 7.3 %collective-permute-done.65 = bf16[144,1024]{1,0:T(8,128)(2,1)S(1)} collective-permute-done((bf16[144,1024]{1,0:T(8,128)(2,1)}, bf16[144,1024]{1,0:T(8,128)(2,1)S(1)}, u32[]{:S(2)}, u32[]{:S(2)}) %collective-permute-start.65) | collective-permute-done | bytes 294944 | tf_op jit(solution)/shard_map/ppermute | solution.py:150
  474.2 6.1 %collective-permute-start.66 = (bf16[2,1024,256]{2,1,0:T(8,128)(2,1)S(1)}, bf16[2,1024,256]{2,1,0:T(8,128)(2,1)}, u32[]{:S(2)}, u32[]{:S(2)}) collective-permute-start(bf16[2,1024,256]{2,1,0:T(8,128)(2,1)S(1)} %bitcast.72), channel_id=1, source_target_pairs={{4,8},{8,4},{5,9},{9,5},{6,10},{10,6},{7,11},{11,7},{20,24},{24,20... | collective-permute-start | bytes 3145736 | tf_op jit(solution)/shard_map/ppermute | solution.py:114
  482.5 9.6 %shard_map.294 = (f32[4,2048,128]{2,1,0:T(8,128)}, f32[4,2048,128]{2,1,0:T(8,128)}, f32[4,128,2048]{2,1,0:T(8,128)}) custom-call(s32[6]{0:T(128)S(1)} %copy-done.78, bf16[2,2048,512]{2,1,0:T(8,128)(2,1)S(1)} %copy-done.37, bf16[2,2048,512]{2,1,0:T(8,128)(2,1)} %collective-permute-done.70.gu_got, bf16[2,256,2048]{2,1,0:T(8,128)(2,1)} %get-tuple-element.168.down_mine, ...), custom_call_target="tpu_custom_call" | custom-call | flops 20000000000 | bytes 1 | tf_op jit(solution)/shard_map/pallas_call | solution.py:992
  492.2 8.9 %collective-permute-done.69.refs_3_ = bf16[2,144,1024]{2,1,0:T(8,128)(2,1)S(1)} collective-permute-done((bf16[2,144,1024]{2,1,0:T(8,128)(2,1)S(1)}, bf16[2,144,1024]{2,1,0:T(8,128)(2,1)S(1)}, u32[]{:S(2)}, u32[]{:S(2)}) %collective-permute-start.69) | collective-permute-done | bytes 589856 | tf_op jit(solution)/shard_map/ppermute | solution.py:41
  510.1 5.4 %shard_map.296 = (f32[2048,256]{1,0:T(8,128)}, f32[2048,256]{1,0:T(8,128)}, f32[2048,256]{1,0:T(8,128)}, f32[256,2048]{1,0:T(8,128)}, f32[16,1024]{1,0:T(8,128)S(1)}) custom-call(s32[6]{0:T(128)S(1)} %copy-done.78, bf16[2,144,1024]{2,1,0:T(8,128)(2,1)S(1)} %copy-done.19, bf16[2,144,1024]{2,1,0:T(8,128)(2,1)S(1)} %copy-done.46, ...), custom_call_target="tpu_custom_call" | custom-call | flops 1 | bytes 1 | tf_op jit(solution)/shard_map/pallas_call | solution.py:954
  (444 shorter events, 171.1 us)
Async XLA Ops:
  26.1 43.3 %collective-permute-start.6 = (bf16[1024,768]{1,0:T(8,128)(2,1)}, bf16[1024,768]{1,0:T(8,128)(2,1)S(1)}, u32[]{:S(2)}, u32[]{:S(2)}) collective-permute-start(bf16[1024,768]{1,0:T(8,128)(2,1)} %pad_maximum_fusion.1), channel_id=1, source_target_pairs={{0,68},{4,64},{64,4},{68,0},{1,69},{5,65},{65,5},{69,1},{2,70},{6,... | collective-permute-start | bytes 4718600 | tf_op jit(solution)/shard_map/ppermute | solution.py:49
  29.7 13.4 %collective-permute-start.2 = (bf16[2,512,256]{2,1,0:T(8,128)(2,1)S(1)}, bf16[2,512,256]{2,1,0:T(8,128)(2,1)S(1)}, u32[]{:S(2)}, u32[]{:S(2)}) collective-permute-start(bf16[2,512,256]{2,1,0:T(8,128)(2,1)S(1)} %pad_maximum_fusion.5.own), channel_id=1, source_target_pairs={{0,3},{1,0},{2,1},{3,2},{4,7},{5,4},{6,5},{7,6},{8,11},{9,8},{10,9... | collective-permute-start | bytes 1572872 | tf_op jit(solution)/shard_map/ppermute | solution.py:41
  32.2 16.9 %collective-permute-start.4 = (bf16[2,512,256]{2,1,0:T(8,128)(2,1)S(1)}, bf16[2,512,256]{2,1,0:T(8,128)(2,1)S(1)}, u32[]{:S(2)}, u32[]{:S(2)}) collective-permute-start(bf16[2,512,256]{2,1,0:T(8,128)(2,1)S(1)} %pad_maximum_fusion.5.own), channel_id=1, source_target_pairs={{0,1},{1,2},{2,3},{3,0},{4,5},{5,6},{6,7},{7,4},{8,9},{9,10},{10,1... | collective-permute-start | bytes 1572872 | tf_op jit(solution)/shard_map/ppermute | solution.py:41
  51.8 13.8 %collective-permute-start.8 = (bf16[512,256]{1,0:T(8,128)(2,1)}, bf16[512,256]{1,0:T(8,128)(2,1)}, u32[]{:S(2)}, u32[]{:S(2)}) collective-permute-start(bf16[512,256]{1,0:T(8,128)(2,1)} %get-tuple-element.196), channel_id=1, source_target_pairs={{0,8},{4,0},{8,12},{12,4},{1,9},{5,1},{9,13},{13,5},{2,10},{6,2},{... | collective-permute-start | bytes 786440 | tf_op jit(solution)/shard_map/ppermute | solution.py:104
  51.8 13.8 %collective-permute-start.7 = (bf16[512,256]{1,0:T(8,128)(2,1)}, bf16[512,256]{1,0:T(8,128)(2,1)}, u32[]{:S(2)}, u32[]{:S(2)}) collective-permute-start(bf16[512,256]{1,0:T(8,128)(2,1)} %get-tuple-element.195), channel_id=1, source_target_pairs={{0,0},{4,8},{8,4},{12,12},{1,1},{5,9},{9,5},{13,13},{2,2},{6,10},{... | collective-permute-start | bytes 786440 | tf_op jit(solution)/shard_map/ppermute | solution.py:104
  70.6 17.7 %collective-permute-start.11 = (bf16[1024,768]{1,0:T(8,128)(2,1)}, bf16[1024,768]{1,0:T(8,128)(2,1)}, u32[]{:S(2)}, u32[]{:S(2)}) collective-permute-start(bf16[1024,768]{1,0:T(8,128)(2,1)} %get-tuple-element.99.refs_3_.refs_12_), channel_id=1, source_target_pairs={{0,8},{8,0},{1,9},{9,1},{2,10},{10,2},{3,11},{11,3},{4,12},{12,4},... | collective-permute-start | bytes 4718600 | tf_op jit(solution)/shard_map/ppermute | solution.py:45
  74.2 14.1 %collective-permute-start.12 = (bf16[128,2048]{1,0:T(8,128)(2,1)S(1)}, bf16[128,2048]{1,0:T(8,128)(2,1)S(1)}, u32[]{:S(2)}, u32[]{:S(2)}) collective-permute-start(bf16[128,2048]{1,0:T(8,128)(2,1)S(1)} %constant_dynamic-slice_fusion.3), channel_id=1, source_target_pairs={{0,68},{4,64},{64,4},{68,0},{1,69},{5,65},{65,5},{69,1},{2,70},{6,... | collective-permute-start | bytes 1572872 | tf_op jit(solution)/shard_map/ppermute | solution.py:49
  76.5 30.0 %collective-permute-start.18 = (f32[2,256]{1,0:T(2,128)S(1)}, f32[2,256]{1,0:T(2,128)S(1)}, u32[]{:S(2)}, u32[]{:S(2)}) collective-permute-start(f32[2,256]{1,0:T(2,128)S(1)} %pad_maximum_fusion.10), channel_id=1, source_target_pairs={{0,68},{4,64},{64,4},{68,0},{1,69},{5,65},{65,5},{69,1},{2,70},{6,... | collective-permute-start | bytes 6152 | tf_op jit(solution)/shard_map/ppermute | solution.py:49
  77.0 33.9 %collective-permute-start.9 = (bf16[2,512,256]{2,1,0:T(8,128)(2,1)}, bf16[2,512,256]{2,1,0:T(8,128)(2,1)S(1)}, u32[]{:S(2)}, u32[]{:S(2)}) collective-permute-start(bf16[2,512,256]{2,1,0:T(8,128)(2,1)} %get-tuple-element.98.own), channel_id=1, source_target_pairs={{0,3},{1,0},{2,1},{3,2},{4,7},{5,4},{6,5},{7,6},{8,11},{9,8},{10,9... | collective-permute-start | bytes 1572872 | tf_op jit(solution)/shard_map/ppermute | solution.py:41
  79.5 31.4 %collective-permute-start.10 = (bf16[2,512,256]{2,1,0:T(8,128)(2,1)}, bf16[2,512,256]{2,1,0:T(8,128)(2,1)S(1)}, u32[]{:S(2)}, u32[]{:S(2)}) collective-permute-start(bf16[2,512,256]{2,1,0:T(8,128)(2,1)} %get-tuple-element.98.own), channel_id=1, source_target_pairs={{0,1},{1,2},{2,3},{3,0},{4,5},{5,6},{6,7},{7,4},{8,9},{9,10},{10,1... | collective-permute-start | bytes 1572872 | tf_op jit(solution)/shard_map/ppermute | solution.py:41
  118.1 13.1 %collective-permute-start.19 = (bf16[512,1280]{1,0:T(8,128)(2,1)}, bf16[512,1280]{1,0:T(8,128)(2,1)}, u32[]{:S(2)}, u32[]{:S(2)}) collective-permute-start(bf16[512,1280]{1,0:T(8,128)(2,1)} %get-tuple-element.106), channel_id=1, source_target_pairs={{0,8},{8,0},{1,9},{9,1},{2,10},{10,2},{3,11},{11,3},{4,12},{12,4},... | collective-permute-start | bytes 3932168 | tf_op jit(solution)/shard_map/ppermute | solution.py:45
  128.1 71.3 %collective-permute-start.30 = (bf16[2,2048,256]{2,1,0:T(8,128)(2,1)}, bf16[2,2048,256]{2,1,0:T(8,128)(2,1)}, u32[]{:S(2)}, u32[]{:S(2)}) collective-permute-start(bf16[2,2048,256]{2,1,0:T(8,128)(2,1)} %pad_maximum_fusion), channel_id=1, source_target_pairs={{0,68},{4,64},{64,4},{68,0},{1,69},{5,65},{65,5},{69,1},{2,70},{6,... | collective-permute-start | bytes 6291464 | tf_op jit(solution)/shard_map/ppermute | solution.py:49
  156.4 14.9 %collective-permute-start.23 = (bf16[128,2048]{1,0:T(8,128)(2,1)S(1)}, bf16[128,2048]{1,0:T(8,128)(2,1)S(1)}, u32[]{:S(2)}, u32[]{:S(2)}) collective-permute-start(bf16[128,2048]{1,0:T(8,128)(2,1)S(1)} %get-tuple-element.112), channel_id=1, source_target_pairs={{0,1},{1,2},{2,3},{3,0},{4,5},{5,6},{6,7},{7,4},{8,9},{9,10},{10,1... | collective-permute-start | bytes 1572872 | tf_op jit(solution)/shard_map/ppermute | solution.py:41
  156.4 23.3 %collective-permute-start.24 = (bf16[128,2048]{1,0:T(8,128)(2,1)S(1)}, bf16[128,2048]{1,0:T(8,128)(2,1)S(1)}, u32[]{:S(2)}, u32[]{:S(2)}) collective-permute-start(bf16[128,2048]{1,0:T(8,128)(2,1)S(1)} %get-tuple-element.113), channel_id=1, source_target_pairs={{0,2},{1,3},{2,0},{3,1},{4,6},{5,7},{6,4},{7,5},{8,10},{9,11},{10,... | collective-permute-start | bytes 1572872 | tf_op jit(solution)/shard_map/ppermute | solution.py:41
  157.7 24.1 %collective-permute-start.25 = (bf16[128,2048]{1,0:T(8,128)(2,1)S(1)}, bf16[128,2048]{1,0:T(8,128)(2,1)S(1)}, u32[]{:S(2)}, u32[]{:S(2)}) collective-permute-start(bf16[128,2048]{1,0:T(8,128)(2,1)S(1)} %get-tuple-element.114), channel_id=1, source_target_pairs={{0,3},{1,0},{2,1},{3,2},{4,7},{5,4},{6,5},{7,6},{8,11},{9,8},{10,9... | collective-permute-start | bytes 1572872 | tf_op jit(solution)/shard_map/ppermute | solution.py:41
  159.3 40.1 %collective-permute-start.31 = (bf16[2,128,2048]{2,1,0:T(8,128)(2,1)S(1)}, bf16[2,128,2048]{2,1,0:T(8,128)(2,1)S(1)}, u32[]{:S(2)}, u32[]{:S(2)}) collective-permute-start(bf16[2,128,2048]{2,1,0:T(8,128)(2,1)S(1)} %constant_dynamic-slice_fusion), channel_id=1, source_target_pairs={{0,68},{4,64},{64,4},{68,0},{1,69},{5,65},{65,5},{69,1},{2,70},{6,... | collective-permute-start | bytes 3145736 | tf_op jit(solution)/shard_map/ppermute | solution.py:49
  184.6 14.8 %collective-permute-start.26 = (bf16[128,2048]{1,0:T(8,128)(2,1)S(1)}, bf16[128,2048]{1,0:T(8,128)(2,1)S(1)}, u32[]{:S(2)}, u32[]{:S(2)}) collective-permute-start(bf16[128,2048]{1,0:T(8,128)(2,1)S(1)} %get-tuple-element.116.own_rows), channel_id=1, source_target_pairs={{0,3},{1,0},{2,1},{3,2},{4,7},{5,4},{6,5},{7,6},{8,11},{9,8},{10,9... | collective-permute-start | bytes 1572872 | tf_op jit(solution)/shard_map/ppermute | solution.py:41
  188.0 13.7 %collective-permute-start.28 = (bf16[128,2048]{1,0:T(8,128)(2,1)S(1)}, bf16[128,2048]{1,0:T(8,128)(2,1)S(1)}, u32[]{:S(2)}, u32[]{:S(2)}) collective-permute-start(bf16[128,2048]{1,0:T(8,128)(2,1)S(1)} %get-tuple-element.116.own_rows), channel_id=1, source_target_pairs={{0,1},{1,2},{2,3},{3,0},{4,5},{5,6},{6,7},{7,4},{8,9},{9,10},{10,1... | collective-permute-start | bytes 1572872 | tf_op jit(solution)/shard_map/ppermute | solution.py:41
  202.5 18.3 %collective-permute-start.33 = (bf16[2,2048,256]{2,1,0:T(8,128)(2,1)}, bf16[2,2048,256]{2,1,0:T(8,128)(2,1)}, u32[]{:S(2)}, u32[]{:S(2)}) collective-permute-start(bf16[2,2048,256]{2,1,0:T(8,128)(2,1)} %get-tuple-element.121.near), channel_id=1, source_target_pairs={{0,8},{8,0},{1,9},{9,1},{2,10},{10,2},{3,11},{11,3},{4,12},{12,4},... | collective-permute-start | bytes 6291464 | tf_op jit(solution)/shard_map/ppermute | solution.py:45
  205.8 43.0 %collective-permute-start.39 = (bf16[512,2048]{1,0:T(8,128)(2,1)}, bf16[512,2048]{1,0:T(8,128)(2,1)S(1)}, u32[]{:S(2)}, u32[]{:S(2)}) collective-permute-start(bf16[512,2048]{1,0:T(8,128)(2,1)} %get-tuple-element.117.cot), channel_id=1, source_target_pairs={{0,8},{8,0},{1,9},{9,1},{2,10},{10,2},{3,11},{11,3},{4,12},{12,4},... | collective-permute-start | bytes 6291464 | tf_op jit(solution)/shard_map/ppermute | solution.py:45
  206.8 14.0 %collective-permute-start.27 = (bf16[64,2048]{1,0:T(8,128)(2,1)S(1)}, bf16[64,2048]{1,0:T(8,128)(2,1)S(1)}, u32[]{:S(2)}, u32[]{:S(2)}) collective-permute-start(bf16[64,2048]{1,0:T(8,128)(2,1)S(1)} %slice.170), channel_id=1, source_target_pairs={{0,3},{1,0},{2,1},{3,2},{4,7},{5,4},{6,5},{7,6},{8,11},{9,8},{10,9... | collective-permute-start | bytes 786440 | tf_op jit(solution)/shard_map/ppermute | solution.py:41
  207.7 13.1 %collective-permute-start.29 = (bf16[64,2048]{1,0:T(8,128)(2,1)S(1)}, bf16[64,2048]{1,0:T(8,128)(2,1)S(1)}, u32[]{:S(2)}, u32[]{:S(2)}) collective-permute-start(bf16[64,2048]{1,0:T(8,128)(2,1)S(1)} %slice.171), channel_id=1, source_target_pairs={{0,1},{1,2},{2,3},{3,0},{4,5},{5,6},{6,7},{7,4},{8,9},{9,10},{10,1... | collective-permute-start | bytes 786440 | tf_op jit(solution)/shard_map/ppermute | solution.py:41
  239.1 14.8 %collective-permute-start.38 = (bf16[512,2048]{1,0:T(8,128)(2,1)S(1)}, bf16[512,2048]{1,0:T(8,128)(2,1)S(1)}, u32[]{:S(2)}, u32[]{:S(2)}) collective-permute-start(bf16[512,2048]{1,0:T(8,128)(2,1)S(1)} %get-tuple-element.134), channel_id=1, source_target_pairs={{0,8},{8,0},{1,9},{9,1},{2,10},{10,2},{3,11},{11,3},{4,12},{12,4},... | collective-permute-start | bytes 6291464 | tf_op jit(solution)/shard_map/ppermute | solution.py:45
  239.2 20.8 %collective-permute-start.34 = (bf16[128,2048]{1,0:T(8,128)(2,1)}, bf16[128,2048]{1,0:T(8,128)(2,1)S(1)}, u32[]{:S(2)}, u32[]{:S(2)}) collective-permute-start(bf16[128,2048]{1,0:T(8,128)(2,1)} %get-tuple-element.129), channel_id=1, source_target_pairs={{0,1},{1,2},{2,3},{3,0},{4,5},{5,6},{6,7},{7,4},{8,9},{9,10},{10,1... | collective-permute-start | bytes 1572872 | tf_op jit(solution)/shard_map/ppermute | solution.py:41
  239.2 25.1 %collective-permute-start.35 = (bf16[128,2048]{1,0:T(8,128)(2,1)}, bf16[128,2048]{1,0:T(8,128)(2,1)S(1)}, u32[]{:S(2)}, u32[]{:S(2)}) collective-permute-start(bf16[128,2048]{1,0:T(8,128)(2,1)} %get-tuple-element.130), channel_id=1, source_target_pairs={{0,2},{1,3},{2,0},{3,1},{4,6},{5,7},{6,4},{7,5},{8,10},{9,11},{10,... | collective-permute-start | bytes 1572872 | tf_op jit(solution)/shard_map/ppermute | solution.py:41
  247.9 17.6 %collective-permute-start.36 = (bf16[128,2048]{1,0:T(8,128)(2,1)S(1)}, bf16[128,2048]{1,0:T(8,128)(2,1)S(1)}, u32[]{:S(2)}, u32[]{:S(2)}) collective-permute-start(bf16[128,2048]{1,0:T(8,128)(2,1)S(1)} %get-tuple-element.131), channel_id=1, source_target_pairs={{0,3},{1,0},{2,1},{3,2},{4,7},{5,4},{6,5},{7,6},{8,11},{9,8},{10,9... | collective-permute-start | bytes 1572872 | tf_op jit(solution)/shard_map/ppermute | solution.py:41
  270.8 159.7 %all-reduce.4.cloned.1.call-start = ((), (), s32[]{:S(2)}) async-start(), calls=%async_computation.1 | async-start | bytes 12582912 | tf_op jit(solution)/shard_map/psum | solution.py:1131
  271.9 14.2 %collective-permute-start.40 = (bf16[128,2048]{1,0:T(8,128)(2,1)S(1)}, bf16[128,2048]{1,0:T(8,128)(2,1)S(1)}, u32[]{:S(2)}, u32[]{:S(2)}) collective-permute-start(bf16[128,2048]{1,0:T(8,128)(2,1)S(1)} %copy-done.100), channel_id=1, source_target_pairs={{0,3},{1,0},{2,1},{3,2},{4,7},{5,4},{6,5},{7,6},{8,11},{9,8},{10,9... | collective-permute-start | bytes 1572872 | tf_op jit(solution)/shard_map/ppermute | solution.py:41
  275.3 14.3 %collective-permute-start.42 = (bf16[128,2048]{1,0:T(8,128)(2,1)S(1)}, bf16[128,2048]{1,0:T(8,128)(2,1)S(1)}, u32[]{:S(2)}, u32[]{:S(2)}) collective-permute-start(bf16[128,2048]{1,0:T(8,128)(2,1)S(1)} %copy-done.100), channel_id=1, source_target_pairs={{0,1},{1,2},{2,3},{3,0},{4,5},{5,6},{6,7},{7,4},{8,9},{9,10},{10,1... | collective-permute-start | bytes 1572872 | tf_op jit(solution)/shard_map/ppermute | solution.py:41
  308.4 14.6 %collective-permute-start.46 = (bf16[128,2048]{1,0:T(8,128)(2,1)}, bf16[128,2048]{1,0:T(8,128)(2,1)S(1)}, u32[]{:S(2)}, u32[]{:S(2)}) collective-permute-start(bf16[128,2048]{1,0:T(8,128)(2,1)} %get-tuple-element.146), channel_id=1, source_target_pairs={{0,1},{1,2},{2,3},{3,0},{4,5},{5,6},{6,7},{7,4},{8,9},{9,10},{10,1... | collective-permute-start | bytes 1572872 | tf_op jit(solution)/shard_map/ppermute | solution.py:41
  308.4 15.4 %collective-permute-start.47 = (bf16[128,2048]{1,0:T(8,128)(2,1)}, bf16[128,2048]{1,0:T(8,128)(2,1)S(1)}, u32[]{:S(2)}, u32[]{:S(2)}) collective-permute-start(bf16[128,2048]{1,0:T(8,128)(2,1)} %get-tuple-element.147), channel_id=1, source_target_pairs={{0,3},{1,0},{2,1},{3,2},{4,7},{5,4},{6,5},{7,6},{8,11},{9,8},{10,9... | collective-permute-start | bytes 1572872 | tf_op jit(solution)/shard_map/ppermute | solution.py:41
  311.1 32.1 %collective-permute-start.21 = (bf16[512,2048]{1,0:T(8,128)(2,1)S(1)}, bf16[512,2048]{1,0:T(8,128)(2,1)}, u32[]{:S(2)}, u32[]{:S(2)}) collective-permute-start(bf16[512,2048]{1,0:T(8,128)(2,1)S(1)} %copy-done.4), channel_id=1, source_target_pairs={{0,8},{8,0},{1,9},{9,1},{2,10},{10,2},{3,11},{11,3},{4,12},{12,4},... | collective-permute-start | bytes 6291464 | tf_op jit(solution)/shard_map/ppermute | solution.py:45
  312.0 33.1 %collective-permute-start.45 = (bf16[512,2048]{1,0:T(8,128)(2,1)}, bf16[512,2048]{1,0:T(8,128)(2,1)}, u32[]{:S(2)}, u32[]{:S(2)}) collective-permute-start(bf16[512,2048]{1,0:T(8,128)(2,1)} %get-tuple-element.138.refs_2_), channel_id=1, source_target_pairs={{0,8},{8,0},{1,9},{9,1},{2,10},{10,2},{3,11},{11,3},{4,12},{12,4},... | collective-permute-start | bytes 6291464 | tf_op jit(solution)/shard_map/ppermute | solution.py:45
  360.8 17.6 %collective-permute-start.57 = (bf16[256,1024]{1,0:T(8,128)(2,1)S(1)}, bf16[256,1024]{1,0:T(8,128)(2,1)S(1)}, u32[]{:S(2)}, u32[]{:S(2)}) collective-permute-start(bf16[256,1024]{1,0:T(8,128)(2,1)S(1)} %get-tuple-element.192), channel_id=1, source_target_pairs={{0,16},{16,32},{32,48},{48,0},{1,17},{17,33},{33,49},{49,1},{2,18}... | collective-permute-start | bytes 1572872 | tf_op jit(solution)/shard_map/ppermute | solution.py:41
  362.3 17.6 %collective-permute-start.59 = (bf16[256,1024]{1,0:T(8,128)(2,1)S(1)}, bf16[256,1024]{1,0:T(8,128)(2,1)S(1)}, u32[]{:S(2)}, u32[]{:S(2)}) collective-permute-start(bf16[256,1024]{1,0:T(8,128)(2,1)S(1)} %get-tuple-element.191), channel_id=1, source_target_pairs={{0,48},{16,0},{32,16},{48,32},{1,49},{17,1},{33,17},{49,33},{2,50}... | collective-permute-start | bytes 1572872 | tf_op jit(solution)/shard_map/ppermute | solution.py:41
  363.8 40.4 %collective-permute-start.55 = (bf16[272,2048]{1,0:T(8,128)(2,1)S(1)}, bf16[272,2048]{1,0:T(8,128)(2,1)S(1)}, u32[]{:S(2)}, u32[]{:S(2)}) collective-permute-start(bf16[272,2048]{1,0:T(8,128)(2,1)S(1)} %get-tuple-element.156), channel_id=1, source_target_pairs={{0,2},{1,3},{2,0},{3,1},{4,6},{5,7},{6,4},{7,5},{8,10},{9,11},{10,... | collective-permute-start | bytes 3342344 | tf_op jit(solution)/shard_map/ppermute | solution.py:41
  378.7 44.4 %collective-permute-start.58 = (bf16[512,1024]{1,0:T(8,128)(2,1)S(1)}, bf16[512,1024]{1,0:T(8,128)(2,1)S(1)}, u32[]{:S(2)}, u32[]{:S(2)}) collective-permute-start(bf16[512,1024]{1,0:T(8,128)(2,1)S(1)} %pad_maximum_fusion.2), channel_id=1, source_target_pairs={{0,16},{16,32},{32,48},{48,0},{1,17},{17,33},{33,49},{49,1},{2,18}... | collective-permute-start | bytes 3145736 | tf_op jit(solution)/shard_map/ppermute | solution.py:41
  380.2 43.0 %collective-permute-start.60 = (bf16[512,1024]{1,0:T(8,128)(2,1)S(1)}, bf16[512,1024]{1,0:T(8,128)(2,1)S(1)}, u32[]{:S(2)}, u32[]{:S(2)}) collective-permute-start(bf16[512,1024]{1,0:T(8,128)(2,1)S(1)} %pad_maximum_fusion.3), channel_id=1, source_target_pairs={{0,48},{16,0},{32,16},{48,32},{1,49},{17,1},{33,17},{49,33},{2,50}... | collective-permute-start | bytes 3145736 | tf_op jit(solution)/shard_map/ppermute | solution.py:41
  383.8 20.4 %collective-permute-start.54 = (bf16[144,2048]{1,0:T(8,128)(2,1)S(1)}, bf16[144,2048]{1,0:T(8,128)(2,1)S(1)}, u32[]{:S(2)}, u32[]{:S(2)}) collective-permute-start(bf16[144,2048]{1,0:T(8,128)(2,1)S(1)} %get-tuple-element.155), channel_id=1, source_target_pairs={{0,1},{1,2},{2,3},{3,0},{4,5},{5,6},{6,7},{7,4},{8,9},{9,10},{10,1... | collective-permute-start | bytes 1769480 | tf_op jit(solution)/shard_map/ppermute | solution.py:41
  383.8 20.4 %collective-permute-start.56 = (bf16[144,2048]{1,0:T(8,128)(2,1)S(1)}, bf16[144,2048]{1,0:T(8,128)(2,1)S(1)}, u32[]{:S(2)}, u32[]{:S(2)}) collective-permute-start(bf16[144,2048]{1,0:T(8,128)(2,1)S(1)} %get-tuple-element.157), channel_id=1, source_target_pairs={{0,3},{1,0},{2,1},{3,2},{4,7},{5,4},{6,5},{7,6},{8,11},{9,8},{10,9... | collective-permute-start | bytes 1769480 | tf_op jit(solution)/shard_map/ppermute | solution.py:41
  430.6 49.7 %collective-permute-start.70 = (bf16[2,2048,512]{2,1,0:T(8,128)(2,1)}, bf16[2,2048,512]{2,1,0:T(8,128)(2,1)}, u32[]{:S(2)}, u32[]{:S(2)}) collective-permute-start(bf16[2,2048,512]{2,1,0:T(8,128)(2,1)} %get-tuple-element.167.gu_mine), channel_id=1, source_target_pairs={{0,8},{12,4},{1,9},{13,5},{2,10},{14,6},{3,11},{15,7},{16,24},{28,... | collective-permute-start | bytes 12582920 | tf_op jit(solution)/shard_map/ppermute | solution.py:155
  434.6 16.3 %collective-permute-start.61 = (bf16[256,1024]{1,0:T(8,128)(2,1)S(1)}, bf16[256,1024]{1,0:T(8,128)(2,1)S(1)}, u32[]{:S(2)}, u32[]{:S(2)}) collective-permute-start(bf16[256,1024]{1,0:T(8,128)(2,1)S(1)} %get-tuple-element.189), channel_id=1, source_target_pairs={{4,8},{8,4},{68,72},{72,68},{5,9},{9,5},{69,73},{73,69},{6,10},{10... | collective-permute-start | bytes 1572872 | tf_op jit(solution)/shard_map/ppermute | solution.py:145
  436.6 37.6 %collective-permute-start.71 = (bf16[2,256,2048]{2,1,0:T(8,128)(2,1)}, bf16[2,256,2048]{2,1,0:T(8,128)(2,1)}, u32[]{:S(2)}, u32[]{:S(2)}) collective-permute-start(bf16[2,256,2048]{2,1,0:T(8,128)(2,1)} %get-tuple-element.168.down_mine), channel_id=1, source_target_pairs={{0,8},{12,4},{1,9},{13,5},{2,10},{14,6},{3,11},{15,7},{16,24},{28,... | collective-permute-start | bytes 6291464 | tf_op jit(solution)/shard_map/ppermute | solution.py:155
  437.9 20.9 %all-to-all-start = ((bf16[8,2,128,256]{3,2,1,0:T(8,128)(2,1)}), bf16[8,2,128,256]{3,2,1,0:T(8,128)(2,1)S(1)}, u32[]{:S(2)}, u32[]{:S(2)}) async-start(bf16[8,2,128,256]{3,2,1,0:T(8,128)(2,1)} %get-tuple-element.163.refs_2_), calls=%async_computation | async-start | bytes 2097152 | tf_op jit(solution)/shard_map/all_to_all | solution.py:109
  469.9 22.3 %collective-permute-start.67 = (bf16[2,144,1024]{2,1,0:T(8,128)(2,1)S(1)}, bf16[2,144,1024]{2,1,0:T(8,128)(2,1)S(1)}, u32[]{:S(2)}, u32[]{:S(2)}) collective-permute-start(bf16[2,144,1024]{2,1,0:T(8,128)(2,1)S(1)} %pad_maximum_fusion.4.refs_1_.refs_0_), channel_id=1, source_target_pairs={{0,48},{16,0},{32,16},{48,32},{1,49},{17,1},{33,17},{49,33},{2,50}... | collective-permute-start | bytes 1769480 | tf_op jit(solution)/shard_map/ppermute | solution.py:41
  471.9 20.3 %collective-permute-start.68 = (bf16[2,144,1024]{2,1,0:T(8,128)(2,1)S(1)}, bf16[2,144,1024]{2,1,0:T(8,128)(2,1)S(1)}, u32[]{:S(2)}, u32[]{:S(2)}) collective-permute-start(bf16[2,144,1024]{2,1,0:T(8,128)(2,1)S(1)} %pad_maximum_fusion.4.refs_1_.refs_0_), channel_id=1, source_target_pairs={{0,32},{16,48},{32,0},{48,16},{1,33},{17,49},{33,1},{49,17},{2,34}... | collective-permute-start | bytes 1769480 | tf_op jit(solution)/shard_map/ppermute | solution.py:41
  472.1 29.0 %collective-permute-start.69 = (bf16[2,144,1024]{2,1,0:T(8,128)(2,1)S(1)}, bf16[2,144,1024]{2,1,0:T(8,128)(2,1)S(1)}, u32[]{:S(2)}, u32[]{:S(2)}) collective-permute-start(bf16[2,144,1024]{2,1,0:T(8,128)(2,1)S(1)} %pad_maximum_fusion.4.refs_1_.refs_0_), channel_id=1, source_target_pairs={{0,16},{16,32},{32,48},{48,0},{1,17},{17,33},{33,49},{49,1},{2,18}... | collective-permute-start | bytes 1769480 | tf_op jit(solution)/shard_map/ppermute | solution.py:41
  474.2 28.9 %collective-permute-start.66 = (bf16[2,1024,256]{2,1,0:T(8,128)(2,1)S(1)}, bf16[2,1024,256]{2,1,0:T(8,128)(2,1)}, u32[]{:S(2)}, u32[]{:S(2)}) collective-permute-start(bf16[2,1024,256]{2,1,0:T(8,128)(2,1)S(1)} %bitcast.72), channel_id=1, source_target_pairs={{4,8},{8,4},{5,9},{9,5},{6,10},{10,6},{7,11},{11,7},{20,24},{24,20... | collective-permute-start | bytes 3145736 | tf_op jit(solution)/shard_map/ppermute | solution.py:114
  (142 other events, 1199.1 us)
Sparse Core Ops, SparseCore 0:
  276.3 143.6 all-reduce.3

commit v2 on v1

--- a/solution.py
+++ b/solution.py
@@ -335,6 +335,7 @@
         ],
         [shape(rows, 768, dtype=F32), shape(rows, 768, dtype=F32), shape(8, rows, dtype=F32)],
         scratch=[pltpu.VMEM((rows, 8), F32)],
+        vmem=BIG,
     )(place, rows_in, *own, near, far, awaited)
 
 
@@ -376,6 +377,7 @@
         ],
         [spec(1280), spec(1280)],
         [shape(rows, 1280), shape(rows, 1280)],
+        vmem=BIG,
     )(place, raw_send, raw_keep, inv_rows, gains, table, *awaited)
 
 
@@ -812,6 +814,7 @@
             whole(2, 256),
         ],
         [shape(512, 768), shape(512, 768), shape(2, 256, dtype=F32)],
+        vmem=BIG,
     )(place, d_query, d_key, d_value, qkv, qkv, sums, inv_rows, gains)
 
 

time: 535 us -> 538 us (level)
  Pallas kernels: 114 us -> 125 us
  local copies, waits for them, and re-layouts: 66.9 us -> 59.2 us
    unnamed x234 -> x224, local copies, waits for them, and re-layouts: 49.6 us -> 40.6 us
  transfers between devices with their start and end apart: 78 -> 78, of which waited for: 40 -> 41; matrix products, arithmetic and copies ran while one was open for 7% -> 8% of each run, Pallas kernels for 19% -> 21%
where the time goes in v2:
time: 538 us; the launch traced here: 527 us
  waiting for transfers between devices  187 us (35%)
  Pallas kernels  125 us (23%)
  starting transfers between devices  110 us (20%)
  local copies, waits for them, and re-layouts  59.2 us (11%)
  between operations  20.9 us (4%)
  other arithmetic  14.9 us (3%)
  matrix products  10.3 us (2%)
    ppermute x40, waiting for transfers between devices, along(): lax.ppermute(value, axis, [(i, (i + shift) % size) for i in range(size)])  131 us
    ppermute x40, starting transfers between devices, along(): lax.ppermute(value, axis, [(i, (i + shift) % size) for i in range(size)])  51.9 us
    unnamed x224, local copies, waits for them, and re-layouts  40.6 us
    ppermute x5, waiting for transfers between devices, other_half_chip(): return lax.ppermute(value, ('zl', 'zh'), [(i, 3 - i) for i in range(4)])  20 us
    pallas_call x1, Pallas kernels, expert_layer(): call(expert_kernel, (4,), [whole(n, width) for n in (128, 128, 64, 64, 12...  18 us
    pallas_call x1, Pallas kernels, back(): call(back_kernel, (width // step,), [block(), block(), block(), block()]...  15.5 us
    ppermute x20, starting transfers between devices, other_core(): return lax.ppermute(value, 'c', [(0, 1), (1, 0)])  15.4 us
    ppermute x4, starting transfers between devices, deal_in(): got.append(lax.ppermute(part, ('c', 'zh'), pairs))  11.8 us
  transfers between devices with their start and end apart: 78, of which 41 were waited for; matrix products, arithmetic and copies ran while one was open for 8% of the time, Pallas kernels for 21%

profile of v2, /device:TPU:1, one launch (start us, length us, event | category | flops | bytes accessed | tf_op | source)
XLA Modules:
  0.0 527.1 jit_solution(14552450781649793753)
XLA Ops:
  8.5 6.9 %collective-permute-start = (bf16[512,256]{1,0:T(8,128)(2,1)S(1)}, bf16[512,256]{1,0:T(8,128)(2,1)S(1)}, u32[]{:S(2)}, u32[]{:S(2)}) collective-permute-start(bf16[512,256]{1,0:T(8,128)(2,1)S(1)} %get-tuple-element.199), channel_id=1, source_target_pairs={{0,0},{4,8},{8,4},{12,12},{1,1},{5,9},{9,5},{13,13},{2,2},{6,10},{... | collective-permute-start | bytes 786440 | tf_op jit(solution)/shard_map/ppermute | solution.py:104
  15.5 3.9 collective-permute-done
  26.1 3.6 collective-permute-start.6
  32.2 10.9 %collective-permute-done.2.after = bf16[2,512,256]{2,1,0:T(8,128)(2,1)S(1)} collective-permute-done((bf16[2,512,256]{2,1,0:T(8,128)(2,1)S(1)}, bf16[2,512,256]{2,1,0:T(8,128)(2,1)S(1)}, u32[]{:S(2)}, u32[]{:S(2)}) %collective-permute-start.2) | collective-permute-done | bytes 524320 | tf_op jit(solution)/shard_map/ppermute | solution.py:41
  45.7 3.4 collective-permute-start.3
  51.8 4.9 collective-permute-start.7
  60.4 3.6 shard_map.264
  80.0 9.4 %collective-permute-done.12.refs_5_.refs_0_ = bf16[128,2048]{1,0:T(8,128)(2,1)S(1)} collective-permute-done((bf16[128,2048]{1,0:T(8,128)(2,1)S(1)}, bf16[128,2048]{1,0:T(8,128)(2,1)S(1)}, u32[]{:S(2)}, u32[]{:S(2)}) %collective-permute-start.12) | collective-permute-done | bytes 524320 | tf_op jit(solution)/shard_map/ppermute | solution.py:49
  90.3 10.7 %shard_map.266 = (f32[512,768]{1,0:T(8,128)}, f32[512,768]{1,0:T(8,128)}, f32[8,512]{1,0:T(8,128)}) custom-call(s32[6]{0:T(128)} %copy-done.67, bf16[512,2048]{1,0:T(8,128)(2,1)} %copy-done.2, bf16[2048,256]{1,0:T(8,128)(2,1)} %refs_9_.1, bf16[2048,256]{1,0:T(8,128)(2,1)} %refs_10_.1, bf16[2048,256]{1,0:T(8,128)(2,1)} %refs_11_.1, ...), custom_call_target="tpu_custom_call" | custom-call | flops 1 | bytes 1 | tf_op jit(solution)/shard_map/pallas_call | solution.py:319
  110.7 5.5 %shard_map.270 = (bf16[512,1280]{1,0:T(8,128)(2,1)}, bf16[512,1280]{1,0:T(8,128)(2,1)}) custom-call(s32[6]{0:T(128)} %copy-done.67, f32[512,768]{1,0:T(8,128)} %get-tuple-element.103.raw_send, f32[512,768]{1,0:T(8,128)} %get-tuple-element.104.raw_keep, f32[2,512]{1,0:T(2,128)} %add_rsqrt_fusion.refs_2_.inv_rows.refs_1_, f32[4,256]{1,0:T(4,128)} %pad_maximum_fusion.9.gains, ...), custom_call_target="tpu_custom_call" | custom-call | flops 1 | bytes 1 | tf_op jit(solution)/shard_map/pallas_call | solution.py:366
  126.9 6.3 %shard_map.271 = (bf16[1024,1280]{1,0:T(8,128)(2,1)S(1)}, bf16[512,256]{1,0:T(8,128)(2,1)S(1)}, bf16[512,256]{1,0:T(8,128)(2,1)S(1)}, f32[2,1024]{1,0:T(2,128)S(1)}) custom-call(s32[6]{0:T(128)S(1)} %copy-done.68, bf16[512,1280]{1,0:T(8,128)(2,1)S(1)} %copy-done.50, bf16[512,1280]{1,0:T(8,128)(2,1)} %collective-permute-done.19.rest, ...), custom_call_target="tpu_custom_call" | custom-call | flops 1 | bytes 1 | tf_op jit(solution)/shard_map/pallas_call | solution.py:407
  140.7 6.6 %collective-permute-done.16.far_low = bf16[1,512,256]{2,1,0:T(8,128)(2,1)S(1)} collective-permute-done((bf16[1,512,256]{2,1,0:T(8,128)(2,1)}, bf16[1,512,256]{2,1,0:T(8,128)(2,1)S(1)}, u32[]{:S(2)}, u32[]{:S(2)}) %collective-permute-start.16) | collective-permute-done | bytes 262176 | tf_op jit(solution)/shard_map/ppermute | solution.py:41
  149.5 4.0 shard_map.275
  159.0 10.0 %collective-permute-done.23.b = bf16[128,2048]{1,0:T(8,128)(2,1)S(1)} collective-permute-done((bf16[128,2048]{1,0:T(8,128)(2,1)S(1)}, bf16[128,2048]{1,0:T(8,128)(2,1)S(1)}, u32[]{:S(2)}, u32[]{:S(2)}) %collective-permute-start.23) | collective-permute-done | bytes 524320 | tf_op jit(solution)/shard_map/ppermute | solution.py:41
  169.0 8.8 %collective-permute-done.24.c = bf16[128,2048]{1,0:T(8,128)(2,1)S(1)} collective-permute-done((bf16[128,2048]{1,0:T(8,128)(2,1)S(1)}, bf16[128,2048]{1,0:T(8,128)(2,1)S(1)}, u32[]{:S(2)}, u32[]{:S(2)}) %collective-permute-start.24) | collective-permute-done | bytes 524320 | tf_op jit(solution)/shard_map/ppermute | solution.py:41
  182.6 3.4 collective-permute-start.26
  186.0 10.3 %collective-permute-done.31.refs_1_ = bf16[2,128,2048]{2,1,0:T(8,128)(2,1)S(1)} collective-permute-done((bf16[2,128,2048]{2,1,0:T(8,128)(2,1)S(1)}, bf16[2,128,2048]{2,1,0:T(8,128)(2,1)S(1)}, u32[]{:S(2)}, u32[]{:S(2)}) %collective-permute-start.31) | collective-permute-done | bytes 1048608 | tf_op jit(solution)/shard_map/ppermute | solution.py:49
  212.7 4.8 shard_map.279.back
  218.8 18.0 %shard_map.280 = (bf16[2,512,768]{2,1,0:T(8,128)(2,1)S(1)}, bf16[2,512,768]{2,1,0:T(8,128)(2,1)S(1)}, bf16[512,2048]{1,0:T(8,128)(2,1)S(1)}, bf16[128,2048]{1,0:...) custom-call(s32[6]{0:T(128)S(1)} %copy-done.68, ...), custom_call_target="tpu_custom_call" | custom-call | flops 1 | bytes 1 | tf_op jit(solution)/shard_map/pallas_call | solution.py:620
  239.6 6.3 %shard_map.281 = (bf16[128,2048]{1,0:T(8,128)(2,1)S(1)}, bf16[128,2048]{1,0:T(8,128)(2,1)S(1)}, bf16[128,2048]{1,0:T(8,128)(2,1)S(1)}, bf16[128,2048]{1,0:T(8,128)(2,1)S(1)}) custom-call(s32[6]{0:T(128)S(1)} %copy-done.68, bf16[2,512,768]{2,1,0:T(8,128)(2,1)S(1)} %get-tuple-element.122.send, bf16[2,512,768]{2,1,0:T(8,128)(2,1)S(1)} %get-tuple-element.123.keep.awaited, ...), custom_call_target="tpu_custom_call" | custom-call | flops 5000000000 | bytes 1 | tf_op jit(solution)/shard_map/pallas_call | solution.py:671
  248.3 3.7 fusion.7.ready_b
  252.1 6.1 %convert_bitcast_fusion.ready_a = bf16[2,2048,512]{2,1,0:T(8,128)(2,1)} fusion(bf16[512,2048]{1,0:T(8,128)(2,1)S(1)} %collective-permute-done.38, bf16[512,2048]{1,0:T(8,128)(2,1)S(1)} %get-tuple-element.134, bf16[2,1024,768]{2,1,0:T(8,128)(2,1)S(1)} %constant_dynamic-update-slice_fusion), kind=kOutput, calls=%fused_computation.8 | convolution fusion | flops 4305453056 | bytes 10485760 | tf_op jit(solution)/shard_map/td,etf->edf/dot_general | solution.py:1118
  258.2 4.3 collective-permute-done.35.c
  264.6 4.6 shard_map.282
  270.2 3.3 collective-permute-start.40
  273.5 10.8 %collective-permute-done.40.after = bf16[128,2048]{1,0:T(8,128)(2,1)S(1)} collective-permute-done((bf16[128,2048]{1,0:T(8,128)(2,1)S(1)}, bf16[128,2048]{1,0:T(8,128)(2,1)S(1)}, u32[]{:S(2)}, u32[]{:S(2)}) %collective-permute-start.40) | collective-permute-done | bytes 524320 | tf_op jit(solution)/shard_map/ppermute | solution.py:41
  284.3 3.5 collective-permute-start.41
  288.1 3.9 collective-permute-done.41.far_low
  292.1 3.5 collective-permute-done.43.far_high
  296.3 5.7 %shard_map.283 = (bf16[512,256]{1,0:T(8,128)(2,1)}, bf16[512,256]{1,0:T(8,128)(2,1)}, bf16[512,2048]{1,0:T(8,128)(2,1)}) custom-call(s32[6]{0:T(128)} %copy-done.67, bf16[128,2048]{1,0:T(8,128)(2,1)} %get-tuple-element.135.own_rows, bf16[128,2048]{1,0:T(8,128)(2,1)} %copy-done.85, bf16[64,2048]{1,0:T(8,128)(2,1)} %copy-done.95, bf16[64,2048]{1,0:T(8,128)(2,1)} %copy-done.96, ...), custom_call_target="tpu_custom_call" | custom-call | flops 1 | bytes 1 | tf_op jit(solution)/shard_map/pallas_call | solution.py:468
  310.2 10.5 %shard_map.285 = (f32[1024,256]{1,0:T(8,128)}, f32[1024,256]{1,0:T(8,128)}, bf16[1024,256]{1,0:T(8,128)(2,1)}, f32[2,1024]{1,0:T(2,128)}) custom-call(s32[6]{0:T(128)} %copy-done.67, bf16[1024,1280]{1,0:T(8,128)(2,1)} %copy-done.7, bf16[512,256]{1,0:T(8,128)(2,1)} %get-tuple-element.140.d_mine, bf16[512,256]{1,0:T(8,128)(2,1)} %copy-done.88, ...), custom_call_target="tpu_custom_call" | custom-call | flops 1 | bytes 1 | tf_op jit(solution)/shard_map/pallas_call | solution.py:745
  328.9 2.7 collective-permute-done.50
  332.4 6.2 %shard_map.288 = (bf16[512,768]{1,0:T(8,128)(2,1)}, bf16[512,768]{1,0:T(8,128)(2,1)}, f32[2,256]{1,0:T(2,128)}) custom-call(s32[6]{0:T(128)} %copy-done.67, f32[1024,256]{1,0:T(8,128)} %get-tuple-element.142.d_query, f32[1024,256]{1,0:T(8,128)} %get-tuple-element.143.d_key, bf16[1024,256]{1,0:T(8,128)(2,1)} %get-tuple-element.144.d_value, ...), custom_call_target="tpu_custom_call" | custom-call | flops 1 | bytes 1 | tf_op jit(solution)/shard_map/pallas_call | solution.py:798
  346.3 15.5 %shard_map.289 = (bf16[512,1024]{1,0:T(8,128)(2,1)S(1)}, bf16[512,1024]{1,0:T(8,128)(2,1)S(1)}, bf16[512,1024]{1,0:T(8,128)(2,1)S(1)}, bf16[512,1024]{1,0:T(8,12...) custom-call(s32[6]{0:T(128)S(1)} %copy-done.69, ...), custom_call_target="tpu_custom_call" | custom-call | flops 1 | bytes 1 | tf_op jit(solution)/shard_map/pallas_call | solution.py:869
  366.7 14.6 %collective-permute-done.57 = bf16[256,1024]{1,0:T(8,128)(2,1)S(1)} collective-permute-done((bf16[256,1024]{1,0:T(8,128)(2,1)S(1)}, bf16[256,1024]{1,0:T(8,128)(2,1)S(1)}, u32[]{:S(2)}, u32[]{:S(2)}) %collective-permute-start.57) | collective-permute-done | bytes 524320 | tf_op jit(solution)/shard_map/ppermute | solution.py:41
  383.0 3.6 collective-permute-start.60
  389.3 15.2 %collective-permute-done.54.refs_1_ = bf16[144,2048]{1,0:T(8,128)(2,1)S(1)} collective-permute-done((bf16[144,2048]{1,0:T(8,128)(2,1)S(1)}, bf16[144,2048]{1,0:T(8,128)(2,1)S(1)}, u32[]{:S(2)}, u32[]{:S(2)}) %collective-permute-start.54) | collective-permute-done | bytes 589856 | tf_op jit(solution)/shard_map/ppermute | solution.py:41
  404.5 19.8 %collective-permute-done.58.refs_12_ = bf16[512,1024]{1,0:T(8,128)(2,1)S(1)} collective-permute-done((bf16[512,1024]{1,0:T(8,128)(2,1)S(1)}, bf16[512,1024]{1,0:T(8,128)(2,1)S(1)}, u32[]{:S(2)}, u32[]{:S(2)}) %collective-permute-start.58) | collective-permute-done | bytes 1048608 | tf_op jit(solution)/shard_map/ppermute | solution.py:41
  425.6 6.1 %shard_map.290 = (bf16[8,2,128,256]{3,2,1,0:T(8,128)(2,1)}, f32[2,2048]{1,0:T(2,128)}) custom-call(s32[6]{0:T(128)} %copy-done.67, bf16[144,2048]{1,0:T(8,128)(2,1)} %copy-done.58, bf16[144,2048]{1,0:T(8,128)(2,1)} %copy-done.89, bf16[272,2048]{1,0:T(8,128)(2,1)} %copy-done.87, bf16[144,2048]{1,0:T(8,128)(2,1)} %copy-done.90, ...), custom_call_target="tpu_custom_call" | custom-call | flops 1 | bytes 1 | tf_op jit(solution)/shard_map/pallas_call | solution.py:911
  434.3 2.9 collective-permute-start.62
  440.4 5.9 %all-to-all-start = ((bf16[8,2,128,256]{3,2,1,0:T(8,128)(2,1)}), bf16[8,2,128,256]{3,2,1,0:T(8,128)(2,1)S(1)}, u32[]{:S(2)}, u32[]{:S(2)}) async-start(bf16[8,2,128,256]{3,2,1,0:T(8,128)(2,1)} %get-tuple-element.163.refs_2_), calls=%async_computation | async-start | bytes 2097152 | tf_op jit(solution)/shard_map/all_to_all | solution.py:109
  446.6 6.8 %collective-permute-done.61 = bf16[256,1024]{1,0:T(8,128)(2,1)S(1)} collective-permute-done((bf16[256,1024]{1,0:T(8,128)(2,1)S(1)}, bf16[256,1024]{1,0:T(8,128)(2,1)S(1)}, u32[]{:S(2)}, u32[]{:S(2)}) %collective-permute-start.61) | collective-permute-done | bytes 524320 | tf_op jit(solution)/shard_map/ppermute | solution.py:145
  453.9 4.1 collective-permute-done.64
  463.0 7.8 %collective-permute-done.65 = bf16[144,1024]{1,0:T(8,128)(2,1)S(1)} collective-permute-done((bf16[144,1024]{1,0:T(8,128)(2,1)}, bf16[144,1024]{1,0:T(8,128)(2,1)S(1)}, u32[]{:S(2)}, u32[]{:S(2)}) %collective-permute-start.65) | collective-permute-done | bytes 294944 | tf_op jit(solution)/shard_map/ppermute | solution.py:150
  476.3 6.7 %collective-permute-start.66 = (bf16[2,1024,256]{2,1,0:T(8,128)(2,1)S(1)}, bf16[2,1024,256]{2,1,0:T(8,128)(2,1)}, u32[]{:S(2)}, u32[]{:S(2)}) collective-permute-start(bf16[2,1024,256]{2,1,0:T(8,128)(2,1)S(1)} %bitcast.71), channel_id=1, source_target_pairs={{4,8},{8,4},{5,9},{9,5},{6,10},{10,6},{7,11},{11,7},{20,24},{24,20... | collective-permute-start | bytes 3145736 | tf_op jit(solution)/shard_map/ppermute | solution.py:114
  485.2 9.6 %shard_map.294 = (f32[4,2048,128]{2,1,0:T(8,128)}, f32[4,2048,128]{2,1,0:T(8,128)}, f32[4,128,2048]{2,1,0:T(8,128)}) custom-call(s32[6]{0:T(128)S(1)} %copy-done.70, bf16[2,2048,512]{2,1,0:T(8,128)(2,1)S(1)} %copy-done.29, bf16[2,2048,512]{2,1,0:T(8,128)(2,1)} %collective-permute-done.70.gu_got, bf16[2,256,2048]{2,1,0:T(8,128)(2,1)} %get-tuple-element.168.down_mine, ...), custom_call_target="tpu_custom_call" | custom-call | flops 20000000000 | bytes 1 | tf_op jit(solution)/shard_map/pallas_call | solution.py:995
  494.9 8.8 %collective-permute-done.69.refs_3_ = bf16[2,144,1024]{2,1,0:T(8,128)(2,1)S(1)} collective-permute-done((bf16[2,144,1024]{2,1,0:T(8,128)(2,1)S(1)}, bf16[2,144,1024]{2,1,0:T(8,128)(2,1)S(1)}, u32[]{:S(2)}, u32[]{:S(2)}) %collective-permute-start.69) | collective-permute-done | bytes 589856 | tf_op jit(solution)/shard_map/ppermute | solution.py:41
  512.6 5.4 %shard_map.296 = (f32[2048,256]{1,0:T(8,128)}, f32[2048,256]{1,0:T(8,128)}, f32[2048,256]{1,0:T(8,128)}, f32[256,2048]{1,0:T(8,128)}, f32[16,1024]{1,0:T(8,128)S(1)}) custom-call(s32[6]{0:T(128)S(1)} %copy-done.70, bf16[2,144,1024]{2,1,0:T(8,128)(2,1)S(1)} %copy-done.16, bf16[2,144,1024]{2,1,0:T(8,128)(2,1)S(1)} %copy-done.42, ...), custom_call_target="tpu_custom_call" | custom-call | flops 1 | bytes 1 | tf_op jit(solution)/shard_map/pallas_call | solution.py:957
  (434 shorter events, 163.3 us)
Async XLA Ops:
  26.1 43.3 %collective-permute-start.6 = (bf16[1024,768]{1,0:T(8,128)(2,1)}, bf16[1024,768]{1,0:T(8,128)(2,1)S(1)}, u32[]{:S(2)}, u32[]{:S(2)}) collective-permute-start(bf16[1024,768]{1,0:T(8,128)(2,1)} %pad_maximum_fusion.1), channel_id=1, source_target_pairs={{0,68},{4,64},{64,4},{68,0},{1,69},{5,65},{65,5},{69,1},{2,70},{6,... | collective-permute-start | bytes 4718600 | tf_op jit(solution)/shard_map/ppermute | solution.py:49
  29.7 13.4 %collective-permute-start.2 = (bf16[2,512,256]{2,1,0:T(8,128)(2,1)S(1)}, bf16[2,512,256]{2,1,0:T(8,128)(2,1)S(1)}, u32[]{:S(2)}, u32[]{:S(2)}) collective-permute-start(bf16[2,512,256]{2,1,0:T(8,128)(2,1)S(1)} %pad_maximum_fusion.5.own), channel_id=1, source_target_pairs={{0,3},{1,0},{2,1},{3,2},{4,7},{5,4},{6,5},{7,6},{8,11},{9,8},{10,9... | collective-permute-start | bytes 1572872 | tf_op jit(solution)/shard_map/ppermute | solution.py:41
  32.2 16.9 %collective-permute-start.4 = (bf16[2,512,256]{2,1,0:T(8,128)(2,1)S(1)}, bf16[2,512,256]{2,1,0:T(8,128)(2,1)S(1)}, u32[]{:S(2)}, u32[]{:S(2)}) collective-permute-start(bf16[2,512,256]{2,1,0:T(8,128)(2,1)S(1)} %pad_maximum_fusion.5.own), channel_id=1, source_target_pairs={{0,1},{1,2},{2,3},{3,0},{4,5},{5,6},{6,7},{7,4},{8,9},{9,10},{10,1... | collective-permute-start | bytes 1572872 | tf_op jit(solution)/shard_map/ppermute | solution.py:41
  51.8 15.3 %collective-permute-start.8 = (bf16[512,256]{1,0:T(8,128)(2,1)}, bf16[512,256]{1,0:T(8,128)(2,1)}, u32[]{:S(2)}, u32[]{:S(2)}) collective-permute-start(bf16[512,256]{1,0:T(8,128)(2,1)} %get-tuple-element.196), channel_id=1, source_target_pairs={{0,8},{4,0},{8,12},{12,4},{1,9},{5,1},{9,13},{13,5},{2,10},{6,2},{... | collective-permute-start | bytes 786440 | tf_op jit(solution)/shard_map/ppermute | solution.py:104
  51.8 15.3 %collective-permute-start.7 = (bf16[512,256]{1,0:T(8,128)(2,1)}, bf16[512,256]{1,0:T(8,128)(2,1)}, u32[]{:S(2)}, u32[]{:S(2)}) collective-permute-start(bf16[512,256]{1,0:T(8,128)(2,1)} %get-tuple-element.195), channel_id=1, source_target_pairs={{0,0},{4,8},{8,4},{12,12},{1,1},{5,9},{9,5},{13,13},{2,2},{6,10},{... | collective-permute-start | bytes 786440 | tf_op jit(solution)/shard_map/ppermute | solution.py:104
  70.6 18.9 %collective-permute-start.11 = (bf16[1024,768]{1,0:T(8,128)(2,1)}, bf16[1024,768]{1,0:T(8,128)(2,1)}, u32[]{:S(2)}, u32[]{:S(2)}) collective-permute-start(bf16[1024,768]{1,0:T(8,128)(2,1)} %get-tuple-element.99.refs_3_.refs_12_), channel_id=1, source_target_pairs={{0,8},{8,0},{1,9},{9,1},{2,10},{10,2},{3,11},{11,3},{4,12},{12,4},... | collective-permute-start | bytes 4718600 | tf_op jit(solution)/shard_map/ppermute | solution.py:45
  74.7 14.8 %collective-permute-start.12 = (bf16[128,2048]{1,0:T(8,128)(2,1)S(1)}, bf16[128,2048]{1,0:T(8,128)(2,1)S(1)}, u32[]{:S(2)}, u32[]{:S(2)}) collective-permute-start(bf16[128,2048]{1,0:T(8,128)(2,1)S(1)} %constant_dynamic-slice_fusion.3), channel_id=1, source_target_pairs={{0,68},{4,64},{64,4},{68,0},{1,69},{5,65},{65,5},{69,1},{2,70},{6,... | collective-permute-start | bytes 1572872 | tf_op jit(solution)/shard_map/ppermute | solution.py:49
  75.7 29.0 %collective-permute-start.18 = (f32[2,256]{1,0:T(2,128)S(1)}, f32[2,256]{1,0:T(2,128)S(1)}, u32[]{:S(2)}, u32[]{:S(2)}) collective-permute-start(f32[2,256]{1,0:T(2,128)S(1)} %pad_maximum_fusion.10), channel_id=1, source_target_pairs={{0,68},{4,64},{64,4},{68,0},{1,69},{5,65},{65,5},{69,1},{2,70},{6,... | collective-permute-start | bytes 6152 | tf_op jit(solution)/shard_map/ppermute | solution.py:49
  77.6 32.1 %collective-permute-start.9 = (bf16[2,512,256]{2,1,0:T(8,128)(2,1)}, bf16[2,512,256]{2,1,0:T(8,128)(2,1)S(1)}, u32[]{:S(2)}, u32[]{:S(2)}) collective-permute-start(bf16[2,512,256]{2,1,0:T(8,128)(2,1)} %get-tuple-element.98.own), channel_id=1, source_target_pairs={{0,3},{1,0},{2,1},{3,2},{4,7},{5,4},{6,5},{7,6},{8,11},{9,8},{10,9... | collective-permute-start | bytes 1572872 | tf_op jit(solution)/shard_map/ppermute | solution.py:41
  80.0 29.7 %collective-permute-start.10 = (bf16[2,512,256]{2,1,0:T(8,128)(2,1)}, bf16[2,512,256]{2,1,0:T(8,128)(2,1)S(1)}, u32[]{:S(2)}, u32[]{:S(2)}) collective-permute-start(bf16[2,512,256]{2,1,0:T(8,128)(2,1)} %get-tuple-element.98.own), channel_id=1, source_target_pairs={{0,1},{1,2},{2,3},{3,0},{4,5},{5,6},{6,7},{7,4},{8,9},{9,10},{10,1... | collective-permute-start | bytes 1572872 | tf_op jit(solution)/shard_map/ppermute | solution.py:41
  125.0 71.3 %collective-permute-start.30 = (bf16[2,2048,256]{2,1,0:T(8,128)(2,1)}, bf16[2,2048,256]{2,1,0:T(8,128)(2,1)}, u32[]{:S(2)}, u32[]{:S(2)}) collective-permute-start(bf16[2,2048,256]{2,1,0:T(8,128)(2,1)} %pad_maximum_fusion), channel_id=1, source_target_pairs={{0,68},{4,64},{64,4},{68,0},{1,69},{5,65},{65,5},{69,1},{2,70},{6,... | collective-permute-start | bytes 6291464 | tf_op jit(solution)/shard_map/ppermute | solution.py:49
  154.3 14.8 %collective-permute-start.23 = (bf16[128,2048]{1,0:T(8,128)(2,1)S(1)}, bf16[128,2048]{1,0:T(8,128)(2,1)S(1)}, u32[]{:S(2)}, u32[]{:S(2)}) collective-permute-start(bf16[128,2048]{1,0:T(8,128)(2,1)S(1)} %get-tuple-element.112), channel_id=1, source_target_pairs={{0,1},{1,2},{2,3},{3,0},{4,5},{5,6},{6,7},{7,4},{8,9},{9,10},{10,1... | collective-permute-start | bytes 1572872 | tf_op jit(solution)/shard_map/ppermute | solution.py:41
  154.4 23.4 %collective-permute-start.24 = (bf16[128,2048]{1,0:T(8,128)(2,1)S(1)}, bf16[128,2048]{1,0:T(8,128)(2,1)S(1)}, u32[]{:S(2)}, u32[]{:S(2)}) collective-permute-start(bf16[128,2048]{1,0:T(8,128)(2,1)S(1)} %get-tuple-element.113), channel_id=1, source_target_pairs={{0,2},{1,3},{2,0},{3,1},{4,6},{5,7},{6,4},{7,5},{8,10},{9,11},{10,... | collective-permute-start | bytes 1572872 | tf_op jit(solution)/shard_map/ppermute | solution.py:41
  155.7 24.1 %collective-permute-start.25 = (bf16[128,2048]{1,0:T(8,128)(2,1)S(1)}, bf16[128,2048]{1,0:T(8,128)(2,1)S(1)}, u32[]{:S(2)}, u32[]{:S(2)}) collective-permute-start(bf16[128,2048]{1,0:T(8,128)(2,1)S(1)} %get-tuple-element.114), channel_id=1, source_target_pairs={{0,3},{1,0},{2,1},{3,2},{4,7},{5,4},{6,5},{7,6},{8,11},{9,8},{10,9... | collective-permute-start | bytes 1572872 | tf_op jit(solution)/shard_map/ppermute | solution.py:41
  157.2 39.1 %collective-permute-start.31 = (bf16[2,128,2048]{2,1,0:T(8,128)(2,1)S(1)}, bf16[2,128,2048]{2,1,0:T(8,128)(2,1)S(1)}, u32[]{:S(2)}, u32[]{:S(2)}) collective-permute-start(bf16[2,128,2048]{2,1,0:T(8,128)(2,1)S(1)} %constant_dynamic-slice_fusion), channel_id=1, source_target_pairs={{0,68},{4,64},{64,4},{68,0},{1,69},{5,65},{65,5},{69,1},{2,70},{6,... | collective-permute-start | bytes 3145736 | tf_op jit(solution)/shard_map/ppermute | solution.py:49
  182.6 14.1 %collective-permute-start.26 = (bf16[128,2048]{1,0:T(8,128)(2,1)S(1)}, bf16[128,2048]{1,0:T(8,128)(2,1)S(1)}, u32[]{:S(2)}, u32[]{:S(2)}) collective-permute-start(bf16[128,2048]{1,0:T(8,128)(2,1)S(1)} %get-tuple-element.116.own_rows), channel_id=1, source_target_pairs={{0,3},{1,0},{2,1},{3,2},{4,7},{5,4},{6,5},{7,6},{8,11},{9,8},{10,9... | collective-permute-start | bytes 1572872 | tf_op jit(solution)/shard_map/ppermute | solution.py:41
  186.0 13.7 %collective-permute-start.28 = (bf16[128,2048]{1,0:T(8,128)(2,1)S(1)}, bf16[128,2048]{1,0:T(8,128)(2,1)S(1)}, u32[]{:S(2)}, u32[]{:S(2)}) collective-permute-start(bf16[128,2048]{1,0:T(8,128)(2,1)S(1)} %get-tuple-element.116.own_rows), channel_id=1, source_target_pairs={{0,1},{1,2},{2,3},{3,0},{4,5},{5,6},{6,7},{7,4},{8,9},{9,10},{10,1... | collective-permute-start | bytes 1572872 | tf_op jit(solution)/shard_map/ppermute | solution.py:41
  200.5 18.3 %collective-permute-start.33 = (bf16[2,2048,256]{2,1,0:T(8,128)(2,1)}, bf16[2,2048,256]{2,1,0:T(8,128)(2,1)}, u32[]{:S(2)}, u32[]{:S(2)}) collective-permute-start(bf16[2,2048,256]{2,1,0:T(8,128)(2,1)} %get-tuple-element.121.near), channel_id=1, source_target_pairs={{0,8},{8,0},{1,9},{9,1},{2,10},{10,2},{3,11},{11,3},{4,12},{12,4},... | collective-permute-start | bytes 6291464 | tf_op jit(solution)/shard_map/ppermute | solution.py:45
  203.8 43.1 %collective-permute-start.39 = (bf16[512,2048]{1,0:T(8,128)(2,1)}, bf16[512,2048]{1,0:T(8,128)(2,1)S(1)}, u32[]{:S(2)}, u32[]{:S(2)}) collective-permute-start(bf16[512,2048]{1,0:T(8,128)(2,1)} %get-tuple-element.117.cot), channel_id=1, source_target_pairs={{0,8},{8,0},{1,9},{9,1},{2,10},{10,2},{3,11},{11,3},{4,12},{12,4},... | collective-permute-start | bytes 6291464 | tf_op jit(solution)/shard_map/ppermute | solution.py:45
  204.8 14.0 %collective-permute-start.27 = (bf16[64,2048]{1,0:T(8,128)(2,1)S(1)}, bf16[64,2048]{1,0:T(8,128)(2,1)S(1)}, u32[]{:S(2)}, u32[]{:S(2)}) collective-permute-start(bf16[64,2048]{1,0:T(8,128)(2,1)S(1)} %slice.170), channel_id=1, source_target_pairs={{0,3},{1,0},{2,1},{3,2},{4,7},{5,4},{6,5},{7,6},{8,11},{9,8},{10,9... | collective-permute-start | bytes 786440 | tf_op jit(solution)/shard_map/ppermute | solution.py:41
  205.7 13.1 %collective-permute-start.29 = (bf16[64,2048]{1,0:T(8,128)(2,1)S(1)}, bf16[64,2048]{1,0:T(8,128)(2,1)S(1)}, u32[]{:S(2)}, u32[]{:S(2)}) collective-permute-start(bf16[64,2048]{1,0:T(8,128)(2,1)S(1)} %slice.171), channel_id=1, source_target_pairs={{0,1},{1,2},{2,3},{3,0},{4,5},{5,6},{6,7},{7,4},{8,9},{9,10},{10,1... | collective-permute-start | bytes 786440 | tf_op jit(solution)/shard_map/ppermute | solution.py:41
  237.3 14.8 %collective-permute-start.38 = (bf16[512,2048]{1,0:T(8,128)(2,1)S(1)}, bf16[512,2048]{1,0:T(8,128)(2,1)S(1)}, u32[]{:S(2)}, u32[]{:S(2)}) collective-permute-start(bf16[512,2048]{1,0:T(8,128)(2,1)S(1)} %get-tuple-element.134), channel_id=1, source_target_pairs={{0,8},{8,0},{1,9},{9,1},{2,10},{10,2},{3,11},{11,3},{4,12},{12,4},... | collective-permute-start | bytes 6291464 | tf_op jit(solution)/shard_map/ppermute | solution.py:45
  237.4 20.8 %collective-permute-start.34 = (bf16[128,2048]{1,0:T(8,128)(2,1)}, bf16[128,2048]{1,0:T(8,128)(2,1)S(1)}, u32[]{:S(2)}, u32[]{:S(2)}) collective-permute-start(bf16[128,2048]{1,0:T(8,128)(2,1)} %get-tuple-element.129), channel_id=1, source_target_pairs={{0,1},{1,2},{2,3},{3,0},{4,5},{5,6},{6,7},{7,4},{8,9},{9,10},{10,1... | collective-permute-start | bytes 1572872 | tf_op jit(solution)/shard_map/ppermute | solution.py:41
  237.4 25.1 %collective-permute-start.35 = (bf16[128,2048]{1,0:T(8,128)(2,1)}, bf16[128,2048]{1,0:T(8,128)(2,1)S(1)}, u32[]{:S(2)}, u32[]{:S(2)}) collective-permute-start(bf16[128,2048]{1,0:T(8,128)(2,1)} %get-tuple-element.130), channel_id=1, source_target_pairs={{0,2},{1,3},{2,0},{3,1},{4,6},{5,7},{6,4},{7,5},{8,10},{9,11},{10,... | collective-permute-start | bytes 1572872 | tf_op jit(solution)/shard_map/ppermute | solution.py:41
  246.0 17.7 %collective-permute-start.36 = (bf16[128,2048]{1,0:T(8,128)(2,1)}, bf16[128,2048]{1,0:T(8,128)(2,1)S(1)}, u32[]{:S(2)}, u32[]{:S(2)}) collective-permute-start(bf16[128,2048]{1,0:T(8,128)(2,1)} %get-tuple-element.131), channel_id=1, source_target_pairs={{0,3},{1,0},{2,1},{3,2},{4,7},{5,4},{6,5},{7,6},{8,11},{9,8},{10,9... | collective-permute-start | bytes 1572872 | tf_op jit(solution)/shard_map/ppermute | solution.py:41
  269.2 162.5 %all-reduce.4.cloned.1.call-start = ((), (), s32[]{:S(2)}) async-start(), calls=%async_computation.1 | async-start | bytes 12582912 | tf_op jit(solution)/shard_map/psum | solution.py:1134
  270.2 14.1 %collective-permute-start.40 = (bf16[128,2048]{1,0:T(8,128)(2,1)S(1)}, bf16[128,2048]{1,0:T(8,128)(2,1)S(1)}, u32[]{:S(2)}, u32[]{:S(2)}) collective-permute-start(bf16[128,2048]{1,0:T(8,128)(2,1)S(1)} %copy-done.91), channel_id=1, source_target_pairs={{0,3},{1,0},{2,1},{3,2},{4,7},{5,4},{6,5},{7,6},{8,11},{9,8},{10,9... | collective-permute-start | bytes 1572872 | tf_op jit(solution)/shard_map/ppermute | solution.py:41
  273.5 14.3 %collective-permute-start.42 = (bf16[128,2048]{1,0:T(8,128)(2,1)S(1)}, bf16[128,2048]{1,0:T(8,128)(2,1)S(1)}, u32[]{:S(2)}, u32[]{:S(2)}) collective-permute-start(bf16[128,2048]{1,0:T(8,128)(2,1)S(1)} %copy-done.91), channel_id=1, source_target_pairs={{0,1},{1,2},{2,3},{3,0},{4,5},{5,6},{6,7},{7,4},{8,9},{9,10},{10,1... | collective-permute-start | bytes 1572872 | tf_op jit(solution)/shard_map/ppermute | solution.py:41
  306.6 14.6 %collective-permute-start.46 = (bf16[128,2048]{1,0:T(8,128)(2,1)}, bf16[128,2048]{1,0:T(8,128)(2,1)S(1)}, u32[]{:S(2)}, u32[]{:S(2)}) collective-permute-start(bf16[128,2048]{1,0:T(8,128)(2,1)} %get-tuple-element.146), channel_id=1, source_target_pairs={{0,1},{1,2},{2,3},{3,0},{4,5},{5,6},{6,7},{7,4},{8,9},{9,10},{10,1... | collective-permute-start | bytes 1572872 | tf_op jit(solution)/shard_map/ppermute | solution.py:41
  306.6 15.4 %collective-permute-start.47 = (bf16[128,2048]{1,0:T(8,128)(2,1)}, bf16[128,2048]{1,0:T(8,128)(2,1)S(1)}, u32[]{:S(2)}, u32[]{:S(2)}) collective-permute-start(bf16[128,2048]{1,0:T(8,128)(2,1)} %get-tuple-element.147), channel_id=1, source_target_pairs={{0,3},{1,0},{2,1},{3,2},{4,7},{5,4},{6,5},{7,6},{8,11},{9,8},{10,9... | collective-permute-start | bytes 1572872 | tf_op jit(solution)/shard_map/ppermute | solution.py:41
  309.3 31.3 %collective-permute-start.21 = (bf16[512,2048]{1,0:T(8,128)(2,1)S(1)}, bf16[512,2048]{1,0:T(8,128)(2,1)}, u32[]{:S(2)}, u32[]{:S(2)}) collective-permute-start(bf16[512,2048]{1,0:T(8,128)(2,1)S(1)} %copy-done.3), channel_id=1, source_target_pairs={{0,8},{8,0},{1,9},{9,1},{2,10},{10,2},{3,11},{11,3},{4,12},{12,4},... | collective-permute-start | bytes 6291464 | tf_op jit(solution)/shard_map/ppermute | solution.py:45
  310.2 32.5 %collective-permute-start.45 = (bf16[512,2048]{1,0:T(8,128)(2,1)}, bf16[512,2048]{1,0:T(8,128)(2,1)}, u32[]{:S(2)}, u32[]{:S(2)}) collective-permute-start(bf16[512,2048]{1,0:T(8,128)(2,1)} %get-tuple-element.138.refs_2_), channel_id=1, source_target_pairs={{0,8},{8,0},{1,9},{9,1},{2,10},{10,2},{3,11},{11,3},{4,12},{12,4},... | collective-permute-start | bytes 6291464 | tf_op jit(solution)/shard_map/ppermute | solution.py:45
  361.9 19.4 %collective-permute-start.57 = (bf16[256,1024]{1,0:T(8,128)(2,1)S(1)}, bf16[256,1024]{1,0:T(8,128)(2,1)S(1)}, u32[]{:S(2)}, u32[]{:S(2)}) collective-permute-start(bf16[256,1024]{1,0:T(8,128)(2,1)S(1)} %get-tuple-element.192), channel_id=1, source_target_pairs={{0,16},{16,32},{32,48},{48,0},{1,17},{17,33},{33,49},{49,1},{2,18}... | collective-permute-start | bytes 1572872 | tf_op jit(solution)/shard_map/ppermute | solution.py:41
  363.3 19.5 %collective-permute-start.59 = (bf16[256,1024]{1,0:T(8,128)(2,1)S(1)}, bf16[256,1024]{1,0:T(8,128)(2,1)S(1)}, u32[]{:S(2)}, u32[]{:S(2)}) collective-permute-start(bf16[256,1024]{1,0:T(8,128)(2,1)S(1)} %get-tuple-element.191), channel_id=1, source_target_pairs={{0,48},{16,0},{32,16},{48,32},{1,49},{17,1},{33,17},{49,33},{2,50}... | collective-permute-start | bytes 1572872 | tf_op jit(solution)/shard_map/ppermute | solution.py:41
  364.9 39.6 %collective-permute-start.55 = (bf16[272,2048]{1,0:T(8,128)(2,1)S(1)}, bf16[272,2048]{1,0:T(8,128)(2,1)S(1)}, u32[]{:S(2)}, u32[]{:S(2)}) collective-permute-start(bf16[272,2048]{1,0:T(8,128)(2,1)S(1)} %get-tuple-element.156), channel_id=1, source_target_pairs={{0,2},{1,3},{2,0},{3,1},{4,6},{5,7},{6,4},{7,5},{8,10},{9,11},{10,... | collective-permute-start | bytes 3342344 | tf_op jit(solution)/shard_map/ppermute | solution.py:41
  381.6 42.7 %collective-permute-start.58 = (bf16[512,1024]{1,0:T(8,128)(2,1)S(1)}, bf16[512,1024]{1,0:T(8,128)(2,1)S(1)}, u32[]{:S(2)}, u32[]{:S(2)}) collective-permute-start(bf16[512,1024]{1,0:T(8,128)(2,1)S(1)} %pad_maximum_fusion.2), channel_id=1, source_target_pairs={{0,16},{16,32},{32,48},{48,0},{1,17},{17,33},{33,49},{49,1},{2,18}... | collective-permute-start | bytes 3145736 | tf_op jit(solution)/shard_map/ppermute | solution.py:41
  383.0 41.3 %collective-permute-start.60 = (bf16[512,1024]{1,0:T(8,128)(2,1)S(1)}, bf16[512,1024]{1,0:T(8,128)(2,1)S(1)}, u32[]{:S(2)}, u32[]{:S(2)}) collective-permute-start(bf16[512,1024]{1,0:T(8,128)(2,1)S(1)} %pad_maximum_fusion.3), channel_id=1, source_target_pairs={{0,48},{16,0},{32,16},{48,32},{1,49},{17,1},{33,17},{49,33},{2,50}... | collective-permute-start | bytes 3145736 | tf_op jit(solution)/shard_map/ppermute | solution.py:41
  386.6 17.9 %collective-permute-start.54 = (bf16[144,2048]{1,0:T(8,128)(2,1)S(1)}, bf16[144,2048]{1,0:T(8,128)(2,1)S(1)}, u32[]{:S(2)}, u32[]{:S(2)}) collective-permute-start(bf16[144,2048]{1,0:T(8,128)(2,1)S(1)} %get-tuple-element.155), channel_id=1, source_target_pairs={{0,1},{1,2},{2,3},{3,0},{4,5},{5,6},{6,7},{7,4},{8,9},{9,10},{10,1... | collective-permute-start | bytes 1769480 | tf_op jit(solution)/shard_map/ppermute | solution.py:41
  386.6 17.9 %collective-permute-start.56 = (bf16[144,2048]{1,0:T(8,128)(2,1)S(1)}, bf16[144,2048]{1,0:T(8,128)(2,1)S(1)}, u32[]{:S(2)}, u32[]{:S(2)}) collective-permute-start(bf16[144,2048]{1,0:T(8,128)(2,1)S(1)} %get-tuple-element.157), channel_id=1, source_target_pairs={{0,3},{1,0},{2,1},{3,2},{4,7},{5,4},{6,5},{7,6},{8,11},{9,8},{10,9... | collective-permute-start | bytes 1769480 | tf_op jit(solution)/shard_map/ppermute | solution.py:41
  431.7 51.3 %collective-permute-start.70 = (bf16[2,2048,512]{2,1,0:T(8,128)(2,1)}, bf16[2,2048,512]{2,1,0:T(8,128)(2,1)}, u32[]{:S(2)}, u32[]{:S(2)}) collective-permute-start(bf16[2,2048,512]{2,1,0:T(8,128)(2,1)} %get-tuple-element.167.gu_mine), channel_id=1, source_target_pairs={{0,8},{12,4},{1,9},{13,5},{2,10},{14,6},{3,11},{15,7},{16,24},{28,... | collective-permute-start | bytes 12582920 | tf_op jit(solution)/shard_map/ppermute | solution.py:155
  434.3 12.3 %collective-permute-start.62 = (bf16[256,1024]{1,0:T(8,128)(2,1)S(1)}, bf16[256,1024]{1,0:T(8,128)(2,1)S(1)}, u32[]{:S(2)}, u32[]{:S(2)}) collective-permute-start(bf16[256,1024]{1,0:T(8,128)(2,1)S(1)} %get-tuple-element.190), channel_id=1, source_target_pairs={{0,64},{4,72},{8,68},{12,76},{64,0},{68,8},{72,4},{76,12},{1,65},{... | collective-permute-start | bytes 1572872 | tf_op jit(solution)/shard_map/ppermute | solution.py:146
  437.2 16.2 %collective-permute-start.61 = (bf16[256,1024]{1,0:T(8,128)(2,1)S(1)}, bf16[256,1024]{1,0:T(8,128)(2,1)S(1)}, u32[]{:S(2)}, u32[]{:S(2)}) collective-permute-start(bf16[256,1024]{1,0:T(8,128)(2,1)S(1)} %get-tuple-element.189), channel_id=1, source_target_pairs={{4,8},{8,4},{68,72},{72,68},{5,9},{9,5},{69,73},{73,69},{6,10},{10... | collective-permute-start | bytes 1572872 | tf_op jit(solution)/shard_map/ppermute | solution.py:145
  439.1 37.2 %collective-permute-start.71 = (bf16[2,256,2048]{2,1,0:T(8,128)(2,1)}, bf16[2,256,2048]{2,1,0:T(8,128)(2,1)}, u32[]{:S(2)}, u32[]{:S(2)}) collective-permute-start(bf16[2,256,2048]{2,1,0:T(8,128)(2,1)} %get-tuple-element.168.down_mine), channel_id=1, source_target_pairs={{0,8},{12,4},{1,9},{13,5},{2,10},{14,6},{3,11},{15,7},{16,24},{28,... | collective-permute-start | bytes 6291464 | tf_op jit(solution)/shard_map/ppermute | solution.py:155
  440.4 20.9 %all-to-all-start = ((bf16[8,2,128,256]{3,2,1,0:T(8,128)(2,1)}), bf16[8,2,128,256]{3,2,1,0:T(8,128)(2,1)S(1)}, u32[]{:S(2)}, u32[]{:S(2)}) async-start(bf16[8,2,128,256]{3,2,1,0:T(8,128)(2,1)} %get-tuple-element.163.refs_2_), calls=%async_computation | async-start | bytes 2097152 | tf_op jit(solution)/shard_map/all_to_all | solution.py:109
  471.8 23.1 %collective-permute-start.67 = (bf16[2,144,1024]{2,1,0:T(8,128)(2,1)S(1)}, bf16[2,144,1024]{2,1,0:T(8,128)(2,1)S(1)}, u32[]{:S(2)}, u32[]{:S(2)}) collective-permute-start(bf16[2,144,1024]{2,1,0:T(8,128)(2,1)S(1)} %pad_maximum_fusion.4.refs_1_.refs_0_), channel_id=1, source_target_pairs={{0,48},{16,0},{32,16},{48,32},{1,49},{17,1},{33,17},{49,33},{2,50}... | collective-permute-start | bytes 1769480 | tf_op jit(solution)/shard_map/ppermute | solution.py:41
  474.3 20.6 %collective-permute-start.68 = (bf16[2,144,1024]{2,1,0:T(8,128)(2,1)S(1)}, bf16[2,144,1024]{2,1,0:T(8,128)(2,1)S(1)}, u32[]{:S(2)}, u32[]{:S(2)}) collective-permute-start(bf16[2,144,1024]{2,1,0:T(8,128)(2,1)S(1)} %pad_maximum_fusion.4.refs_1_.refs_0_), channel_id=1, source_target_pairs={{0,32},{16,48},{32,0},{48,16},{1,33},{17,49},{33,1},{49,17},{2,34}... | collective-permute-start | bytes 1769480 | tf_op jit(solution)/shard_map/ppermute | solution.py:41
  474.7 29.0 %collective-permute-start.69 = (bf16[2,144,1024]{2,1,0:T(8,128)(2,1)S(1)}, bf16[2,144,1024]{2,1,0:T(8,128)(2,1)S(1)}, u32[]{:S(2)}, u32[]{:S(2)}) collective-permute-start(bf16[2,144,1024]{2,1,0:T(8,128)(2,1)S(1)} %pad_maximum_fusion.4.refs_1_.refs_0_), channel_id=1, source_target_pairs={{0,16},{16,32},{32,48},{48,0},{1,17},{17,33},{33,49},{49,1},{2,18}... | collective-permute-start | bytes 1769480 | tf_op jit(solution)/shard_map/ppermute | solution.py:41
  476.3 29.2 %collective-permute-start.66 = (bf16[2,1024,256]{2,1,0:T(8,128)(2,1)S(1)}, bf16[2,1024,256]{2,1,0:T(8,128)(2,1)}, u32[]{:S(2)}, u32[]{:S(2)}) collective-permute-start(bf16[2,1024,256]{2,1,0:T(8,128)(2,1)S(1)} %bitcast.71), channel_id=1, source_target_pairs={{4,8},{8,4},{5,9},{9,5},{6,10},{10,6},{7,11},{11,7},{20,24},{24,20... | collective-permute-start | bytes 3145736 | tf_op jit(solution)/shard_map/ppermute | solution.py:114
  (137 other events, 1286.6 us)
Sparse Core Ops, SparseCore 0:
  274.6 144.7 all-reduce.3
